TPU v7x, 128 devices: a whole 4x4x4 slice. The times are simulated.
128 devices in a mesh: group: 16 (over y_hi, x, core), inner: 8 (over y_lo, z).
Axes of the slice: x: 4, y: 4 (y_hi: 2, y_lo: 2; y = y_hi * 2 + y_lo), z: 4, core: 2. Of those that a mesh axis runs over, the one named last changes fastest.
Arguments:
- latents: bfloat16 [128, 1536, 640], P(('group', 'inner')), may hold values from -45 to 45
- cotangent: bfloat16 [128, 1536, 640], P(('group', 'inner')), may hold values from -6 to 6
- gain: float32 [640], replicated, may hold values from 0.25 to 1.75
- bias: float32 [640], replicated, may hold values from -3 to 3
- weight: float32 [16, 5760, 640], P('group', 'inner'), may hold values from -6 to 6
- momentum: float32 [16, 5760, 640], P('group', 'inner'), may hold values from -6 to 6
- step: int32 [1], replicated, may hold values from 0 to 999
Outputs:
- block_out: bfloat16 [128, 1536, 640], P(('group', 'inner'))
- new_weight: float32 [16, 5760, 640], P('group', 'inner')
- new_momentum: float32 [16, 5760, 640], P('group', 'inner')
All inputs are finite; a program needn't handle non-finite values.
Results may differ from a plain program's by a relative error of at most 0.014.
Values may be sent and summed in bfloat16 or wider, within the bound.
No kernel may reach another device: no remote copies, remote signals or barrier semaphores. Data moves between devices by JAX's collectives and lax.ppermute only.
A program may use at most 256 MiB of HBM per device.

v0:
```python
from functools import partial

import jax
import jax.numpy as jnp
from jax import lax
from jax.sharding import PartitionSpec as P

GN_GROUPS = 32
HEIGHT = 48
WIDTH = 32


def for_sending(value):

    def short(part):
        return part.astype(jnp.bfloat16) if part.dtype == jnp.float32 else part

    return jax.tree.map(short, value)


def from_behind(value, axis, by):
    devices = lax.axis_size(axis)
    return lax.ppermute(value, axis, [(i, (i + by) % devices) for i in range(devices)])


def norm_act(latents, gain, bias):
    count, pixels, chans = latents.shape
    values = latents.astype(jnp.float32).reshape(count, pixels, GN_GROUPS, chans // GN_GROUPS)
    center = jnp.mean(values, axis=(1, 3), keepdims=True)
    spread = jnp.mean((values - center) * (values - center), axis=(1, 3), keepdims=True)
    normed = ((values - center) * lax.rsqrt(spread + 1e-05)).reshape(
        count, pixels, chans
    ) * gain + bias
    return jax.nn.silu(normed).astype(jnp.bfloat16)


def unfold(hidden):
    count, pixels, chans = hidden.shape
    image = hidden.reshape(count, HEIGHT, WIDTH, chans)
    padded = jnp.pad(image, ((0, 0), (1, 1), (1, 1), (0, 0)))
    taps = [padded[:, a : a + HEIGHT, b : b + WIDTH, :] for a in range(3) for b in range(3)]
    return jnp.concatenate(taps, axis=-1).reshape(count * pixels, 9 * chans)


def shift_after(state, by):
    return jax.tree.map(
        lambda part, own: part.astype(own.dtype),
        from_behind(for_sending(state), "group", by),
        state,
    )


def from_partner(mover, state, step):
    span = lax.axis_size("group")
    levels = span.bit_length() - 1
    branches = [partial(mover, by=span - (1 << level)) for level in range(levels)]
    return lax.switch(step[0] % levels, branches, state)


def on_device(latents, cotangent, gain, bias, weight, momentum, step):
    chans = latents.shape[2]
    scale = (9 * chans) ** (-0.5)
    own_weight = weight[0]
    own_moment = momentum[0]
    hidden = norm_act(latents, gain, bias)
    columns = unfold(hidden)
    part_cols = columns
    conv = jnp.dot(
        part_cols,
        lax.all_gather(own_weight.astype(jnp.bfloat16), "inner", axis=0, tiled=True),
        preferred_element_type=jnp.float32,
    )
    block_out = (latents.astype(jnp.float32) + scale * conv.reshape(latents.shape)).astype(
        jnp.bfloat16
    )
    upstream = cotangent.reshape(-1, chans)
    part_cols = columns
    grad = lax.psum_scatter(
        (
            scale
            * lax.dot_general(
                part_cols, upstream, (((0,), (0,)), ((), ())), preferred_element_type=jnp.float32
            )
        ).astype(jnp.bfloat16),
        "inner",
        scatter_dimension=0,
        tiled=True,
    ).astype(jnp.float32)
    moved = 0.9 * own_moment + grad
    stepped = own_weight - 0.05 * moved
    partner_stepped, partner_moved = from_partner(shift_after, (stepped, moved), step)
    new_weight = 0.5 * (stepped + partner_stepped)
    new_moment = 0.5 * (moved + partner_moved)
    return (block_out, new_weight[None], new_moment[None])


def solution(mesh):
    placed = (
        P(("group", "inner"), None, None),
        P(("group", "inner"), None, None),
        P(),
        P(),
        P("group", "inner", None),
        P("group", "inner", None),
        P(),
    )
    return jax.shard_map(
        on_device,
        mesh=mesh,
        in_specs=placed,
        out_specs=(
            P(("group", "inner"), None, None),
            P("group", "inner", None),
            P("group", "inner", None),
        ),
        check_vma=False,
    )
```

profile of v0, /device:TPU:0, one launch (start us, length us, event | category | flops | bytes accessed | tf_op | source)
XLA Modules:
  0.0 244.6 jit_solution(253425905791006029)
XLA Ops:
  7.2 2.7 %bitcast_convert_fusion = bf16[720,640]{1,0:T(8,128)(2,1)} fusion(f32[1,720,640]{2,1,0:T(8,128)} %param.15), kind=kLoop, calls=%fused_computation.29 | loop fusion | flops 460800 | bytes 2764800 | tf_op jit(solution)/shard_map/convert_element_type | solution.py:70
  10.0 1.9 convert_reduce_fusion
  12.0 0.1 reduce_sum.25
  12.3 2.1 fusion.2
  14.5 0.1 reduce_sum.37
  14.9 2.9 %fusion.10 = bf16[1,1536,640]{2,1,0:T(8,128)(2,1)S(1)} fusion(bf16[1,1536,640]{2,1,0:T(8,128)(2,1)} %param.11, f32[640]{0:T(1024)S(1)} %copy-done.4, f32[640]{0:T(1024)S(1)} %copy-done.5, f32[640]{0:T(1024)S(1)} %mul.76, f32[640]{0:T(1024)S(1)} %sub.30), kind=kLoop, calls=%fused_computation.15 | loop fusion | flops 9830400 | bytes 3942400 | tf_op jit(solution)/shard_map/convert_element_type | solution.py:34
  17.8 5.6 %pad_slice_fusion = (bf16[1,48,32,640]{3,2,1,0:T(8,128)(2,1)S(1)}, bf16[1,48,32,640]{3,2,1,0:T(8,128)(2,1)S(1)}, bf16[1,48,32,640]{3,2,1,0:T(8,128)(2,1)S(1)}, b...) fusion(bf16[1,48,32,640]{3,2,1,0:T(8,128)(2,1)S(1)} %bitcast.41), kind=kLoop, calls=%fused_computation.17 | loop fusion | bytes 17694720 | tf_op jit(solution)/shard_map/slice | solution.py:41
  23.4 1.5 constant_dynamic-update-slice_fusion.7
  24.8 1.5 constant_dynamic-update-slice_fusion.6
  26.4 1.5 constant_dynamic-update-slice_fusion.5
  27.9 1.5 constant_dynamic-update-slice_fusion.4
  29.4 0.7 copy-done.2
  30.1 2.7 %bitcast_dynamic-update-slice_fusion = bf16[1536,5760]{1,0:T(8,128)(2,1)} fusion(bf16[1536,5760]{1,0:T(8,128)(2,1)} %constant_dynamic-update-slice_fusion.4, f32[640]{0:T(1024)S(1)} %copy-done.4, f32[640]{0:T(1024)S(1)} %copy-done.5, f32[640]{0:T(1024)S(1)} %mul.76, f32[640]{0:T(1024)S(1)} %sub.30, bf16[1,1536,640]{2,1,0:T(8,128)(2,1)S(1)} %copy-done.2), kind=kLoop, calls=%fused_computation.26 | loop fusion | flops 9830400 | bytes 3942400
  32.9 1.5 constant_dynamic-update-slice_fusion.3
  34.4 1.6 constant_dynamic-update-slice_fusion.2
  36.0 1.5 constant_dynamic-update-slice_fusion.1
  37.5 1.5 constant_dynamic-update-slice_fusion
  39.0 18.6 %multiply_convert_fusion = bf16[5760,640]{1,0:T(8,128)(2,1)} fusion(bf16[1536,5760]{1,0:T(8,128)(2,1)} %constant_dynamic-update-slice_fusion, bf16[1,1536,640]{2,1,0:T(8,128)(2,1)S(1)} %copy-done), kind=kOutput, calls=%fused_computation | convolution fusion | flops 11331993600 | bytes 27033600 | tf_op jit(solution)/shard_map/dot_general | solution.py:81
  58.4 36.9 %all-gather.2.cloned.1.call-done = bf16[5760,640]{1,0:T(8,128)(2,1)} async-done(((bf16[720,640]{1,0:T(8,128)(2,1)}), bf16[5760,640]{1,0:T(8,128)(2,1)}) %all-gather.2.cloned.1.call-update) | async-done | bytes 7372816 | tf_op jit(solution)/shard_map/all_gather | solution.py:70
  95.3 20.1 %fusion.11 = bf16[1,1536,640]{2,1,0:T(8,128)(2,1)} fusion(bf16[1,1536,640]{2,1,0:T(8,128)(2,1)S(1)} %copy-done.3, bf16[1536,5760]{1,0:T(8,128)(2,1)} %constant_dynamic-update-slice_fusion, bf16[5760,640]{1,0:T(8,128)(2,1)} %all-gather.2.cloned.1.call-done), kind=kOutput, calls=%fused_computation.16 | convolution fusion | flops 11328552960 | bytes 28999680 | tf_op jit(solution)/shard_map/dot_general | solution.py:68
  115.4 64.6 %reduce-scatter.2.cloned.1.call-done = bf16[720,640]{1,0:T(8,128)(2,1)} async-done(((bf16[5760,640]{1,0:T(8,128)(2,1)}), bf16[720,640]{1,0:T(8,128)(2,1)}) %reduce-scatter.2.cloned.1.call-update) | async-done | bytes 921616 | tf_op jit(solution)/shard_map/reduce_scatter | solution.py:78
  180.0 4.5 %bitcast_subtract_fusion = (f32[720,640]{1,0:T(8,128)}, f32[720,640]{1,0:T(8,128)}) fusion(f32[1,720,640]{2,1,0:T(8,128)} %param.15, bf16[720,640]{1,0:T(8,128)(2,1)} %reduce-scatter.2.cloned.1.call-done, f32[1,720,640]{2,1,0:T(8,128)} %param.16), kind=kLoop, calls=%fused_computation.28 | loop fusion | flops 2304000 | bytes 8294400 | tf_op jit(solution)/shard_map/sub | solution.py:90
  184.5 47.7 %conditional.4 = (f32[720,640]{1,0:T(8,128)}, f32[720,640]{1,0:T(8,128)}) conditional(s32[]{:T(128)} %clamp.3, (f32[720,640]{1,0:T(8,128)}, f32[720,640]{1,0:T(8,128)}) %bitcast_subtract_fusion, (f32[720,640]{1,0:T(8,128)}, f32[720,640]{1,0:T(8,128)}) %bitcast_subtract_fusion, (f32[720,640]{1,0:T(8,128)}, ...), branch_computations={%region_5.6_spmd, %region_6.7_spmd, %region_7.8_spmd, %region_8.9_... | conditional | flops 1843200 | bytes 18432096
  184.5 1.6 convert_element_type.77
  186.1 5.2 %collective-permute-start.4 = (bf16[720,640]{1,0:T(8,128)(2,1)S(1)}, bf16[720,640]{1,0:T(8,128)(2,1)S(1)}, u32[]{:S(2)}, u32[]{:S(2)}) collective-permute-start(bf16[720,640]{1,0:T(8,128)(2,1)S(1)} %convert_element_type.77), channel_id=1, source_target_pairs={{0,96},{8,104},{16,112},{24,120},{32,0},{40,8},{48,16},{56,24},{64... | collective-permute-start | bytes 2764808 | tf_op jit(solution)/shard_map/cond/branch_2_fun/ppermute | solution.py:23
  191.3 1.6 convert_element_type.79
  193.0 0.6 collective-permute-start.5
  193.5 18.6 %collective-permute-done.4 = bf16[720,640]{1,0:T(8,128)(2,1)S(1)} collective-permute-done((bf16[720,640]{1,0:T(8,128)(2,1)S(1)}, bf16[720,640]{1,0:T(8,128)(2,1)S(1)}, u32[]{:S(2)}, u32[]{:S(2)}) %collective-permute-start.4) | collective-permute-done | bytes 921632 | tf_op jit(solution)/shard_map/cond/branch_2_fun/ppermute | solution.py:23
  212.2 1.4 convert_element_type.101
  213.6 17.3 %collective-permute-done.5 = bf16[720,640]{1,0:T(8,128)(2,1)S(1)} collective-permute-done((bf16[720,640]{1,0:T(8,128)(2,1)S(1)}, bf16[720,640]{1,0:T(8,128)(2,1)S(1)}, u32[]{:S(2)}, u32[]{:S(2)}) %collective-permute-start.5) | collective-permute-done | bytes 921632 | tf_op jit(solution)/shard_map/cond/branch_2_fun/ppermute | solution.py:23
  230.9 1.4 convert_element_type.105
  232.2 5.5 %multiply_bitcast_fusion = (f32[1,720,640]{2,1,0:T(8,128)}, f32[1,720,640]{2,1,0:T(8,128)}) fusion(f32[720,640]{1,0:T(8,128)} %get-tuple-element.50, f32[720,640]{1,0:T(8,128)} %get-tuple-element.48, f32[720,640]{1,0:T(8,128)} %get-tuple-element.49, f32[720,640]{1,0:T(8,128)} %get-tuple-element.47), kind=kLoop, calls=%fused_computation.30 | loop fusion | flops 1843200 | bytes 11059200 | tf_op jit(solution)/shard_map/broadcast_in_dim | solution.py:94
  (23 shorter events, 0.7 us)
Async XLA Ops:
  7.2 31.8 %copy-start = (bf16[1,1536,640]{2,1,0:T(8,128)(2,1)S(1)}, bf16[1,1536,640]{2,1,0:T(8,128)(2,1)}, u32[]{:S(2)}) copy-start(bf16[1,1536,640]{2,1,0:T(8,128)(2,1)} %param.12) | copy-start | bytes 5898244
  7.2 88.2 %all-gather.2.cloned.1.call-start = ((), (), s32[]{:S(2)}) async-start(), calls=%async_computation.1 | async-start | bytes 8294400 | tf_op jit(solution)/shard_map/all_gather | solution.py:70
  9.9 5.0 %copy-start.4 = (f32[640]{0:T(1024)S(1)}, f32[640]{0:T(1024)}, u32[]{:S(2)}) copy-start(f32[640]{0:T(1024)} %param.14) | copy-start | bytes 7684
  9.9 5.0 %copy-start.5 = (f32[640]{0:T(1024)S(1)}, f32[640]{0:T(1024)}, u32[]{:S(2)}) copy-start(f32[640]{0:T(1024)} %param.13) | copy-start | bytes 7684
  9.9 170.1 %reduce-scatter.2.cloned.1.call-start = ((), (), s32[]{:S(2)}) async-start(), calls=%async_computation.2 | async-start | bytes 8294400 | tf_op jit(solution)/shard_map/reduce_scatter | solution.py:78
  27.9 2.3 copy-start.2
  57.6 37.7 %copy-start.3 = (bf16[1,1536,640]{2,1,0:T(8,128)(2,1)S(1)}, bf16[1,1536,640]{2,1,0:T(8,128)(2,1)}, u32[]{:S(2)}) copy-start(bf16[1,1536,640]{2,1,0:T(8,128)(2,1)} %param.11) | copy-start | bytes 5898244
  186.1 26.1 %collective-permute-start.4 = (bf16[720,640]{1,0:T(8,128)(2,1)S(1)}, bf16[720,640]{1,0:T(8,128)(2,1)S(1)}, u32[]{:S(2)}, u32[]{:S(2)}) collective-permute-start(bf16[720,640]{1,0:T(8,128)(2,1)S(1)} %convert_element_type.77), channel_id=1, source_target_pairs={{0,96},{8,104},{16,112},{24,120},{32,0},{40,8},{48,16},{56,24},{64... | collective-permute-start | bytes 2764808 | tf_op jit(solution)/shard_map/cond/branch_2_fun/ppermute | solution.py:23
  193.0 37.9 %collective-permute-start.5 = (bf16[720,640]{1,0:T(8,128)(2,1)S(1)}, bf16[720,640]{1,0:T(8,128)(2,1)S(1)}, u32[]{:S(2)}, u32[]{:S(2)}) collective-permute-start(bf16[720,640]{1,0:T(8,128)(2,1)S(1)} %convert_element_type.79), channel_id=1, source_target_pairs={{0,96},{8,104},{16,112},{24,120},{32,0},{40,8},{48,16},{56,24},{64... | collective-permute-start | bytes 2764808 | tf_op jit(solution)/shard_map/cond/branch_2_fun/ppermute | solution.py:23
  232.2 5.5 %copy-start.1 = (bf16[1,1536,640]{2,1,0:T(8,128)(2,1)S(1)}, bf16[1,1536,640]{2,1,0:T(8,128)(2,1)}, u32[]{:S(2)}) copy-start(bf16[1,1536,640]{2,1,0:T(8,128)(2,1)} %param.12) | copy-start | bytes 5898244
Sparse Core Ops, SparseCore 0:
  10.2 85.0 all-gather.1
  97.8 82.1 reduce-scatter.1
where the time goes:
time: 246 us; the launch traced here: 245 us
  waiting for transfers between devices  137 us (56%)
  matrix products  38.7 us (16%)
  other arithmetic  28.6 us (12%)
  local copies, waits for them, and re-layouts  19.1 us (8%)
  between operations  14.9 us (6%)
  starting transfers between devices  5.9 us (2%)
    reduce_scatter x1, waiting for transfers between devices, on_device(): lax.psum_scatter((scale * lax.dot_general(part_cols, upstream, (((0,), (0...  64.6 us
    all_gather x1, waiting for transfers between devices, on_device(): lax.all_gather(own_weight.astype(jnp.bfloat16), 'inner', axis=0, tiled=True)  36.9 us
    ppermute x2, waiting for transfers between devices, from_behind(): lax.ppermute(value, axis, [(i, (i + by) % devices) for i in range(devices)])  35.9 us
    dot_general x1, matrix products, on_device(): jnp.dot(part_cols, lax.all_gather(own_weight.astype(jnp.bfloat16), 'inner...  20.1 us
    dot_general x1, matrix products, on_device(): lax.dot_general(part_cols, upstream, (((0,), (0,)), ((), ())), preferred_...  18.6 us
    unnamed x19, local copies, waits for them, and re-layouts  11.4 us
    ppermute x2, starting transfers between devices, from_behind(): lax.ppermute(value, axis, [(i, (i + by) % devices) for i in range(devices)])  5.82 us
    slice x1, local copies, waits for them, and re-layouts, unfold(): padded[:, a:a + HEIGHT, b:b + WIDTH, :]  5.58 us
  transfers between devices with their start and end apart: 4, of which 4 were waited for; matrix products, arithmetic and copies ran while one was open for 29% of the time, Pallas kernels for 0%

commit v1 on v0

v1 whole, which is shorter than its diff:
```python
from functools import partial

import jax
import jax.numpy as jnp
from jax import lax
from jax.experimental import pallas as pl
from jax.experimental.pallas import tpu as pltpu
from jax.sharding import PartitionSpec as P

GN_GROUPS = 32
HEIGHT = 48
WIDTH = 32
PIXELS = HEIGHT * WIDTH
CHANS = 640
KROWS = 9 * CHANS
ROWS = KROWS // 8
SPAN = 3 * CHANS
HALF = 352
PADDED = PIXELS + 2 * WIDTH
SCALE = KROWS ** (-0.5)
MIB = 1 << 20


def send_inner(value, dy, dz):
    def place(i):
        return ((i // 4 + dy) % 2) * 4 + (i % 4 + dz) % 4

    return lax.ppermute(value, "inner", [(i, place(i)) for i in range(8)])


def from_partner(value, by):
    return lax.ppermute(value, "group", [(i, (i - by) % 16) for i in range(16)])


def weight_from_partner(own, other, by):
    group = lax.axis_index("group")
    value = jnp.where(group // 8 != ((group - by) % 16) // 8, other, own)
    pairs = []
    for i in range(16):
        to = (i - by) % 16
        for j in range(8):
            pairs.append((i * 8 + j, to * 8 + (j if i // 8 == to // 8 else (j + 4) % 8)))
    return lax.ppermute(value, ("group", "inner"), pairs)


def block_at(dy, dz):
    me = lax.axis_index("inner")
    return ((me // 4 + dy) % 2) * 4 + (me % 4 + dz) % 4


NEAR = [(0, 0), (0, 1), (0, 3), (0, 2), (1, 0), (1, 1), (1, 3), (1, 2)]


def group_mean(sums):
    chans = lax.broadcasted_iota(jnp.int32, (CHANS, 128), 0)
    first = lax.broadcasted_iota(jnp.int32, (CHANS, 128), 1) * (CHANS // GN_GROUPS)
    member = jnp.where((chans >= first) & (chans < first + CHANS // GN_GROUPS), 1.0, 0.0)
    total = jnp.broadcast_to(jnp.sum(sums, axis=0, keepdims=True), (8, CHANS))
    grouped = lax.dot_general(
        total, member, (((1,), (0,)), ((), ())), precision=lax.Precision.HIGHEST,
        preferred_element_type=jnp.float32,
    ) * (1.0 / (PIXELS * (CHANS // GN_GROUPS)))
    return lax.dot_general(
        grouped, member, (((1,), (1,)), ((), ())), precision=lax.Precision.HIGHEST,
        preferred_element_type=jnp.float32,
    )[0:1]


def shifted(value):
    place = lax.broadcasted_iota(jnp.int32, (WIDTH, CHANS), 0)
    before = jnp.where(place == 0, 0.0, pltpu.roll(value, 1, 0))
    after = jnp.where(place == WIDTH - 1, 0.0, pltpu.roll(value, WIDTH - 1, 0))
    return before, value, after


def row_at(r):
    return pl.ds(pl.multiple_of(r * WIDTH, WIDTH), WIDTH)


def spread_rows(src, ref, turn):
    blank = jnp.zeros((WIDTH, SPAN), jnp.bfloat16)
    ref[0:WIDTH, :] = blank
    ref[PADDED - WIDTH : PADDED, :] = blank

    @pl.loop(0, HEIGHT, unroll=4)
    def _(r):
        parts = shifted(src[row_at(r), :].astype(jnp.float32))
        for b in range(3):
            part = parts[2 - b if turn else b]
            ref[row_at(r + 1), b * CHANS : (b + 1) * CHANS] = part.astype(jnp.bfloat16)


def grad_half(dy, turned, cots, grads, outs, sem):
    half = block_at(dy, 0) // 4
    first = half * 4

    def place(q):
        tap = q // 5
        return tap, pl.multiple_of((q - tap * 5) * 128, 128)

    def load(q):
        tap, col = place(q)
        a = (first + tap) // 3
        b = first + tap - 3 * a
        rows = pl.ds(pl.multiple_of((2 - a) * WIDTH, WIDTH), PIXELS)
        return cots[rows, pl.ds(pl.multiple_of(b * CHANS + col, 128), 128)]

    def tile(q, wide):
        right = jnp.concatenate([load(q + i) for i in range(wide)], axis=1)
        found = SCALE * jnp.dot(turned[...], right, preferred_element_type=jnp.float32)
        found = found.astype(jnp.bfloat16)
        for i in range(wide):
            tap, col = place(q + i)
            rows = pl.ds(pl.multiple_of(tap * CHANS, CHANS), CHANS)
            grads[rows, pl.ds(col, 128)] = found[:, i * 128 : (i + 1) * 128]

    @pl.loop(0, 24 // TILE)
    def _(j):
        tile(TILE * j, TILE)

    tile(24, 1)
    copies = []
    for j, dz in enumerate((0, 1, 3, 2)):
        begin = half * (4 * ROWS - 4 * CHANS) + (block_at(0, dz) % 4) * ROWS
        rows = pl.ds(pl.multiple_of(begin, 16), ROWS)
        copies.append(pltpu.make_async_copy(grads.at[rows], outs[j], sem.at[j]))
        copies[-1].start()
    for copy in copies:
        copy.wait()


def norm_grad_kernel(lat, cot, gain, bias, hidden_out, turned_out, *rest):
    outs, (hidden, turned, cots, grads, sem, sem_out) = rest[:4], rest[4:]

    def chunk_at(r):
        return pl.ds(pl.multiple_of(r * CHUNK, CHUNK), CHUNK)

    def chunk_of(r):
        return lat[chunk_at(r), :].astype(jnp.float32)

    def fold(value):
        return jnp.sum(value.reshape(CHUNK // 8, 8, CHANS), axis=0)

    chunks = PIXELS // CHUNK
    zeros = jnp.zeros((8, CHANS), jnp.float32)
    center = group_mean(lax.fori_loop(0, chunks, lambda r, s: s + fold(chunk_of(r)), zeros))

    def squares(r, s):
        off = chunk_of(r) - center
        return s + fold(off * off)

    var = group_mean(lax.fori_loop(0, chunks, squares, zeros))
    slope = lax.rsqrt(var + 1e-05) * gain[...]
    shift = bias[...]

    @pl.loop(0, chunks)
    def _(r):
        halved = 0.5 * ((chunk_of(r) - center) * slope + shift)
        rounded = (halved + halved * jnp.tanh(halved)).astype(jnp.bfloat16)
        hidden[chunk_at(r), :] = rounded
        turned[:, chunk_at(r)] = rounded.T

    spread_rows(cot, cots, True)
    keep = [
        pltpu.make_async_copy(hidden, hidden_out, sem_out.at[0]),
        pltpu.make_async_copy(turned, turned_out, sem_out.at[1]),
    ]
    for copy in keep:
        copy.start()
    grad_half(1, turned, cots, grads, outs, sem)
    for copy in keep:
        copy.wait()


def rest_grad_kernel(turned, cot, *rest):
    outs, (cots, grads, sem) = rest[:4], rest[4:]
    spread_rows(cot, cots, True)
    grad_half(0, turned, cots, grads, outs, sem)


def spread_kernel(hidden, taps):
    spread_rows(hidden, taps, False)


GRAD_SCRATCH = [
    pltpu.VMEM((PADDED, SPAN), jnp.bfloat16),
    pltpu.VMEM((5 * CHANS, CHANS), jnp.bfloat16),
    pltpu.SemaphoreType.DMA((4,)),
]
TILE = 6
WINDOW = 7 * 128
TALL = 512
STEPS = PIXELS // TALL
CHUNK = 128
SHORT = pl.CostEstimate(flops=10**6, bytes_accessed=10**5, transcendentals=0)
IN_VMEM = pl.BlockSpec(memory_space=pltpu.VMEM)
IN_ANY = pl.BlockSpec(memory_space=pl.ANY)


def norm_grad(latents, cotangent, gain, bias):
    return pl.pallas_call(
        norm_grad_kernel,
        out_shape=[
            jax.ShapeDtypeStruct((PIXELS, CHANS), jnp.bfloat16),
            jax.ShapeDtypeStruct((CHANS, PIXELS), jnp.bfloat16),
        ] + [jax.ShapeDtypeStruct((ROWS, CHANS), jnp.bfloat16)] * 4,
        in_specs=[IN_VMEM] * 4,
        out_specs=[IN_ANY] * 6,
        scratch_shapes=[
            pltpu.VMEM((PIXELS, CHANS), jnp.bfloat16),
            pltpu.VMEM((CHANS, PIXELS), jnp.bfloat16),
        ] + GRAD_SCRATCH + [pltpu.SemaphoreType.DMA((2,))],
        compiler_params=pltpu.CompilerParams(vmem_limit_bytes=58 * MIB),
        cost_estimate=SHORT,
        name="norm_grad",
    )(latents, cotangent, gain[None], bias[None])


def rest_grad(turned, cotangent):
    return pl.pallas_call(
        rest_grad_kernel,
        out_shape=[jax.ShapeDtypeStruct((ROWS, CHANS), jnp.bfloat16)] * 4,
        in_specs=[IN_VMEM] * 2,
        out_specs=[IN_ANY] * 4,
        scratch_shapes=GRAD_SCRATCH,
        compiler_params=pltpu.CompilerParams(vmem_limit_bytes=58 * MIB),
        cost_estimate=SHORT,
        name="rest_grad",
    )(turned, cotangent)


def spread(hidden):
    return pl.pallas_call(
        spread_kernel,
        out_shape=jax.ShapeDtypeStruct((PADDED, SPAN), jnp.bfloat16),
        in_specs=[IN_VMEM],
        out_specs=IN_VMEM,
        compiler_params=pltpu.CompilerParams(vmem_limit_bytes=20 * MIB),
        cost_estimate=SHORT,
        name="spread",
    )(hidden)


def conv_kernel(places, last, *refs):
    count = len(places)
    taps_hbm, pieces, refs = refs[0], refs[1 : 1 + count], refs[1 + count :]
    before_hbm = lat_hbm = None
    if last:
        before_hbm, lat_hbm, refs = refs[0], refs[1], refs[2:]
    out_hbm, taps, weights, before, lat, out, sem_w, sem_in, sem_out = refs

    def rows_of(m):
        return pl.ds(pl.multiple_of(m * TALL, TALL), TALL)

    def inputs(m):
        rows = pl.ds(pl.multiple_of(m * TALL + 2 * WIDTH, 2 * WIDTH), TALL)
        found = [pltpu.make_async_copy(taps_hbm.at[rows], taps.at[rows], sem_in.at[3 * m])]
        if last:
            rows = rows_of(m)
            found.append(pltpu.make_async_copy(before_hbm.at[rows], before.at[rows], sem_in.at[3 * m + 1]))
            found.append(pltpu.make_async_copy(lat_hbm.at[rows], lat.at[rows], sem_in.at[3 * m + 2]))
        return found

    def result(m):
        return pltpu.make_async_copy(out.at[rows_of(m)], out_hbm.at[rows_of(m)], sem_out.at[m])

    weights[...] = jnp.zeros_like(weights)
    head = pl.ds(0, 2 * WIDTH)
    copies = [pltpu.make_async_copy(taps_hbm.at[head], taps.at[head], sem_in.at[3 * STEPS])]
    copies[0].start()
    tiles = []
    blocks = list(dict.fromkeys(place[:2] for place in places))
    for j, (dy, dz, row, rows) in enumerate(places):
        block = block_at(dy, dz)
        base = block * ROWS // 128
        slot = blocks.index((dy, dz)) * WINDOW
        to = pl.ds(pl.multiple_of(slot + block * ROWS - base * 128 + row, 16), rows)
        copies.append(pltpu.make_async_copy(pieces[j], weights.at[to], sem_w.at[j]))
        copies[-1].start()
        if row == 0:
            for k in range(WINDOW // 128):
                tile = jnp.minimum(base + k, KROWS // 128 - 1)
                a = tile // (SPAN // 128)
                tiles.append((a * WIDTH, pl.multiple_of(tile * 128 - a * SPAN, 128)))
    for copy in inputs(0):
        copy.start()
    for copy in copies + inputs(0):
        copy.wait()
    for m in range(1, STEPS):
        for copy in inputs(m):
            copy.start()

    @pl.loop(0, STEPS)
    def _(m):
        @pl.when(m > 0)
        def _():
            for copy in inputs(m):
                copy.wait()

        left = jnp.concatenate([
            taps[pl.ds(pl.multiple_of(m * TALL + down, WIDTH), TALL), pl.ds(lane, 128)]
            for down, lane in tiles
        ], axis=1)
        total = jnp.dot(left, weights[...], preferred_element_type=jnp.float32)
        if last:
            total += before[rows_of(m), :].astype(jnp.float32)
            total = lat[rows_of(m), :].astype(jnp.float32) + SCALE * total
        out[rows_of(m), :] = total.astype(jnp.bfloat16)
        result(m).start()

    for m in range(STEPS):
        result(m).wait()


def conv(taps, places, pieces, others=()):
    blocks = len(set(place[:2] for place in places))
    return pl.pallas_call(
        partial(conv_kernel, places, len(others) > 0),
        out_shape=jax.ShapeDtypeStruct((PIXELS, CHANS), jnp.bfloat16),
        in_specs=[IN_ANY] * (1 + len(pieces) + len(others)),
        out_specs=IN_ANY,
        scratch_shapes=[
            pltpu.VMEM((PADDED, SPAN), jnp.bfloat16),
            pltpu.VMEM((blocks * WINDOW, CHANS), jnp.bfloat16),
            pltpu.VMEM((PIXELS, CHANS), jnp.bfloat16),
            pltpu.VMEM((PIXELS, CHANS), jnp.bfloat16),
            pltpu.VMEM((PIXELS, CHANS), jnp.bfloat16),
            pltpu.SemaphoreType.DMA((len(pieces),)),
            pltpu.SemaphoreType.DMA((3 * STEPS + 1,)),
            pltpu.SemaphoreType.DMA((STEPS,)),
        ],
        compiler_params=pltpu.CompilerParams(vmem_limit_bytes=58 * MIB),
        cost_estimate=SHORT,
        name="conv",
    )(taps, *pieces, *others)


def together(values, *others):
    return lax.optimization_barrier(tuple(values) + others)[: len(values)]


def add(*values):
    return sum(v.astype(jnp.float32) for v in values).astype(jnp.bfloat16)


def from_switch(step, branch, *state):
    return lax.switch(step[0] % 4, [partial(branch, 1 << level) for level in range(4)], *state)


def partner_and_conv(by, own, other, taps, w_m, w_p, top, bottom):
    w_partner = weight_from_partner(own, other, by)
    places = [
        (0, 0, 0, ROWS), (1, 0, 0, ROWS), (0, 3, 0, ROWS), (0, 1, 0, ROWS),
        (0, 2, 0, HALF), (0, 2, HALF, ROWS - HALF),
    ]
    return w_partner, conv(taps, places, (own, other, w_m, w_p, top, bottom))


def sums_kernel(a_y, g02, a_p, a_m, g10, far_top, far_bottom, near):
    def add(rows, *refs):
        return sum(ref[rows, :].astype(jnp.float32) for ref in refs).astype(jnp.bfloat16)

    far_top[...] = add(slice(0, HALF), a_y, g02)
    far_bottom[...] = add(slice(HALF, ROWS), a_y, g02)
    near[...] = add(slice(0, ROWS), a_p, a_m, g10)


def sums(*values):
    return pl.pallas_call(
        sums_kernel,
        out_shape=[jax.ShapeDtypeStruct((rows, CHANS), jnp.bfloat16) for rows in (HALF, ROWS - HALF, ROWS)],
        in_specs=[IN_VMEM] * 5,
        out_specs=[IN_VMEM] * 3,
        compiler_params=pltpu.CompilerParams(vmem_limit_bytes=20 * MIB),
        cost_estimate=SHORT,
        name="sums",
    )(*values)


def finish(by, moved, own_weight, w_partner):
    partner = from_partner(moved.astype(jnp.bfloat16), by).astype(jnp.float32)
    both = moved + partner
    new_moment = 0.5 * both
    new_weight = 0.5 * (own_weight + w_partner.astype(jnp.float32)) - 0.025 * both
    return new_weight, new_moment


def on_device(latents, cotangent, gain, bias, weight, momentum, step):
    latents, cotangent, own_weight, own_moment = latents[0], cotangent[0], weight[0], momentum[0]
    own = own_weight.astype(jnp.bfloat16)
    w_y = send_inner(own, 1, 0)
    w_m = send_inner(own, 0, 1)
    w_p = send_inner(own, 0, -1)
    latents, cotangent = together((latents, cotangent), own)
    hidden, turned, g10, g1p, g1m, g12 = norm_grad(latents, cotangent, gain, bias)
    g12, g1p, g1m, w_m, w_p, w_y = together((g12, g1p, g1m, w_m, w_p, w_y))
    a_y = send_inner(g12, 1, 0)
    a_p = send_inner(g1p, 0, 1)
    a_m = send_inner(g1m, 0, -1)
    top = send_inner(w_m[:HALF], 0, 1)
    bottom = send_inner(w_p[HALF:], 0, -1)
    g00, g0p, g0m, g02 = rest_grad(turned, cotangent)
    far_top, far_bottom, near = sums(a_y, g02, a_p, a_m, g10)
    b_up = send_inner(far_top, 0, 1)
    b_dn = send_inner(far_bottom, 0, -1)
    near, top, bottom, hidden = together((near, top, bottom, hidden))
    b_y = send_inner(near, 1, 0)
    corner = send_inner(jnp.concatenate([top, bottom]), 1, 0)
    taps = spread(hidden)
    b_up, b_dn, taps = together((b_up, b_dn, taps))
    to_up = jnp.concatenate([add(b_up, g0p[:HALF]), g0p[HALF:]])
    to_dn = jnp.concatenate([g0m[:HALF], add(b_dn, g0m[HALF:])])
    c_up = send_inner(to_up, 0, 1)
    c_dn = send_inner(to_dn, 0, -1)
    taps = together((taps,), to_up, to_dn)[0]
    w_partner, acc = from_switch(step, partner_and_conv, own, w_y, taps, w_m, w_p, top, bottom)
    w_y = together((w_y,), acc)[0]
    y_m = send_inner(w_y, 0, 1)
    y_p = send_inner(w_y, 0, -1)
    grad = (
        g00.astype(jnp.float32) + b_y.astype(jnp.float32)
        + c_up.astype(jnp.float32) + c_dn.astype(jnp.float32)
    )
    moved = 0.9 * own_moment + grad
    new_weight, new_moment = from_switch(step, finish, moved, own_weight, w_partner)
    y_m, y_p, corner = together((y_m, y_p, corner), new_weight, new_moment)
    places = [(1, 2, 0, ROWS), (1, 3, 0, ROWS), (1, 1, 0, ROWS)]
    block_out = conv(taps, places, (corner, y_m, y_p), (acc, latents))
    return (block_out[None], new_weight[None], new_moment[None])


def solution(mesh):
    placed = (
        P(("group", "inner"), None, None),
        P(("group", "inner"), None, None),
        P(),
        P(),
        P("group", "inner", None),
        P("group", "inner", None),
        P(),
    )
    return jax.shard_map(
        on_device,
        mesh=mesh,
        in_specs=placed,
        out_specs=(
            P(("group", "inner"), None, None),
            P("group", "inner", None),
            P("group", "inner", None),
        ),
        check_vma=False,
    )
```

time: 246 us -> 147 us (0.60)
  waiting for transfers between devices: 137 us -> 32.6 us
  Pallas kernels: 0 us -> 63.4 us
  matrix products: 38.7 us -> 0 us
  starting transfers between devices: 5.9 us -> 27.7 us
  other arithmetic: 28.6 us -> 14.3 us
  between operations: 14.9 us -> 1.68 us
  local copies, waits for them, and re-layouts: 19.1 us -> 6.96 us
    reduce_scatter x1 -> x0, waiting for transfers between devices: 64.6 us -> none  [on_device(): lax.psum_scatter((scale * lax.dot_general(part_cols, upstream, (((0,), (0...]
    pallas_call x0 -> x6, Pallas kernels: none -> 63.4 us  [the longest x2 27.3 us: conv(): pl.pallas_call(partial(conv_kernel, places, len(others) > 0), out_shape=j...]
    dot_general x2 -> x0, matrix products: 38.7 us -> none  [the longest x1 20.1 us: on_device(): jnp.dot(part_cols, lax.all_gather(own_weight.astype(jnp.bfloat16), 'inner...]
    all_gather x1 -> x0, waiting for transfers between devices: 36.9 us -> none  [on_device(): lax.all_gather(own_weight.astype(jnp.bfloat16), 'inner', axis=0, tiled=True)]
    ppermute x2 -> x18, starting transfers between devices: 5.82 us -> 27.7 us  [the longest x16 21.4 us: send_inner(): return lax.ppermute(value, 'inner', [(i, place(i)) for i in range(8)])]
    convert_element_type x6 -> x4, other arithmetic: 11.5 us -> 1.95 us  [the longest x1 1.61 us: on_device(): own = own_weight.astype(jnp.bfloat16)]
    unnamed x19 -> x26, local copies, waits for them, and re-layouts: 11.4 us -> 3.88 us
    broadcast_in_dim x1 -> x0, other arithmetic: 5.49 us -> none  [on_device(): return (block_out, new_weight[None], new_moment[None])]
  transfers between devices with their start and end apart: 4 -> 18, of which waited for: 4 -> 6; matrix products, arithmetic and copies ran while one was open for 29% -> 11% of each run, Pallas kernels for 0% -> 36%
where the time goes in v1:
time: 147 us
  Pallas kernels  63.4 us (43%)
  waiting for transfers between devices  32.6 us (22%)
  starting transfers between devices  27.7 us (19%)
  other arithmetic  14.3 us (10%)
  local copies, waits for them, and re-layouts  6.96 us (5%)
  between operations  1.68 us (1%)
    pallas_call x2, Pallas kernels, conv(): pl.pallas_call(partial(conv_kernel, places, len(others) > 0), out_shape=j...  27.3 us
    ppermute x16, starting transfers between devices, send_inner(): return lax.ppermute(value, 'inner', [(i, place(i)) for i in range(8)])  21.4 us
    ppermute x16, waiting for transfers between devices, send_inner(): return lax.ppermute(value, 'inner', [(i, place(i)) for i in range(8)])  19.6 us
    pallas_call x1, Pallas kernels, norm_grad(): pl.pallas_call(norm_grad_kernel, out_shape=[jax.ShapeDtypeStruct((PIXELS,...  18.1 us
    pallas_call x1, Pallas kernels, rest_grad(): pl.pallas_call(rest_grad_kernel, out_shape=[jax.ShapeDtypeStruct((ROWS, C...  13.5 us
    ppermute x1, waiting for transfers between devices, from_partner(): return lax.ppermute(value, 'group', [(i, (i - by) % 16) for i in range(16)])  13 us
    ppermute x1, starting transfers between devices, weight_from_partner(): return lax.ppermute(value, ('group', 'inner'), pairs)  4.26 us
    pallas_call x1, Pallas kernels, spread(): pl.pallas_call(spread_kernel, out_shape=jax.ShapeDtypeStruct((PADDED, SPA...  3.92 us
  transfers between devices with their start and end apart: 18, of which 6 were waited for; matrix products, arithmetic and copies ran while one was open for 11% of the time, Pallas kernels for 36%

profile of v1, /device:TPU:0, one launch (start us, length us, event | category | flops | bytes accessed | tf_op | source)
XLA Modules:
  0.0 146.7 jit_solution(12824158735097099027)
XLA Ops:
  0.7 1.6 %bitcast_convert_fusion = bf16[720,640]{1,0:T(8,128)(2,1)S(1)} fusion(f32[1,720,640]{2,1,0:T(8,128)} %param.19), kind=kLoop, calls=%fused_computation.22 | loop fusion | flops 460800 | bytes 2764800 | tf_op jit(solution)/shard_map/convert_element_type | solution.py:390
  2.3 1.7 %collective-permute-start.10 = (bf16[720,640]{1,0:T(8,128)(2,1)S(1)}, bf16[720,640]{1,0:T(8,128)(2,1)}, u32[]{:S(2)}, u32[]{:S(2)}) collective-permute-start(bf16[720,640]{1,0:T(8,128)(2,1)S(1)} %bitcast_convert_fusion), channel_id=1, source_target_pairs={{0,4},{1,5},{2,6},{3,7},{4,0},{5,1},{6,2},{7,3},{8,12},{9,13},{10,... | collective-permute-start | bytes 2764808 | tf_op jit(solution)/shard_map/ppermute | solution.py:28
  4.0 1.9 %collective-permute-start.8 = (bf16[720,640]{1,0:T(8,128)(2,1)S(1)}, bf16[720,640]{1,0:T(8,128)(2,1)S(1)}, u32[]{:S(2)}, u32[]{:S(2)}) collective-permute-start(bf16[720,640]{1,0:T(8,128)(2,1)S(1)} %bitcast_convert_fusion), channel_id=1, source_target_pairs={{0,1},{1,2},{2,3},{3,0},{4,5},{5,6},{6,7},{7,4},{8,9},{9,10},{10,1... | collective-permute-start | bytes 2764808 | tf_op jit(solution)/shard_map/ppermute | solution.py:28
  5.9 2.1 %collective-permute-start.9 = (bf16[720,640]{1,0:T(8,128)(2,1)S(1)}, bf16[720,640]{1,0:T(8,128)(2,1)S(1)}, u32[]{:S(2)}, u32[]{:S(2)}) collective-permute-start(bf16[720,640]{1,0:T(8,128)(2,1)S(1)} %bitcast_convert_fusion), channel_id=1, source_target_pairs={{0,3},{1,0},{2,1},{3,2},{4,7},{5,4},{6,5},{7,6},{8,11},{9,8},{10,9... | collective-permute-start | bytes 2764808 | tf_op jit(solution)/shard_map/ppermute | solution.py:28
  9.2 18.1 %norm_grad.1 = (bf16[1536,640]{1,0:T(8,128)(2,1)}, bf16[640,1536]{1,0:T(8,128)(2,1)}, bf16[720,640]{1,0:T(8,128)(2,1)}, bf16[720,640]{1,0:T(8,128)(2,1)}, bf16[7...) custom-call(bf16[1536,640]{1,0:T(8,128)(2,1)} %bitcast.19, bf16[1536,640]{1,0:T(8,128)(2,1)} %bitcast.17, ...), custom_call_target="tpu_custom_call" | custom-call | flops 1000000 | bytes 100000 | tf_op jit(solution)/shard_map/norm_grad/pallas_call | solution.py:201
  28.2 0.9 copy-done.6
  29.9 2.9 %collective-permute-start.13 = (bf16[720,640]{1,0:T(8,128)(2,1)}, bf16[720,640]{1,0:T(8,128)(2,1)S(1)}, u32[]{:S(2)}, u32[]{:S(2)}) collective-permute-start(bf16[720,640]{1,0:T(8,128)(2,1)} %get-tuple-element.169), channel_id=1, source_target_pairs={{0,3},{1,0},{2,1},{3,2},{4,7},{5,4},{6,5},{7,6},{8,11},{9,8},{10,9... | collective-permute-start | bytes 2764808 | tf_op jit(solution)/shard_map/ppermute | solution.py:28
  34.4 13.5 %rest_grad.1 = (bf16[720,640]{1,0:T(8,128)(2,1)}, bf16[720,640]{1,0:T(8,128)(2,1)}, bf16[720,640]{1,0:T(8,128)(2,1)}, bf16[720,640]{1,0:T(8,128)(2,1)}) custom-call(bf16[640,1536]{1,0:T(8,128)(2,1)} %get-tuple-element.166.turned, bf16[1536,640]{1,0:T(8,128)(2,1)} %bitcast.18), custom_call_target="tpu_custom_call" | custom-call | flops 1000000 | bytes 100000 | tf_op jit(solution)/shard_map/rest_grad/pallas_call | solution.py:220
  47.9 2.7 %collective-permute-done.11.a_y = bf16[720,640]{1,0:T(8,128)(2,1)S(1)} collective-permute-done((bf16[720,640]{1,0:T(8,128)(2,1)}, bf16[720,640]{1,0:T(8,128)(2,1)S(1)}, u32[]{:S(2)}, u32[]{:S(2)}) %collective-permute-start.11) | collective-permute-done | bytes 921632 | tf_op jit(solution)/shard_map/ppermute | solution.py:28
  50.7 1.4 collective-permute-done.12.a_p
  52.0 2.0 %collective-permute-done.13.a_m = bf16[720,640]{1,0:T(8,128)(2,1)S(1)} collective-permute-done((bf16[720,640]{1,0:T(8,128)(2,1)}, bf16[720,640]{1,0:T(8,128)(2,1)S(1)}, u32[]{:S(2)}, u32[]{:S(2)}) %collective-permute-start.13) | collective-permute-done | bytes 921632 | tf_op jit(solution)/shard_map/ppermute | solution.py:28
  54.0 1.2 copy-done.2
  55.8 3.7 %collective-permute-start.15 = (bf16[368,640]{1,0:T(8,128)(2,1)S(1)}, bf16[368,640]{1,0:T(8,128)(2,1)S(1)}, u32[]{:S(2)}, u32[]{:S(2)}) collective-permute-start(bf16[368,640]{1,0:T(8,128)(2,1)S(1)} %get-tuple-element.172), channel_id=1, source_target_pairs={{0,3},{1,0},{2,1},{3,2},{4,7},{5,4},{6,5},{7,6},{8,11},{9,8},{10,9... | collective-permute-start | bytes 1413128 | tf_op jit(solution)/shard_map/ppermute | solution.py:28
  59.5 1.1 slice.18
  60.8 12.6 %collective-permute-done.16 = bf16[352,640]{1,0:T(8,128)(2,1)S(1)} collective-permute-done((bf16[352,640]{1,0:T(8,128)(2,1)S(1)}, bf16[352,640]{1,0:T(8,128)(2,1)S(1)}, u32[]{:S(2)}, u32[]{:S(2)}) %collective-permute-start.16) | collective-permute-done | bytes 450592 | tf_op jit(solution)/shard_map/ppermute | solution.py:28
  74.3 1.6 %collective-permute-start.21 = (bf16[720,640]{1,0:T(8,128)(2,1)S(1)}, bf16[720,640]{1,0:T(8,128)(2,1)}, u32[]{:S(2)}, u32[]{:S(2)}) collective-permute-start(bf16[720,640]{1,0:T(8,128)(2,1)S(1)} %get-tuple-element.191), channel_id=1, source_target_pairs={{0,4},{1,5},{2,6},{3,7},{4,0},{5,1},{6,2},{7,3},{8,12},{9,13},{10,... | collective-permute-start | bytes 2764808 | tf_op jit(solution)/shard_map/ppermute | solution.py:28
  75.9 3.9 %spread.1.refs_0_ = bf16[1600,1920]{1,0:T(8,128)(2,1)} custom-call(bf16[1536,640]{1,0:T(8,128)(2,1)S(1)} %copy-done), custom_call_target="tpu_custom_call" | custom-call | flops 1000000 | bytes 100000 | tf_op jit(solution)/shard_map/spread/pallas_call | solution.py:233
  79.9 1.0 pad_maximum_fusion.1
  81.1 1.0 pad_maximum_fusion
  82.1 2.0 %collective-permute-start.22 = (bf16[720,640]{1,0:T(8,128)(2,1)}, bf16[720,640]{1,0:T(8,128)(2,1)}, u32[]{:S(2)}, u32[]{:S(2)}) collective-permute-start(bf16[720,640]{1,0:T(8,128)(2,1)} %pad_maximum_fusion), channel_id=1, source_target_pairs={{0,1},{1,2},{2,3},{3,0},{4,5},{5,6},{6,7},{7,4},{8,9},{9,10},{10,1... | collective-permute-start | bytes 2764808 | tf_op jit(solution)/shard_map/ppermute | solution.py:28
  84.8 2.0 %pad_maximum_fusion.2 = bf16[720,640]{1,0:T(8,128)(2,1)} fusion(bf16[368,640]{1,0:T(8,128)(2,1)S(1)} %collective-permute-done.17, bf16[352,640]{1,0:T(8,128)(2,1)} %copy-done.11), kind=kLoop, calls=%fused_computation.20 | loop fusion | flops 1843200 | bytes 1843200 | tf_op jit(solution)/shard_map/concatenate | solution.py:408
  87.2 21.7 %conditional.2 = (bf16[720,640]{1,0:T(8,128)(2,1)}, bf16[1536,640]{1,0:T(8,128)(2,1)}) conditional(s32[]{:T(128)} %clamp.4, (bf16[720,640]{1,0:T(8,128)(2,1)}, bf16[720,640]{1,0:T(8,128)(2,1)S(1)}, bf16[1600,1920]{1,0:T(8,128)(2,1)}, bf16[720,640]{1,0:T(8,128)(2,1)}, bf16[720,640]{1,0:T(8,128)(2,1)S(1)}, ...), branch_computations={%region_0.1_spmd, %region_1.2_spmd, %region_2.3_spmd, %region_3.4_... | conditional | flops 1460846 | bytes 12040415 | solution.py:347
  87.2 1.4 broadcast_select_fusion.2
  88.6 4.3 %collective-permute-start.2 = (bf16[720,640]{1,0:T(8,128)(2,1)S(1)}, bf16[720,640]{1,0:T(8,128)(2,1)}, u32[]{:S(2)}, u32[]{:S(2)}) collective-permute-start(bf16[720,640]{1,0:T(8,128)(2,1)S(1)} %broadcast_select_fusion.2), channel_id=1, source_target_pairs={{0,100},{1,101},{2,102},{3,103},{4,96},{5,97},{6,98},{7,99},{8,108... | collective-permute-start | bytes 2764808 | tf_op jit(solution)/shard_map/cond/branch_2_fun/ppermute | solution.py:43
  92.9 16.1 %conv.7 = bf16[1536,640]{1,0:T(8,128)(2,1)} custom-call(bf16[1600,1920]{1,0:T(8,128)(2,1)} %get-tuple-element.96.refs_0_, bf16[720,640]{1,0:T(8,128)(2,1)S(1)} %get-tuple-element.95.refs_1_, bf16[720,640]{1,0:T(8,128)(2,1)} %get-tuple-element.94.refs_2_, bf16[720,640]{1,0:T(8,128)(2,1)S(1)} %copy-done.9, bf16[720,640]{1,0:T(8,128)(2,1)S(1)} %get-tuple-element.98.refs_4_, ...), custom_call_target="tpu_custom_call" | custom-call | flops 1000000 | bytes 100000 | tf_op jit(solution)/shard_map/cond/branch_2_fun/conv/pallas_call | solution.py:317
  109.1 3.2 %collective-permute-start.19 = (bf16[720,640]{1,0:T(8,128)(2,1)}, bf16[720,640]{1,0:T(8,128)(2,1)}, u32[]{:S(2)}, u32[]{:S(2)}) collective-permute-start(bf16[720,640]{1,0:T(8,128)(2,1)} %collective-permute-done.10), channel_id=1, source_target_pairs={{0,3},{1,0},{2,1},{3,2},{4,7},{5,4},{6,5},{7,6},{8,11},{9,8},{10,9... | collective-permute-start | bytes 2764808 | tf_op jit(solution)/shard_map/ppermute | solution.py:28
  112.3 3.3 %bitcast_add_fusion = f32[720,640]{1,0:T(8,128)S(1)} fusion(bf16[720,640]{1,0:T(8,128)(2,1)} %collective-permute-done.23, bf16[720,640]{1,0:T(8,128)(2,1)} %collective-permute-done.22, bf16[720,640]{1,0:T(8,128)(2,1)} %collective-permute-done.21, bf16[720,640]{1,0:T(8,128)(2,1)} %get-tuple-element.190, f32[1,720,640]{2,1,0:T(8,128)} %param.20), kind=kLoop, calls=%fused_computation.16 | loop fusion | flops 4147200 | bytes 7372800 | tf_op jit(solution)/shard_map/add | solution.py:424
  115.6 18.8 %conditional.3 = (f32[720,640]{1,0:T(8,128)}, f32[720,640]{1,0:T(8,128)}) conditional(s32[]{:T(128)} %clamp.4, (bf16[720,640]{1,0:T(8,128)(2,1)}, f32[720,640]{1,0:T(8,128)S(1)}, f32[720,640]{1,0:T(8,128)S(1)}) %tuple.69, (bf16[720,640]{1,0:T(8,128)(2,1)}, f32[720,640]{1,0:T(8,128)S(1)}, ...), branch_computations={%region_4.5_spmd, %region_5.6_spmd, %region_6.7_spmd, %region_7.8_... | conditional | flops 4147200 | bytes 15667256 | solution.py:347
  115.7 2.0 %collective-permute-start.6 = (bf16[720,640]{1,0:T(8,128)(2,1)S(1)}, bf16[720,640]{1,0:T(8,128)(2,1)S(1)}, u32[]{:S(2)}, u32[]{:S(2)}) collective-permute-start(bf16[720,640]{1,0:T(8,128)(2,1)S(1)} %convert_element_type.53), channel_id=1, source_target_pairs={{0,96},{8,104},{16,112},{24,120},{32,0},{40,8},{48,16},{56,24},{64... | collective-permute-start | bytes 2764808 | tf_op jit(solution)/shard_map/cond/branch_2_fun/ppermute | solution.py:32
  117.8 13.0 %collective-permute-done.6 = bf16[720,640]{1,0:T(8,128)(2,1)S(1)} collective-permute-done((bf16[720,640]{1,0:T(8,128)(2,1)S(1)}, bf16[720,640]{1,0:T(8,128)(2,1)S(1)}, u32[]{:S(2)}, u32[]{:S(2)}) %collective-permute-start.6) | collective-permute-done | bytes 921632 | tf_op jit(solution)/shard_map/cond/branch_2_fun/ppermute | solution.py:32
  130.7 3.6 %fusion.2 = (f32[720,640]{1,0:T(8,128)}, f32[720,640]{1,0:T(8,128)}) fusion(f32[720,640]{1,0:T(8,128)S(1)} %get-tuple-element.116, bf16[720,640]{1,0:T(8,128)(2,1)S(1)} %collective-permute-done.6, f32[720,640]{1,0:T(8,128)S(1)} %get-tuple-element.114, bf16[720,640]{1,0:T(8,128)(2,1)} %get-tuple-element.115), kind=kLoop, calls=%fused_computation.12 | loop fusion | flops 3686400 | bytes 9216000 | tf_op jit(solution)/shard_map/cond/branch_2_fun/mul | solution.py:383
  135.3 11.2 %conv.9 = bf16[1536,640]{1,0:T(8,128)(2,1)} custom-call(bf16[1600,1920]{1,0:T(8,128)(2,1)} %spread.1.refs_0_, bf16[720,640]{1,0:T(8,128)(2,1)} %collective-permute-done.20.refs_1_, bf16[720,640]{1,0:T(8,128)(2,1)} %copy-done.18, bf16[720,640]{1,0:T(8,128)(2,1)} %collective-permute-done.19.refs_3_, bf16[1536,640]{1,0:T(8,128)(2,1)} %get-tuple-element.187.refs_4_, ...), custom_call_target="tpu_custom_call" | custom-call | flops 1000000 | bytes 100000 | tf_op jit(solution)/shard_map/conv/pallas_call | solution.py:317
  (58 shorter events, 7.8 us)
Async XLA Ops:
  0.6 7.4 %copy-start.19 = (f32[640]{0:T(1024)S(1)}, f32[640]{0:T(1024)}, u32[]{:S(2)}) copy-start(f32[640]{0:T(1024)} %param.17) | copy-start | bytes 7684
  0.6 8.0 %copy-start.20 = (f32[640]{0:T(1024)S(1)}, f32[640]{0:T(1024)}, u32[]{:S(2)}) copy-start(f32[640]{0:T(1024)} %param.18) | copy-start | bytes 7684
  2.3 25.1 %collective-permute-start.10 = (bf16[720,640]{1,0:T(8,128)(2,1)S(1)}, bf16[720,640]{1,0:T(8,128)(2,1)}, u32[]{:S(2)}, u32[]{:S(2)}) collective-permute-start(bf16[720,640]{1,0:T(8,128)(2,1)S(1)} %bitcast_convert_fusion), channel_id=1, source_target_pairs={{0,4},{1,5},{2,6},{3,7},{4,0},{5,1},{6,2},{7,3},{8,12},{9,13},{10,... | collective-permute-start | bytes 2764808 | tf_op jit(solution)/shard_map/ppermute | solution.py:28
  4.0 24.2 %collective-permute-start.8 = (bf16[720,640]{1,0:T(8,128)(2,1)S(1)}, bf16[720,640]{1,0:T(8,128)(2,1)S(1)}, u32[]{:S(2)}, u32[]{:S(2)}) collective-permute-start(bf16[720,640]{1,0:T(8,128)(2,1)S(1)} %bitcast_convert_fusion), channel_id=1, source_target_pairs={{0,1},{1,2},{2,3},{3,0},{4,5},{5,6},{6,7},{7,4},{8,9},{9,10},{10,1... | collective-permute-start | bytes 2764808 | tf_op jit(solution)/shard_map/ppermute | solution.py:28
  5.9 22.3 %collective-permute-start.9 = (bf16[720,640]{1,0:T(8,128)(2,1)S(1)}, bf16[720,640]{1,0:T(8,128)(2,1)S(1)}, u32[]{:S(2)}, u32[]{:S(2)}) collective-permute-start(bf16[720,640]{1,0:T(8,128)(2,1)S(1)} %bitcast_convert_fusion), channel_id=1, source_target_pairs={{0,3},{1,0},{2,1},{3,2},{4,7},{5,4},{6,5},{7,6},{8,11},{9,8},{10,9... | collective-permute-start | bytes 2764808 | tf_op jit(solution)/shard_map/ppermute | solution.py:28
  28.2 1.0 copy-start.6
  28.2 19.7 %copy-start.4 = (bf16[720,640]{1,0:T(8,128)(2,1)}, bf16[720,640]{1,0:T(8,128)(2,1)S(1)}, u32[]{:S(2)}) copy-start(bf16[720,640]{1,0:T(8,128)(2,1)S(1)} %collective-permute-done.9) | copy-start | bytes 2764804
  29.1 21.5 %collective-permute-start.11 = (bf16[720,640]{1,0:T(8,128)(2,1)}, bf16[720,640]{1,0:T(8,128)(2,1)S(1)}, u32[]{:S(2)}, u32[]{:S(2)}) collective-permute-start(bf16[720,640]{1,0:T(8,128)(2,1)} %get-tuple-element.165), channel_id=1, source_target_pairs={{0,4},{1,5},{2,6},{3,7},{4,0},{5,1},{6,2},{7,3},{8,12},{9,13},{10,... | collective-permute-start | bytes 2764808 | tf_op jit(solution)/shard_map/ppermute | solution.py:28
  29.6 22.4 %collective-permute-start.12 = (bf16[720,640]{1,0:T(8,128)(2,1)}, bf16[720,640]{1,0:T(8,128)(2,1)S(1)}, u32[]{:S(2)}, u32[]{:S(2)}) collective-permute-start(bf16[720,640]{1,0:T(8,128)(2,1)} %get-tuple-element.168), channel_id=1, source_target_pairs={{0,1},{1,2},{2,3},{3,0},{4,5},{5,6},{6,7},{7,4},{8,9},{9,10},{10,1... | collective-permute-start | bytes 2764808 | tf_op jit(solution)/shard_map/ppermute | solution.py:28
  29.9 24.1 %collective-permute-start.13 = (bf16[720,640]{1,0:T(8,128)(2,1)}, bf16[720,640]{1,0:T(8,128)(2,1)S(1)}, u32[]{:S(2)}, u32[]{:S(2)}) collective-permute-start(bf16[720,640]{1,0:T(8,128)(2,1)} %get-tuple-element.169), channel_id=1, source_target_pairs={{0,3},{1,0},{2,1},{3,2},{4,7},{5,4},{6,5},{7,6},{8,11},{9,8},{10,9... | collective-permute-start | bytes 2764808 | tf_op jit(solution)/shard_map/ppermute | solution.py:28
  33.6 39.9 %collective-permute-start.17 = (bf16[368,640]{1,0:T(8,128)(2,1)}, bf16[368,640]{1,0:T(8,128)(2,1)S(1)}, u32[]{:S(2)}, u32[]{:S(2)}) collective-permute-start(bf16[368,640]{1,0:T(8,128)(2,1)} %slice.19), channel_id=1, source_target_pairs={{0,3},{1,0},{2,1},{3,2},{4,7},{5,4},{6,5},{7,6},{8,11},{9,8},{10,9... | collective-permute-start | bytes 1413128 | tf_op jit(solution)/shard_map/ppermute | solution.py:28
  34.4 19.6 %copy-start.1 = (bf16[720,640]{1,0:T(8,128)(2,1)S(1)}, bf16[720,640]{1,0:T(8,128)(2,1)}, u32[]{:S(2)}) copy-start(bf16[720,640]{1,0:T(8,128)(2,1)} %get-tuple-element.170.g10) | copy-start | bytes 2764804
  54.0 1.2 copy-start.2
  55.2 5.5 %copy-start.17 = (bf16[720,640]{1,0:T(8,128)(2,1)S(1)}, bf16[720,640]{1,0:T(8,128)(2,1)}, u32[]{:S(2)}) copy-start(bf16[720,640]{1,0:T(8,128)(2,1)} %get-tuple-element.181) | copy-start | bytes 2764804
  55.2 5.6 %copy-start.16 = (bf16[720,640]{1,0:T(8,128)(2,1)S(1)}, bf16[720,640]{1,0:T(8,128)(2,1)}, u32[]{:S(2)}) copy-start(bf16[720,640]{1,0:T(8,128)(2,1)} %get-tuple-element.180) | copy-start | bytes 2764804
  55.8 20.0 %copy-start = (bf16[1536,640]{1,0:T(8,128)(2,1)S(1)}, bf16[1536,640]{1,0:T(8,128)(2,1)}, u32[]{:S(2)}) copy-start(bf16[1536,640]{1,0:T(8,128)(2,1)} %get-tuple-element.177.hidden) | copy-start | bytes 5898244
  55.8 23.9 %collective-permute-start.15 = (bf16[368,640]{1,0:T(8,128)(2,1)S(1)}, bf16[368,640]{1,0:T(8,128)(2,1)S(1)}, u32[]{:S(2)}, u32[]{:S(2)}) collective-permute-start(bf16[368,640]{1,0:T(8,128)(2,1)S(1)} %get-tuple-element.172), channel_id=1, source_target_pairs={{0,3},{1,0},{2,1},{3,2},{4,7},{5,4},{6,5},{7,6},{8,11},{9,8},{10,9... | collective-permute-start | bytes 1413128 | tf_op jit(solution)/shard_map/ppermute | solution.py:28
  60.6 12.9 %collective-permute-start.16 = (bf16[352,640]{1,0:T(8,128)(2,1)S(1)}, bf16[352,640]{1,0:T(8,128)(2,1)S(1)}, u32[]{:S(2)}, u32[]{:S(2)}) collective-permute-start(bf16[352,640]{1,0:T(8,128)(2,1)S(1)} %slice.18), channel_id=1, source_target_pairs={{0,1},{1,2},{2,3},{3,0},{4,5},{5,6},{6,7},{7,4},{8,9},{9,10},{10,1... | collective-permute-start | bytes 1351688 | tf_op jit(solution)/shard_map/ppermute | solution.py:28
  60.6 19.1 %collective-permute-start.14 = (bf16[352,640]{1,0:T(8,128)(2,1)S(1)}, bf16[352,640]{1,0:T(8,128)(2,1)S(1)}, u32[]{:S(2)}, u32[]{:S(2)}) collective-permute-start(bf16[352,640]{1,0:T(8,128)(2,1)S(1)} %get-tuple-element.171), channel_id=1, source_target_pairs={{0,1},{1,2},{2,3},{3,0},{4,5},{5,6},{6,7},{7,4},{8,9},{9,10},{10,1... | collective-permute-start | bytes 1351688 | tf_op jit(solution)/shard_map/ppermute | solution.py:28
  74.3 34.8 %collective-permute-start.21 = (bf16[720,640]{1,0:T(8,128)(2,1)S(1)}, bf16[720,640]{1,0:T(8,128)(2,1)}, u32[]{:S(2)}, u32[]{:S(2)}) collective-permute-start(bf16[720,640]{1,0:T(8,128)(2,1)S(1)} %get-tuple-element.191), channel_id=1, source_target_pairs={{0,4},{1,5},{2,6},{3,7},{4,0},{5,1},{6,2},{7,3},{8,12},{9,13},{10,... | collective-permute-start | bytes 2764808 | tf_op jit(solution)/shard_map/ppermute | solution.py:28
  80.9 31.4 %collective-permute-start.23 = (bf16[720,640]{1,0:T(8,128)(2,1)}, bf16[720,640]{1,0:T(8,128)(2,1)}, u32[]{:S(2)}, u32[]{:S(2)}) collective-permute-start(bf16[720,640]{1,0:T(8,128)(2,1)} %pad_maximum_fusion.1), channel_id=1, source_target_pairs={{0,3},{1,0},{2,1},{3,2},{4,7},{5,4},{6,5},{7,6},{8,11},{9,8},{10,9... | collective-permute-start | bytes 2764808 | tf_op jit(solution)/shard_map/ppermute | solution.py:28
  81.0 6.2 %copy-start.5 = (bf16[720,640]{1,0:T(8,128)(2,1)S(1)}, bf16[720,640]{1,0:T(8,128)(2,1)}, u32[]{:S(2)}) copy-start(bf16[720,640]{1,0:T(8,128)(2,1)} %copy-done.4) | copy-start | bytes 2764804
  82.1 30.2 %collective-permute-start.22 = (bf16[720,640]{1,0:T(8,128)(2,1)}, bf16[720,640]{1,0:T(8,128)(2,1)}, u32[]{:S(2)}, u32[]{:S(2)}) collective-permute-start(bf16[720,640]{1,0:T(8,128)(2,1)} %pad_maximum_fusion), channel_id=1, source_target_pairs={{0,1},{1,2},{2,3},{3,0},{4,5},{5,6},{6,7},{7,4},{8,9},{9,10},{10,1... | collective-permute-start | bytes 2764808 | tf_op jit(solution)/shard_map/ppermute | solution.py:28
  86.8 47.6 %collective-permute-start.20 = (bf16[720,640]{1,0:T(8,128)(2,1)}, bf16[720,640]{1,0:T(8,128)(2,1)}, u32[]{:S(2)}, u32[]{:S(2)}) collective-permute-start(bf16[720,640]{1,0:T(8,128)(2,1)} %pad_maximum_fusion.2), channel_id=1, source_target_pairs={{0,4},{1,5},{2,6},{3,7},{4,0},{5,1},{6,2},{7,3},{8,12},{9,13},{10,... | collective-permute-start | bytes 2764808 | tf_op jit(solution)/shard_map/ppermute | solution.py:28
  87.2 5.7 %copy-start.9 = (bf16[720,640]{1,0:T(8,128)(2,1)S(1)}, bf16[720,640]{1,0:T(8,128)(2,1)}, u32[]{:S(2)}) copy-start(bf16[720,640]{1,0:T(8,128)(2,1)} %get-tuple-element.97.refs_3_) | copy-start | bytes 2764804 | tf_op jit(solution)/shard_map/cond
  87.2 5.7 %copy-start.14 = (bf16[352,640]{1,0:T(8,128)(2,1)S(1)}, bf16[352,640]{1,0:T(8,128)(2,1)}, u32[]{:S(2)}) copy-start(bf16[352,640]{1,0:T(8,128)(2,1)} %get-tuple-element.99.refs_5_) | copy-start | bytes 1351684 | tf_op jit(solution)/shard_map/cond
  88.6 20.3 %collective-permute-start.2 = (bf16[720,640]{1,0:T(8,128)(2,1)S(1)}, bf16[720,640]{1,0:T(8,128)(2,1)}, u32[]{:S(2)}, u32[]{:S(2)}) collective-permute-start(bf16[720,640]{1,0:T(8,128)(2,1)S(1)} %broadcast_select_fusion.2), channel_id=1, source_target_pairs={{0,100},{1,101},{2,102},{3,103},{4,96},{5,97},{6,98},{7,99},{8,108... | collective-permute-start | bytes 2764808 | tf_op jit(solution)/shard_map/cond/branch_2_fun/ppermute | solution.py:43
  109.0 25.4 %collective-permute-start.18 = (bf16[720,640]{1,0:T(8,128)(2,1)}, bf16[720,640]{1,0:T(8,128)(2,1)S(1)}, u32[]{:S(2)}, u32[]{:S(2)}) collective-permute-start(bf16[720,640]{1,0:T(8,128)(2,1)} %collective-permute-done.10), channel_id=1, source_target_pairs={{0,1},{1,2},{2,3},{3,0},{4,5},{5,6},{6,7},{7,4},{8,9},{9,10},{10,1... | collective-permute-start | bytes 2764808 | tf_op jit(solution)/shard_map/ppermute | solution.py:28
  109.1 25.3 %collective-permute-start.19 = (bf16[720,640]{1,0:T(8,128)(2,1)}, bf16[720,640]{1,0:T(8,128)(2,1)}, u32[]{:S(2)}, u32[]{:S(2)}) collective-permute-start(bf16[720,640]{1,0:T(8,128)(2,1)} %collective-permute-done.10), channel_id=1, source_target_pairs={{0,3},{1,0},{2,1},{3,2},{4,7},{5,4},{6,5},{7,6},{8,11},{9,8},{10,9... | collective-permute-start | bytes 2764808 | tf_op jit(solution)/shard_map/ppermute | solution.py:28
  112.3 3.3 %copy-start.3 = (f32[1,720,640]{2,1,0:T(8,128)S(1)}, f32[1,720,640]{2,1,0:T(8,128)}, u32[]{:S(2)}) copy-start(f32[1,720,640]{2,1,0:T(8,128)} %param.19) | copy-start | bytes 5529604
  115.7 15.0 %collective-permute-start.6 = (bf16[720,640]{1,0:T(8,128)(2,1)S(1)}, bf16[720,640]{1,0:T(8,128)(2,1)S(1)}, u32[]{:S(2)}, u32[]{:S(2)}) collective-permute-start(bf16[720,640]{1,0:T(8,128)(2,1)S(1)} %convert_element_type.53), channel_id=1, source_target_pairs={{0,96},{8,104},{16,112},{24,120},{32,0},{40,8},{48,16},{56,24},{64... | collective-permute-start | bytes 2764808 | tf_op jit(solution)/shard_map/cond/branch_2_fun/ppermute | solution.py:32
  134.4 0.9 copy-start.18
  (1 other events, 0.8 us)

commit v2 on v1

--- a/solution.py
+++ b/solution.py
@@ -32,9 +32,13 @@
     return lax.ppermute(value, "group", [(i, (i - by) % 16) for i in range(16)])
 
 
-def weight_from_partner(own, other, by):
+def to_send(own, other, step):
     group = lax.axis_index("group")
-    value = jnp.where(group // 8 != ((group - by) % 16) // 8, other, own)
+    by = jnp.left_shift(jnp.int32(1), step[0] % 4)
+    return jnp.where(group // 8 != ((group - by) % 16) // 8, other, own)
+
+
+def weight_from_partner(value, by):
     pairs = []
     for i in range(16):
         to = (i - by) % 16
@@ -189,8 +193,6 @@
 ]
 TILE = 6
 WINDOW = 7 * 128
-TALL = 512
-STEPS = PIXELS // TALL
 CHUNK = 128
 SHORT = pl.CostEstimate(flops=10**6, bytes_accessed=10**5, transcendentals=0)
 IN_VMEM = pl.BlockSpec(memory_space=pltpu.VMEM)
@@ -241,23 +243,28 @@
     )(hidden)
 
 
-def conv_kernel(places, last, *refs):
+def conv_kernel(places, added, tall, *refs):
+    steps = PIXELS // tall
     count = len(places)
     taps_hbm, pieces, refs = refs[0], refs[1 : 1 + count], refs[1 + count :]
     before_hbm = lat_hbm = None
+    last = added == 2
+    if added:
+        before_hbm, refs = refs[0], refs[1:]
     if last:
-        before_hbm, lat_hbm, refs = refs[0], refs[1], refs[2:]
+        lat_hbm, refs = refs[0], refs[1:]
     out_hbm, taps, weights, before, lat, out, sem_w, sem_in, sem_out = refs
 
     def rows_of(m):
-        return pl.ds(pl.multiple_of(m * TALL, TALL), TALL)
+        return pl.ds(pl.multiple_of(m * tall, tall), tall)
 
     def inputs(m):
-        rows = pl.ds(pl.multiple_of(m * TALL + 2 * WIDTH, 2 * WIDTH), TALL)
+        rows = pl.ds(pl.multiple_of(m * tall + 2 * WIDTH, 2 * WIDTH), tall)
         found = [pltpu.make_async_copy(taps_hbm.at[rows], taps.at[rows], sem_in.at[3 * m])]
+        rows = rows_of(m)
+        if added:
+            found.append(pltpu.make_async_copy(before_hbm.at[rows], before.at[rows], sem_in.at[3 * m + 1]))
         if last:
-            rows = rows_of(m)
-            found.append(pltpu.make_async_copy(before_hbm.at[rows], before.at[rows], sem_in.at[3 * m + 1]))
             found.append(pltpu.make_async_copy(lat_hbm.at[rows], lat.at[rows], sem_in.at[3 * m + 2]))
         return found
 
@@ -266,7 +273,7 @@
 
     weights[...] = jnp.zeros_like(weights)
     head = pl.ds(0, 2 * WIDTH)
-    copies = [pltpu.make_async_copy(taps_hbm.at[head], taps.at[head], sem_in.at[3 * STEPS])]
+    copies = [pltpu.make_async_copy(taps_hbm.at[head], taps.at[head], sem_in.at[3 * steps])]
     copies[0].start()
     tiles = []
     blocks = list(dict.fromkeys(place[:2] for place in places))
@@ -286,11 +293,11 @@
         copy.start()
     for copy in copies + inputs(0):
         copy.wait()
-    for m in range(1, STEPS):
+    for m in range(1, steps):
         for copy in inputs(m):
             copy.start()
 
-    @pl.loop(0, STEPS)
+    @pl.loop(0, steps)
     def _(m):
         @pl.when(m > 0)
         def _():
@@ -298,24 +305,26 @@
                 copy.wait()
 
         left = jnp.concatenate([
-            taps[pl.ds(pl.multiple_of(m * TALL + down, WIDTH), TALL), pl.ds(lane, 128)]
+            taps[pl.ds(pl.multiple_of(m * tall + down, WIDTH), tall), pl.ds(lane, 128)]
             for down, lane in tiles
         ], axis=1)
         total = jnp.dot(left, weights[...], preferred_element_type=jnp.float32)
+        if added:
+            total += before[rows_of(m), :].astype(jnp.float32)
         if last:
-            total += before[rows_of(m), :].astype(jnp.float32)
             total = lat[rows_of(m), :].astype(jnp.float32) + SCALE * total
         out[rows_of(m), :] = total.astype(jnp.bfloat16)
         result(m).start()
 
-    for m in range(STEPS):
+    for m in range(steps):
         result(m).wait()
 
 
 def conv(taps, places, pieces, others=()):
     blocks = len(set(place[:2] for place in places))
-    return pl.pallas_call(
-        partial(conv_kernel, places, len(others) > 0),
+    tall = 256 if blocks > 2 else 512
+    return pl.pallas_call(
+        partial(conv_kernel, places, len(others), tall),
         out_shape=jax.ShapeDtypeStruct((PIXELS, CHANS), jnp.bfloat16),
         in_specs=[IN_ANY] * (1 + len(pieces) + len(others)),
         out_specs=IN_ANY,
@@ -326,8 +335,8 @@
             pltpu.VMEM((PIXELS, CHANS), jnp.bfloat16),
             pltpu.VMEM((PIXELS, CHANS), jnp.bfloat16),
             pltpu.SemaphoreType.DMA((len(pieces),)),
-            pltpu.SemaphoreType.DMA((3 * STEPS + 1,)),
-            pltpu.SemaphoreType.DMA((STEPS,)),
+            pltpu.SemaphoreType.DMA((3 * (PIXELS // tall) + 1,)),
+            pltpu.SemaphoreType.DMA((PIXELS // tall,)),
         ],
         compiler_params=pltpu.CompilerParams(vmem_limit_bytes=58 * MIB),
         cost_estimate=SHORT,
@@ -339,16 +348,12 @@
     return lax.optimization_barrier(tuple(values) + others)[: len(values)]
 
 
-def add(*values):
-    return sum(v.astype(jnp.float32) for v in values).astype(jnp.bfloat16)
-
-
 def from_switch(step, branch, *state):
     return lax.switch(step[0] % 4, [partial(branch, 1 << level) for level in range(4)], *state)
 
 
-def partner_and_conv(by, own, other, taps, w_m, w_p, top, bottom):
-    w_partner = weight_from_partner(own, other, by)
+def partner_and_conv(by, chosen, own, other, taps, w_m, w_p, top, bottom):
+    w_partner = weight_from_partner(chosen, by)
     places = [
         (0, 0, 0, ROWS), (1, 0, 0, ROWS), (0, 3, 0, ROWS), (0, 1, 0, ROWS),
         (0, 2, 0, HALF), (0, 2, HALF, ROWS - HALF),
@@ -356,33 +361,65 @@
     return w_partner, conv(taps, places, (own, other, w_m, w_p, top, bottom))
 
 
-def sums_kernel(a_y, g02, a_p, a_m, g10, far_top, far_bottom, near):
-    def add(rows, *refs):
-        return sum(ref[rows, :].astype(jnp.float32) for ref in refs).astype(jnp.bfloat16)
-
-    far_top[...] = add(slice(0, HALF), a_y, g02)
-    far_bottom[...] = add(slice(HALF, ROWS), a_y, g02)
-    near[...] = add(slice(0, ROWS), a_p, a_m, g10)
-
-
-def sums(*values):
-    return pl.pallas_call(
-        sums_kernel,
-        out_shape=[jax.ShapeDtypeStruct((rows, CHANS), jnp.bfloat16) for rows in (HALF, ROWS - HALF, ROWS)],
-        in_specs=[IN_VMEM] * 5,
-        out_specs=[IN_VMEM] * 3,
+def added(rows, *refs):
+    return sum(ref[rows, :].astype(jnp.float32) for ref in refs).astype(jnp.bfloat16)
+
+
+def sums_kernel(a_y, g02, a_p, a_m, g10, w_m, w_p, far_top, far_bottom, near, w_top, w_bottom):
+    far_top[...] = added(slice(0, HALF), a_y, g02)
+    far_bottom[...] = added(slice(HALF, ROWS), a_y, g02)
+    near[...] = added(slice(0, ROWS), a_p, a_m, g10)
+    w_top[...] = w_m[0:HALF, :]
+    w_bottom[...] = w_p[HALF:ROWS, :]
+
+
+def ends_kernel(b_up, g0p, b_dn, g0m, to_up, to_dn):
+    to_up[0:HALF, :] = added(slice(0, HALF), b_up, g0p)
+    to_up[HALF:ROWS, :] = g0p[HALF:ROWS, :]
+    to_dn[0:HALF, :] = g0m[0:HALF, :]
+    lower = b_dn[...].astype(jnp.float32) + g0m[HALF:ROWS, :].astype(jnp.float32)
+    to_dn[HALF:ROWS, :] = lower.astype(jnp.bfloat16)
+
+
+def small(kernel, name, rows, *values):
+    return pl.pallas_call(
+        kernel,
+        out_shape=[jax.ShapeDtypeStruct((count, CHANS), jnp.bfloat16) for count in rows],
+        in_specs=[IN_VMEM] * len(values),
+        out_specs=[IN_VMEM] * len(rows),
         compiler_params=pltpu.CompilerParams(vmem_limit_bytes=20 * MIB),
         cost_estimate=SHORT,
-        name="sums",
+        name=name,
     )(*values)
 
 
-def finish(by, moved, own_weight, w_partner):
-    partner = from_partner(moved.astype(jnp.bfloat16), by).astype(jnp.float32)
+def moved_kernel(moment, g00, b_y, c_up, c_dn, moved, rounded):
+    grad = sum(ref[...].astype(jnp.float32) for ref in (g00, b_y, c_up, c_dn))
+    value = 0.9 * moment[...] + grad
+    moved[...] = value
+    rounded[...] = value.astype(jnp.bfloat16)
+
+
+def moved_rows(*values):
+    rows = pl.BlockSpec((ROWS // 3, CHANS), lambda i: (i, 0))
+    return pl.pallas_call(
+        moved_kernel,
+        out_shape=[jax.ShapeDtypeStruct((ROWS, CHANS), kind) for kind in (jnp.float32, jnp.bfloat16)],
+        grid=(3,),
+        in_specs=[rows] * 5,
+        out_specs=[rows] * 2,
+        compiler_params=pltpu.CompilerParams(vmem_limit_bytes=20 * MIB),
+        cost_estimate=SHORT,
+        name="moved",
+    )(*values)
+
+
+def finish(by, rounded, moved, own_weight, w_partner, taps, corner, acc):
+    partner = from_partner(rounded, by).astype(jnp.float32)
     both = moved + partner
     new_moment = 0.5 * both
     new_weight = 0.5 * (own_weight + w_partner.astype(jnp.float32)) - 0.025 * both
-    return new_weight, new_moment
+    return new_weight, new_moment, conv(taps, [(1, 2, 0, ROWS)], (corner,), (acc,))
 
 
 def on_device(latents, cotangent, gain, bias, weight, momentum, step):
@@ -397,35 +434,39 @@
     a_y = send_inner(g12, 1, 0)
     a_p = send_inner(g1p, 0, 1)
     a_m = send_inner(g1m, 0, -1)
-    top = send_inner(w_m[:HALF], 0, 1)
-    bottom = send_inner(w_p[HALF:], 0, -1)
     g00, g0p, g0m, g02 = rest_grad(turned, cotangent)
-    far_top, far_bottom, near = sums(a_y, g02, a_p, a_m, g10)
+    hidden = together((hidden,), g02)[0]
+    taps = spread(hidden)
+    a_y, a_p, a_m, taps = together((a_y, a_p, a_m, taps))
+    far_top, far_bottom, near, w_top, w_bottom = small(
+        sums_kernel, "sums", (HALF, ROWS - HALF, ROWS, HALF, ROWS - HALF),
+        a_y, g02, a_p, a_m, g10, w_m, w_p,
+    )
     b_up = send_inner(far_top, 0, 1)
     b_dn = send_inner(far_bottom, 0, -1)
-    near, top, bottom, hidden = together((near, top, bottom, hidden))
     b_y = send_inner(near, 1, 0)
-    corner = send_inner(jnp.concatenate([top, bottom]), 1, 0)
-    taps = spread(hidden)
-    b_up, b_dn, taps = together((b_up, b_dn, taps))
-    to_up = jnp.concatenate([add(b_up, g0p[:HALF]), g0p[HALF:]])
-    to_dn = jnp.concatenate([g0m[:HALF], add(b_dn, g0m[HALF:])])
+    top = send_inner(w_top, 0, 1)
+    bottom = send_inner(w_bottom, 0, -1)
+    own_late, w_y_late = together((own, w_y), far_top)
+    chosen = to_send(own_late, w_y_late, step)
+    b_up, b_dn, chosen = together((b_up, b_dn, chosen))
+    to_up, to_dn = small(ends_kernel, "ends", (ROWS, ROWS), b_up, g0p, b_dn, g0m)
     c_up = send_inner(to_up, 0, 1)
     c_dn = send_inner(to_dn, 0, -1)
-    taps = together((taps,), to_up, to_dn)[0]
-    w_partner, acc = from_switch(step, partner_and_conv, own, w_y, taps, w_m, w_p, top, bottom)
+    taps, top, bottom, b_y = together((taps, top, bottom, b_y), to_up, to_dn)
+    corner = send_inner(jnp.concatenate([top, bottom]), 1, 0)
+    w_partner, acc = from_switch(
+        step, partner_and_conv, chosen, own, w_y, taps, w_m, w_p, top, bottom
+    )
     w_y = together((w_y,), acc)[0]
     y_m = send_inner(w_y, 0, 1)
     y_p = send_inner(w_y, 0, -1)
-    grad = (
-        g00.astype(jnp.float32) + b_y.astype(jnp.float32)
-        + c_up.astype(jnp.float32) + c_dn.astype(jnp.float32)
+    moved, rounded = moved_rows(own_moment, g00, b_y, c_up, c_dn)
+    new_weight, new_moment, acc = from_switch(
+        step, finish, rounded, moved, own_weight, w_partner, taps, corner, acc
     )
-    moved = 0.9 * own_moment + grad
-    new_weight, new_moment = from_switch(step, finish, moved, own_weight, w_partner)
-    y_m, y_p, corner = together((y_m, y_p, corner), new_weight, new_moment)
-    places = [(1, 2, 0, ROWS), (1, 3, 0, ROWS), (1, 1, 0, ROWS)]
-    block_out = conv(taps, places, (corner, y_m, y_p), (acc, latents))
+    y_m, y_p = together((y_m, y_p), new_weight, new_moment)
+    block_out = conv(taps, [(1, 3, 0, ROWS), (1, 1, 0, ROWS)], (y_m, y_p), (acc, latents))
     return (block_out[None], new_weight[None], new_moment[None])
 
 

time: 147 us -> 144 us (0.980)
  Pallas kernels: 63.4 us -> 75.2 us
  waiting for transfers between devices: 32.6 us -> 26.5 us
  other arithmetic: 14.3 us -> 10.4 us
  local copies, waits for them, and re-layouts: 6.96 us -> 3.37 us
  starting transfers between devices: 27.7 us -> 25.6 us
    pallas_call x3 -> x6, Pallas kernels: 27.9 us -> 39.6 us  [the longest x3 31.5 us: conv(): pl.pallas_call(partial(conv_kernel, places, len(others), tall), out_shape...]
    ppermute x1, waiting for transfers between devices: 13 us -> 8.01 us  [from_partner(): return lax.ppermute(value, 'group', [(i, (i - by) % 16) for i in range(16)])]
    add x1 -> x0, other arithmetic: 3.29 us -> none  [on_device(): moved = 0.9 * own_moment + grad]
    concatenate x2 -> x0, other arithmetic: 2.01 us -> none  [the longest x1 1.01 us: on_device(): to_dn = jnp.concatenate([g0m[:HALF], add(b_dn, g0m[HALF:])])]
    slice x4 -> x0, local copies, waits for them, and re-layouts: 1.94 us -> none  [the longest x1 1.05 us: on_device(): top = send_inner(w_m[:HALF], 0, 1)]
    unnamed x26 -> x32, local copies, waits for them, and re-layouts: 3.88 us -> 2.18 us
  transfers between devices with their start and end apart: 18 -> 18, of which waited for: 6 -> 6; matrix products, arithmetic and copies ran while one was open for 11% -> 7% of each run, Pallas kernels for 36% -> 45%
where the time goes in v2:
time: 144 us; the launch traced here: 143 us
  Pallas kernels  75.2 us (52%)
  waiting for transfers between devices  26.5 us (18%)
  starting transfers between devices  25.6 us (18%)
  other arithmetic  10.4 us (7%)
  local copies, waits for them, and re-layouts  3.37 us (2%)
  between operations  1.7 us (1%)
    pallas_call x3, Pallas kernels, conv(): pl.pallas_call(partial(conv_kernel, places, len(others), tall), out_shape...  31.5 us
    ppermute x16, starting transfers between devices, send_inner(): return lax.ppermute(value, 'inner', [(i, place(i)) for i in range(8)])  21.8 us
    ppermute x16, waiting for transfers between devices, send_inner(): return lax.ppermute(value, 'inner', [(i, place(i)) for i in range(8)])  18.4 us
    pallas_call x1, Pallas kernels, norm_grad(): pl.pallas_call(norm_grad_kernel, out_shape=[jax.ShapeDtypeStruct((PIXELS,...  18.1 us
    pallas_call x1, Pallas kernels, rest_grad(): pl.pallas_call(rest_grad_kernel, out_shape=[jax.ShapeDtypeStruct((ROWS, C...  13.6 us
    ppermute x1, waiting for transfers between devices, from_partner(): return lax.ppermute(value, 'group', [(i, (i - by) % 16) for i in range(16)])  8.01 us
    pallas_call x2, Pallas kernels, small(): pl.pallas_call(kernel, out_shape=[jax.ShapeDtypeStruct((count, CHANS), jn...  4.13 us
    mul x1, other arithmetic, finish(): new_moment = 0.5 * both  4.09 us
  transfers between devices with their start and end apart: 18, of which 6 were waited for; matrix products, arithmetic and copies ran while one was open for 7% of the time, Pallas kernels for 45%

profile of v2, /device:TPU:0, one launch (start us, length us, event | category | flops | bytes accessed | tf_op | source)
XLA Modules:
  0.0 142.7 jit_solution(14602895371813788741)
XLA Ops:
  0.7 1.6 %bitcast_convert_fusion = bf16[720,640]{1,0:T(8,128)(2,1)S(1)} fusion(f32[1,720,640]{2,1,0:T(8,128)} %param.19), kind=kLoop, calls=%fused_computation.14 | loop fusion | flops 460800 | bytes 2764800 | tf_op jit(solution)/shard_map/convert_element_type | solution.py:427
  2.3 1.7 %collective-permute-start.10 = (bf16[720,640]{1,0:T(8,128)(2,1)S(1)}, bf16[720,640]{1,0:T(8,128)(2,1)S(1)}, u32[]{:S(2)}, u32[]{:S(2)}) collective-permute-start(bf16[720,640]{1,0:T(8,128)(2,1)S(1)} %bitcast_convert_fusion), channel_id=1, source_target_pairs={{0,4},{1,5},{2,6},{3,7},{4,0},{5,1},{6,2},{7,3},{8,12},{9,13},{10,... | collective-permute-start | bytes 2764808 | tf_op jit(solution)/shard_map/ppermute | solution.py:28
  4.0 4.0 %collective-permute-start.9 = (bf16[720,640]{1,0:T(8,128)(2,1)S(1)}, bf16[720,640]{1,0:T(8,128)(2,1)S(1)}, u32[]{:S(2)}, u32[]{:S(2)}) collective-permute-start(bf16[720,640]{1,0:T(8,128)(2,1)S(1)} %bitcast_convert_fusion), channel_id=1, source_target_pairs={{0,3},{1,0},{2,1},{3,2},{4,7},{5,4},{6,5},{7,6},{8,11},{9,8},{10,9... | collective-permute-start | bytes 2764808 | tf_op jit(solution)/shard_map/ppermute | solution.py:28
  9.2 18.1 %norm_grad.1 = (bf16[1536,640]{1,0:T(8,128)(2,1)}, bf16[640,1536]{1,0:T(8,128)(2,1)}, bf16[720,640]{1,0:T(8,128)(2,1)}, bf16[720,640]{1,0:T(8,128)(2,1)}, bf16[7...) custom-call(bf16[1536,640]{1,0:T(8,128)(2,1)} %bitcast.19, bf16[1536,640]{1,0:T(8,128)(2,1)} %bitcast.17, ...), custom_call_target="tpu_custom_call" | custom-call | flops 1000000 | bytes 100000 | tf_op jit(solution)/shard_map/norm_grad/pallas_call | solution.py:203
  27.5 3.4 %collective-permute-done.8.w_m = bf16[720,640]{1,0:T(8,128)(2,1)S(1)} collective-permute-done((bf16[720,640]{1,0:T(8,128)(2,1)S(1)}, bf16[720,640]{1,0:T(8,128)(2,1)S(1)}, u32[]{:S(2)}, u32[]{:S(2)}) %collective-permute-start.8) | collective-permute-done | bytes 921632 | tf_op jit(solution)/shard_map/ppermute | solution.py:28
  30.9 0.9 copy-done.15
  32.3 3.2 %collective-permute-start.13 = (bf16[720,640]{1,0:T(8,128)(2,1)}, bf16[720,640]{1,0:T(8,128)(2,1)S(1)}, u32[]{:S(2)}, u32[]{:S(2)}) collective-permute-start(bf16[720,640]{1,0:T(8,128)(2,1)} %get-tuple-element.239), channel_id=1, source_target_pairs={{0,3},{1,0},{2,1},{3,2},{4,7},{5,4},{6,5},{7,6},{8,11},{9,8},{10,9... | collective-permute-start | bytes 2764808 | tf_op jit(solution)/shard_map/ppermute | solution.py:28
  35.5 13.6 %rest_grad.1 = (bf16[720,640]{1,0:T(8,128)(2,1)}, bf16[720,640]{1,0:T(8,128)(2,1)}, bf16[720,640]{1,0:T(8,128)(2,1)}, bf16[720,640]{1,0:T(8,128)(2,1)}) custom-call(bf16[640,1536]{1,0:T(8,128)(2,1)} %get-tuple-element.241.turned, bf16[1536,640]{1,0:T(8,128)(2,1)} %bitcast.18), custom_call_target="tpu_custom_call" | custom-call | flops 1000000 | bytes 100000 | tf_op jit(solution)/shard_map/rest_grad/pallas_call | solution.py:222
  49.1 3.8 %spread.1.refs_0_ = bf16[1600,1920]{1,0:T(8,128)(2,1)} custom-call(bf16[1536,640]{1,0:T(8,128)(2,1)S(1)} %copy-done), custom_call_target="tpu_custom_call" | custom-call | flops 1000000 | bytes 100000 | tf_op jit(solution)/shard_map/spread/pallas_call | solution.py:235
  53.0 1.1 collective-permute-done.12.a_p
  54.2 1.7 %sums.1 = (bf16[352,640]{1,0:T(8,128)(2,1)}, bf16[368,640]{1,0:T(8,128)(2,1)}, bf16[720,640]{1,0:T(8,128)(2,1)}, bf16[352,640]{1,0:T(8,128)(2,1)}, bf16[368,640]{1,0:T(8,128)(2,1)}) custom-call(bf16[720,640]{1,0:T(8,128)(2,1)S(1)} %collective-permute-done.11.a_y, bf16[720,640]{1,0:T(8,128)(2,1)S(1)} %copy-done.6, ...), custom_call_target="tpu_custom_call" | custom-call | flops 1000000 | bytes 100000 | tf_op jit(solution)/shard_map/sums/pallas_call | solution.py:385
  55.8 1.6 %collective-permute-start.16 = (bf16[720,640]{1,0:T(8,128)(2,1)}, bf16[720,640]{1,0:T(8,128)(2,1)S(1)}, u32[]{:S(2)}, u32[]{:S(2)}) collective-permute-start(bf16[720,640]{1,0:T(8,128)(2,1)} %get-tuple-element.253), channel_id=1, source_target_pairs={{0,4},{1,5},{2,6},{3,7},{4,0},{5,1},{6,2},{7,3},{8,12},{9,13},{10,... | collective-permute-start | bytes 2764808 | tf_op jit(solution)/shard_map/ppermute | solution.py:28
  57.4 2.9 %collective-permute-start.18 = (bf16[368,640]{1,0:T(8,128)(2,1)}, bf16[368,640]{1,0:T(8,128)(2,1)S(1)}, u32[]{:S(2)}, u32[]{:S(2)}) collective-permute-start(bf16[368,640]{1,0:T(8,128)(2,1)} %get-tuple-element.255), channel_id=1, source_target_pairs={{0,3},{1,0},{2,1},{3,2},{4,7},{5,4},{6,5},{7,6},{8,11},{9,8},{10,9... | collective-permute-start | bytes 1413128 | tf_op jit(solution)/shard_map/ppermute | solution.py:28
  60.4 2.0 %collective-permute-start.17 = (bf16[352,640]{1,0:T(8,128)(2,1)}, bf16[352,640]{1,0:T(8,128)(2,1)}, u32[]{:S(2)}, u32[]{:S(2)}) collective-permute-start(bf16[352,640]{1,0:T(8,128)(2,1)} %get-tuple-element.254), channel_id=1, source_target_pairs={{0,1},{1,2},{2,3},{3,0},{4,5},{5,6},{6,7},{7,4},{8,9},{9,10},{10,1... | collective-permute-start | bytes 1351688 | tf_op jit(solution)/shard_map/ppermute | solution.py:28
  63.1 2.2 %broadcast_select_fusion = bf16[720,640]{1,0:T(8,128)(2,1)} fusion(bf16[720,640]{1,0:T(8,128)(2,1)} %copy-done.17, bf16[720,640]{1,0:T(8,128)(2,1)} %copy-done.13, pred[]{:T(512)S(6)} %ne.37), kind=kLoop, calls=%fused_computation.13 | loop fusion | flops 460800 | bytes 2764801 | tf_op jit(solution)/shard_map/jit(_where)/select_n | solution.py:38
  65.4 9.9 %collective-permute-done.17.b_up = bf16[352,640]{1,0:T(8,128)(2,1)} collective-permute-done((bf16[352,640]{1,0:T(8,128)(2,1)}, bf16[352,640]{1,0:T(8,128)(2,1)}, u32[]{:S(2)}, u32[]{:S(2)}) %collective-permute-start.17) | collective-permute-done | bytes 450592 | tf_op jit(solution)/shard_map/ppermute | solution.py:28
  75.2 2.4 %ends.1 = (bf16[720,640]{1,0:T(8,128)(2,1)}, bf16[720,640]{1,0:T(8,128)(2,1)}) custom-call(bf16[352,640]{1,0:T(8,128)(2,1)} %collective-permute-done.17.b_up, bf16[720,640]{1,0:T(8,128)(2,1)S(1)} %copy-done.7, bf16[368,640]{1,0:T(8,128)(2,1)S(1)} %collective-permute-done.18.b_dn, bf16[720,640]{1,0:T(8,128)(2,1)S(1)} %copy-done.8), custom_call_target="tpu_custom_call" | custom-call | flops 1000000 | bytes 100000 | tf_op jit(solution)/shard_map/ends/pallas_call | solution.py:385
  78.4 2.5 %collective-permute-start.22 = (bf16[720,640]{1,0:T(8,128)(2,1)}, bf16[720,640]{1,0:T(8,128)(2,1)}, u32[]{:S(2)}, u32[]{:S(2)}) collective-permute-start(bf16[720,640]{1,0:T(8,128)(2,1)} %get-tuple-element.264), channel_id=1, source_target_pairs={{0,3},{1,0},{2,1},{3,2},{4,7},{5,4},{6,5},{7,6},{8,11},{9,8},{10,9... | collective-permute-start | bytes 2764808 | tf_op jit(solution)/shard_map/ppermute | solution.py:28
  80.9 4.0 %collective-permute-done.14 = bf16[352,640]{1,0:T(8,128)(2,1)} collective-permute-done((bf16[352,640]{1,0:T(8,128)(2,1)}, bf16[352,640]{1,0:T(8,128)(2,1)}, u32[]{:S(2)}, u32[]{:S(2)}) %collective-permute-start.14) | collective-permute-done | bytes 450592 | tf_op jit(solution)/shard_map/ppermute | solution.py:28
  84.9 2.5 %pad_maximum_fusion = bf16[720,640]{1,0:T(8,128)(2,1)} fusion(bf16[368,640]{1,0:T(8,128)(2,1)} %collective-permute-done.15, bf16[352,640]{1,0:T(8,128)(2,1)} %collective-permute-done.14), kind=kLoop, calls=%fused_computation.12 | loop fusion | flops 1843200 | bytes 1843200 | tf_op jit(solution)/shard_map/concatenate | solution.py:457
  87.8 19.4 %conditional.2 = (bf16[720,640]{1,0:T(8,128)(2,1)}, bf16[1536,640]{1,0:T(8,128)(2,1)S(1)}) conditional(s32[]{:T(128)} %clamp.4, (bf16[720,640]{1,0:T(8,128)(2,1)}, bf16[1600,1920]{1,0:T(8,128)(2,1)}, bf16[720,640]{1,0:T(8,128)(2,1)}, bf16[720,640]{1,0:T(8,128)(2,1)}, bf16[720,640]{1,0:T(8,128)(2,1)}, ...), branch_computations={%region_0.1_spmd, %region_1.2_spmd, %region_2.3_spmd, %region_3.4_... | conditional | flops 1000000 | bytes 3786456 | solution.py:352
  87.8 3.1 %collective-permute-start.3 = (bf16[720,640]{1,0:T(8,128)(2,1)}, bf16[720,640]{1,0:T(8,128)(2,1)}, u32[]{:S(2)}, u32[]{:S(2)}) collective-permute-start(bf16[720,640]{1,0:T(8,128)(2,1)} %get-tuple-element.144), channel_id=1, source_target_pairs={{0,68},{1,69},{2,70},{3,71},{4,64},{5,65},{6,66},{7,67},{8,76},{9,... | collective-permute-start | bytes 2764808 | tf_op jit(solution)/shard_map/cond/branch_3_fun/ppermute | solution.py:47
  90.9 16.3 %conv.12 = bf16[1536,640]{1,0:T(8,128)(2,1)S(1)} custom-call(bf16[1600,1920]{1,0:T(8,128)(2,1)} %get-tuple-element.145.refs_0_, bf16[720,640]{1,0:T(8,128)(2,1)} %get-tuple-element.146.refs_1_, bf16[720,640]{1,0:T(8,128)(2,1)} %get-tuple-element.147.refs_2_, bf16[720,640]{1,0:T(8,128)(2,1)} %get-tuple-element.148.refs_3_, ...), custom_call_target="tpu_custom_call" | custom-call | flops 1000000 | bytes 100000 | tf_op jit(solution)/shard_map/cond/branch_3_fun/conv/pallas_call | solution.py:326
  107.3 0.9 collective-permute-start.20
  108.2 1.2 collective-permute-start.19
  109.4 1.2 copy-done.4
  110.6 3.9 %moved.1 = (f32[720,640]{1,0:T(8,128)}, bf16[720,640]{1,0:T(8,128)(2,1)}) custom-call(f32[720,640]{1,0:T(8,128)S(1)} %bitcast.12, bf16[720,640]{1,0:T(8,128)(2,1)S(1)} %copy-done.2, bf16[720,640]{1,0:T(8,128)(2,1)S(1)} %copy-done.4, bf16[720,640]{1,0:T(8,128)(2,1)} %collective-permute-done.21.c_up, bf16[720,640]{1,0:T(8,128)(2,1)} %collective-permute-done.22.c_dn), custom_call_target="tpu_custom_call" | custom-call | flops 1000000 | bytes 100000 | tf_op jit(solution)/shard_map/moved/pallas_call | solution.py:405
  114.5 19.3 %conditional.3 = (f32[720,640]{1,0:T(8,128)}, f32[720,640]{1,0:T(8,128)}, bf16[1536,640]{1,0:T(8,128)(2,1)}) conditional(s32[]{:T(128)} %clamp.4, (bf16[720,640]{1,0:T(8,128)(2,1)}, f32[720,640]{1,0:T(8,128)}, bf16[720,640]{1,0:T(8,128)(2,1)}, f32[720,640]{1,0:T(8,128)}, bf16[1600,1920]{1,0:T(8,128)(2,1)}, ...), branch_computations={%region_4.5_spmd, %region_5.6_spmd, %region_6.7_spmd, %region_7.8_... | conditional | flops 4686400 | bytes 20375292 | solution.py:352
  115.2 6.5 %conv.16 = bf16[1536,640]{1,0:T(8,128)(2,1)} custom-call(bf16[1600,1920]{1,0:T(8,128)(2,1)} %get-tuple-element.177.refs_0_, bf16[720,640]{1,0:T(8,128)(2,1)} %get-tuple-element.178.refs_1_, bf16[1536,640]{1,0:T(8,128)(2,1)S(1)} %get-tuple-element.179.refs_2_), custom_call_target="tpu_custom_call" | custom-call | flops 1000000 | bytes 100000 | tf_op jit(solution)/shard_map/cond/branch_3_fun/conv/pallas_call | solution.py:326
  121.7 8.0 %collective-permute-done.7 = bf16[720,640]{1,0:T(8,128)(2,1)S(1)} collective-permute-done((bf16[720,640]{1,0:T(8,128)(2,1)}, bf16[720,640]{1,0:T(8,128)(2,1)S(1)}, u32[]{:S(2)}, u32[]{:S(2)}) %collective-permute-start.7) | collective-permute-done | bytes 921632 | tf_op jit(solution)/shard_map/cond/branch_3_fun/ppermute | solution.py:32
  129.7 4.1 %fusion.3 = (f32[720,640]{1,0:T(8,128)}, f32[720,640]{1,0:T(8,128)}) fusion(f32[720,640]{1,0:T(8,128)} %get-tuple-element.175, bf16[720,640]{1,0:T(8,128)(2,1)S(1)} %collective-permute-done.7, f32[720,640]{1,0:T(8,128)S(1)} %copy-done.12, bf16[720,640]{1,0:T(8,128)(2,1)} %get-tuple-element.174), kind=kLoop, calls=%fused_computation.11 | loop fusion | flops 3686400 | bytes 9216000 | tf_op jit(solution)/shard_map/cond/branch_3_fun/mul | solution.py:420
  133.8 8.7 %conv.17 = bf16[1536,640]{1,0:T(8,128)(2,1)} custom-call(bf16[1600,1920]{1,0:T(8,128)(2,1)} %spread.1.refs_0_, bf16[720,640]{1,0:T(8,128)(2,1)} %collective-permute-done.19.refs_1_, bf16[720,640]{1,0:T(8,128)(2,1)} %collective-permute-done.20.refs_2_, bf16[1536,640]{1,0:T(8,128)(2,1)} %get-tuple-element.280.refs_3_, bf16[1536,640]{1,0:T(8,128)(2,1)} %bitcast.20), custom_call_target="tpu_custom_call" | custom-call | flops 1000000 | bytes 100000 | tf_op jit(solution)/shard_map/conv/pallas_call | solution.py:326
  (55 shorter events, 3.8 us)
Async XLA Ops:
  0.6 7.4 %copy-start.18 = (f32[640]{0:T(1024)S(1)}, f32[640]{0:T(1024)}, u32[]{:S(2)}) copy-start(f32[640]{0:T(1024)} %param.17) | copy-start | bytes 7684
  0.6 8.0 %copy-start.19 = (f32[640]{0:T(1024)S(1)}, f32[640]{0:T(1024)}, u32[]{:S(2)}) copy-start(f32[640]{0:T(1024)} %param.18) | copy-start | bytes 7684
  2.3 28.6 %copy-start.13 = (bf16[720,640]{1,0:T(8,128)(2,1)}, bf16[720,640]{1,0:T(8,128)(2,1)S(1)}, u32[]{:S(2)}) copy-start(bf16[720,640]{1,0:T(8,128)(2,1)S(1)} %bitcast_convert_fusion) | copy-start | bytes 2764804
  2.3 25.1 %collective-permute-start.10 = (bf16[720,640]{1,0:T(8,128)(2,1)S(1)}, bf16[720,640]{1,0:T(8,128)(2,1)S(1)}, u32[]{:S(2)}, u32[]{:S(2)}) collective-permute-start(bf16[720,640]{1,0:T(8,128)(2,1)S(1)} %bitcast_convert_fusion), channel_id=1, source_target_pairs={{0,4},{1,5},{2,6},{3,7},{4,0},{5,1},{6,2},{7,3},{8,12},{9,13},{10,... | collective-permute-start | bytes 2764808 | tf_op jit(solution)/shard_map/ppermute | solution.py:28
  4.0 23.5 %collective-permute-start.9 = (bf16[720,640]{1,0:T(8,128)(2,1)S(1)}, bf16[720,640]{1,0:T(8,128)(2,1)S(1)}, u32[]{:S(2)}, u32[]{:S(2)}) collective-permute-start(bf16[720,640]{1,0:T(8,128)(2,1)S(1)} %bitcast_convert_fusion), channel_id=1, source_target_pairs={{0,3},{1,0},{2,1},{3,2},{4,7},{5,4},{6,5},{7,6},{8,11},{9,8},{10,9... | collective-permute-start | bytes 2764808 | tf_op jit(solution)/shard_map/ppermute | solution.py:28
  8.1 22.8 %collective-permute-start.8 = (bf16[720,640]{1,0:T(8,128)(2,1)S(1)}, bf16[720,640]{1,0:T(8,128)(2,1)S(1)}, u32[]{:S(2)}, u32[]{:S(2)}) collective-permute-start(bf16[720,640]{1,0:T(8,128)(2,1)S(1)} %bitcast_convert_fusion), channel_id=1, source_target_pairs={{0,1},{1,2},{2,3},{3,0},{4,5},{5,6},{6,7},{7,4},{8,9},{9,10},{10,1... | collective-permute-start | bytes 2764808 | tf_op jit(solution)/shard_map/ppermute | solution.py:28
  27.4 4.9 %copy-start.17 = (bf16[720,640]{1,0:T(8,128)(2,1)}, bf16[720,640]{1,0:T(8,128)(2,1)S(1)}, u32[]{:S(2)}) copy-start(bf16[720,640]{1,0:T(8,128)(2,1)S(1)} %collective-permute-done.10) | copy-start | bytes 2764804
  27.5 26.7 %copy-start.14 = (bf16[720,640]{1,0:T(8,128)(2,1)}, bf16[720,640]{1,0:T(8,128)(2,1)S(1)}, u32[]{:S(2)}) copy-start(bf16[720,640]{1,0:T(8,128)(2,1)S(1)} %collective-permute-done.9.w_p) | copy-start | bytes 2764804
  31.8 21.2 %collective-permute-start.11 = (bf16[720,640]{1,0:T(8,128)(2,1)}, bf16[720,640]{1,0:T(8,128)(2,1)S(1)}, u32[]{:S(2)}, u32[]{:S(2)}) collective-permute-start(bf16[720,640]{1,0:T(8,128)(2,1)} %get-tuple-element.237), channel_id=1, source_target_pairs={{0,4},{1,5},{2,6},{3,7},{4,0},{5,1},{6,2},{7,3},{8,12},{9,13},{10,... | collective-permute-start | bytes 2764808 | tf_op jit(solution)/shard_map/ppermute | solution.py:28
  32.3 21.8 %collective-permute-start.12 = (bf16[720,640]{1,0:T(8,128)(2,1)}, bf16[720,640]{1,0:T(8,128)(2,1)S(1)}, u32[]{:S(2)}, u32[]{:S(2)}) collective-permute-start(bf16[720,640]{1,0:T(8,128)(2,1)} %get-tuple-element.238), channel_id=1, source_target_pairs={{0,1},{1,2},{2,3},{3,0},{4,5},{5,6},{6,7},{7,4},{8,9},{9,10},{10,1... | collective-permute-start | bytes 2764808 | tf_op jit(solution)/shard_map/ppermute | solution.py:28
  32.3 21.8 %collective-permute-start.13 = (bf16[720,640]{1,0:T(8,128)(2,1)}, bf16[720,640]{1,0:T(8,128)(2,1)S(1)}, u32[]{:S(2)}, u32[]{:S(2)}) collective-permute-start(bf16[720,640]{1,0:T(8,128)(2,1)} %get-tuple-element.239), channel_id=1, source_target_pairs={{0,3},{1,0},{2,1},{3,2},{4,7},{5,4},{6,5},{7,6},{8,11},{9,8},{10,9... | collective-permute-start | bytes 2764808 | tf_op jit(solution)/shard_map/ppermute | solution.py:28
  35.5 13.6 %copy-start = (bf16[1536,640]{1,0:T(8,128)(2,1)S(1)}, bf16[1536,640]{1,0:T(8,128)(2,1)}, u32[]{:S(2)}) copy-start(bf16[1536,640]{1,0:T(8,128)(2,1)} %get-tuple-element.243.hidden) | copy-start | bytes 5898244
  49.1 5.0 %copy-start.5 = (bf16[720,640]{1,0:T(8,128)(2,1)S(1)}, bf16[720,640]{1,0:T(8,128)(2,1)}, u32[]{:S(2)}) copy-start(bf16[720,640]{1,0:T(8,128)(2,1)} %get-tuple-element.248.g10) | copy-start | bytes 2764804
  49.1 5.0 %copy-start.6 = (bf16[720,640]{1,0:T(8,128)(2,1)S(1)}, bf16[720,640]{1,0:T(8,128)(2,1)}, u32[]{:S(2)}) copy-start(bf16[720,640]{1,0:T(8,128)(2,1)} %get-tuple-element.242.g02) | copy-start | bytes 2764804
  49.1 5.0 %copy-start.16 = (bf16[720,640]{1,0:T(8,128)(2,1)S(1)}, bf16[720,640]{1,0:T(8,128)(2,1)}, u32[]{:S(2)}) copy-start(bf16[720,640]{1,0:T(8,128)(2,1)} %copy-done.15) | copy-start | bytes 2764804
  55.8 19.4 %copy-start.7 = (bf16[720,640]{1,0:T(8,128)(2,1)S(1)}, bf16[720,640]{1,0:T(8,128)(2,1)}, u32[]{:S(2)}) copy-start(bf16[720,640]{1,0:T(8,128)(2,1)} %get-tuple-element.260.g0p) | copy-start | bytes 2764804
  55.8 19.4 %copy-start.8 = (bf16[720,640]{1,0:T(8,128)(2,1)S(1)}, bf16[720,640]{1,0:T(8,128)(2,1)}, u32[]{:S(2)}) copy-start(bf16[720,640]{1,0:T(8,128)(2,1)} %get-tuple-element.262.g0m) | copy-start | bytes 2764804
  55.8 29.0 %collective-permute-start.16 = (bf16[720,640]{1,0:T(8,128)(2,1)}, bf16[720,640]{1,0:T(8,128)(2,1)S(1)}, u32[]{:S(2)}, u32[]{:S(2)}) collective-permute-start(bf16[720,640]{1,0:T(8,128)(2,1)} %get-tuple-element.253), channel_id=1, source_target_pairs={{0,4},{1,5},{2,6},{3,7},{4,0},{5,1},{6,2},{7,3},{8,12},{9,13},{10,... | collective-permute-start | bytes 2764808 | tf_op jit(solution)/shard_map/ppermute | solution.py:28
  57.4 17.8 %collective-permute-start.18 = (bf16[368,640]{1,0:T(8,128)(2,1)}, bf16[368,640]{1,0:T(8,128)(2,1)S(1)}, u32[]{:S(2)}, u32[]{:S(2)}) collective-permute-start(bf16[368,640]{1,0:T(8,128)(2,1)} %get-tuple-element.255), channel_id=1, source_target_pairs={{0,3},{1,0},{2,1},{3,2},{4,7},{5,4},{6,5},{7,6},{8,11},{9,8},{10,9... | collective-permute-start | bytes 1413128 | tf_op jit(solution)/shard_map/ppermute | solution.py:28
  60.4 24.5 %collective-permute-start.15 = (bf16[368,640]{1,0:T(8,128)(2,1)}, bf16[368,640]{1,0:T(8,128)(2,1)}, u32[]{:S(2)}, u32[]{:S(2)}) collective-permute-start(bf16[368,640]{1,0:T(8,128)(2,1)} %get-tuple-element.252), channel_id=1, source_target_pairs={{0,3},{1,0},{2,1},{3,2},{4,7},{5,4},{6,5},{7,6},{8,11},{9,8},{10,9... | collective-permute-start | bytes 1413128 | tf_op jit(solution)/shard_map/ppermute | solution.py:28
  60.4 14.8 %collective-permute-start.17 = (bf16[352,640]{1,0:T(8,128)(2,1)}, bf16[352,640]{1,0:T(8,128)(2,1)}, u32[]{:S(2)}, u32[]{:S(2)}) collective-permute-start(bf16[352,640]{1,0:T(8,128)(2,1)} %get-tuple-element.254), channel_id=1, source_target_pairs={{0,1},{1,2},{2,3},{3,0},{4,5},{5,6},{6,7},{7,4},{8,9},{9,10},{10,1... | collective-permute-start | bytes 1351688 | tf_op jit(solution)/shard_map/ppermute | solution.py:28
  62.4 22.5 %collective-permute-start.14 = (bf16[352,640]{1,0:T(8,128)(2,1)}, bf16[352,640]{1,0:T(8,128)(2,1)}, u32[]{:S(2)}, u32[]{:S(2)}) collective-permute-start(bf16[352,640]{1,0:T(8,128)(2,1)} %get-tuple-element.251), channel_id=1, source_target_pairs={{0,1},{1,2},{2,3},{3,0},{4,5},{5,6},{6,7},{7,4},{8,9},{9,10},{10,1... | collective-permute-start | bytes 1351688 | tf_op jit(solution)/shard_map/ppermute | solution.py:28
  77.7 31.7 %collective-permute-start.21 = (bf16[720,640]{1,0:T(8,128)(2,1)}, bf16[720,640]{1,0:T(8,128)(2,1)}, u32[]{:S(2)}, u32[]{:S(2)}) collective-permute-start(bf16[720,640]{1,0:T(8,128)(2,1)} %get-tuple-element.263), channel_id=1, source_target_pairs={{0,1},{1,2},{2,3},{3,0},{4,5},{5,6},{6,7},{7,4},{8,9},{9,10},{10,1... | collective-permute-start | bytes 2764808 | tf_op jit(solution)/shard_map/ppermute | solution.py:28
  78.4 30.9 %collective-permute-start.22 = (bf16[720,640]{1,0:T(8,128)(2,1)}, bf16[720,640]{1,0:T(8,128)(2,1)}, u32[]{:S(2)}, u32[]{:S(2)}) collective-permute-start(bf16[720,640]{1,0:T(8,128)(2,1)} %get-tuple-element.264), channel_id=1, source_target_pairs={{0,3},{1,0},{2,1},{3,2},{4,7},{5,4},{6,5},{7,6},{8,11},{9,8},{10,9... | collective-permute-start | bytes 2764808 | tf_op jit(solution)/shard_map/ppermute | solution.py:28
  87.4 27.1 %collective-permute-start.23 = (bf16[720,640]{1,0:T(8,128)(2,1)}, bf16[720,640]{1,0:T(8,128)(2,1)}, u32[]{:S(2)}, u32[]{:S(2)}) collective-permute-start(bf16[720,640]{1,0:T(8,128)(2,1)} %pad_maximum_fusion), channel_id=1, source_target_pairs={{0,4},{1,5},{2,6},{3,7},{4,0},{5,1},{6,2},{7,3},{8,12},{9,13},{10,... | collective-permute-start | bytes 2764808 | tf_op jit(solution)/shard_map/ppermute | solution.py:28
  87.8 21.5 %copy-start.1 = (f32[1,720,640]{2,1,0:T(8,128)S(1)}, f32[1,720,640]{2,1,0:T(8,128)}, u32[]{:S(2)}) copy-start(f32[1,720,640]{2,1,0:T(8,128)} %param.20) | copy-start | bytes 5529604
  87.8 21.6 %copy-start.2 = (bf16[720,640]{1,0:T(8,128)(2,1)S(1)}, bf16[720,640]{1,0:T(8,128)(2,1)}, u32[]{:S(2)}) copy-start(bf16[720,640]{1,0:T(8,128)(2,1)} %get-tuple-element.272.g00) | copy-start | bytes 2764804
  87.8 19.4 %collective-permute-start.3 = (bf16[720,640]{1,0:T(8,128)(2,1)}, bf16[720,640]{1,0:T(8,128)(2,1)}, u32[]{:S(2)}, u32[]{:S(2)}) collective-permute-start(bf16[720,640]{1,0:T(8,128)(2,1)} %get-tuple-element.144), channel_id=1, source_target_pairs={{0,68},{1,69},{2,70},{3,71},{4,64},{5,65},{6,66},{7,67},{8,76},{9,... | collective-permute-start | bytes 2764808 | tf_op jit(solution)/shard_map/cond/branch_3_fun/ppermute | solution.py:47
  107.3 26.6 %collective-permute-start.20 = (bf16[720,640]{1,0:T(8,128)(2,1)}, bf16[720,640]{1,0:T(8,128)(2,1)}, u32[]{:S(2)}, u32[]{:S(2)}) collective-permute-start(bf16[720,640]{1,0:T(8,128)(2,1)} %copy-done.17), channel_id=1, source_target_pairs={{0,3},{1,0},{2,1},{3,2},{4,7},{5,4},{6,5},{7,6},{8,11},{9,8},{10,9... | collective-permute-start | bytes 2764808 | tf_op jit(solution)/shard_map/ppermute | solution.py:28
  108.2 25.7 %collective-permute-start.19 = (bf16[720,640]{1,0:T(8,128)(2,1)}, bf16[720,640]{1,0:T(8,128)(2,1)}, u32[]{:S(2)}, u32[]{:S(2)}) collective-permute-start(bf16[720,640]{1,0:T(8,128)(2,1)} %copy-done.17), channel_id=1, source_target_pairs={{0,1},{1,2},{2,3},{3,0},{4,5},{5,6},{6,7},{7,4},{8,9},{9,10},{10,1... | collective-permute-start | bytes 2764808 | tf_op jit(solution)/shard_map/ppermute | solution.py:28
  114.5 15.2 %collective-permute-start.7 = (bf16[720,640]{1,0:T(8,128)(2,1)}, bf16[720,640]{1,0:T(8,128)(2,1)S(1)}, u32[]{:S(2)}, u32[]{:S(2)}) collective-permute-start(bf16[720,640]{1,0:T(8,128)(2,1)} %get-tuple-element.176), channel_id=1, source_target_pairs={{0,64},{8,72},{16,80},{24,88},{32,96},{40,104},{48,112},{56,120},{... | collective-permute-start | bytes 2764808 | tf_op jit(solution)/shard_map/cond/branch_3_fun/ppermute | solution.py:32
  115.2 14.5 %copy-start.12 = (f32[720,640]{1,0:T(8,128)S(1)}, f32[720,640]{1,0:T(8,128)}, u32[]{:S(2)}) copy-start(f32[720,640]{1,0:T(8,128)} %get-tuple-element.173) | copy-start | bytes 5529604 | tf_op jit(solution)/shard_map/cond
  (3 other events, 5.1 us)

commit v3 on v2

--- a/solution.py
+++ b/solution.py
@@ -133,7 +133,7 @@
         copy.wait()
 
 
-def norm_grad_kernel(lat, cot, gain, bias, hidden_out, turned_out, *rest):
+def norm_grad_kernel(lat, cot, affine, hidden_out, turned_out, *rest):
     outs, (hidden, turned, cots, grads, sem, sem_out) = rest[:4], rest[4:]
 
     def chunk_at(r):
@@ -154,8 +154,8 @@
         return s + fold(off * off)
 
     var = group_mean(lax.fori_loop(0, chunks, squares, zeros))
-    slope = lax.rsqrt(var + 1e-05) * gain[...]
-    shift = bias[...]
+    slope = lax.rsqrt(var + 1e-05) * affine[0:1, :]
+    shift = affine[1:2, :]
 
     @pl.loop(0, chunks)
     def _(r):
@@ -206,7 +206,7 @@
             jax.ShapeDtypeStruct((PIXELS, CHANS), jnp.bfloat16),
             jax.ShapeDtypeStruct((CHANS, PIXELS), jnp.bfloat16),
         ] + [jax.ShapeDtypeStruct((ROWS, CHANS), jnp.bfloat16)] * 4,
-        in_specs=[IN_VMEM] * 4,
+        in_specs=[IN_VMEM] * 3,
         out_specs=[IN_ANY] * 6,
         scratch_shapes=[
             pltpu.VMEM((PIXELS, CHANS), jnp.bfloat16),
@@ -215,7 +215,7 @@
         compiler_params=pltpu.CompilerParams(vmem_limit_bytes=58 * MIB),
         cost_estimate=SHORT,
         name="norm_grad",
-    )(latents, cotangent, gain[None], bias[None])
+    )(latents, cotangent, jnp.stack([gain, bias]))
 
 
 def rest_grad(turned, cotangent):
@@ -320,9 +320,9 @@
         result(m).wait()
 
 
-def conv(taps, places, pieces, others=()):
+def conv(taps, places, pieces, others=(), tall=None):
     blocks = len(set(place[:2] for place in places))
-    tall = 256 if blocks > 2 else 512
+    tall = tall or (256 if blocks > 2 else 512)
     return pl.pallas_call(
         partial(conv_kernel, places, len(others), tall),
         out_shape=jax.ShapeDtypeStruct((PIXELS, CHANS), jnp.bfloat16),
@@ -352,13 +352,15 @@
     return lax.switch(step[0] % 4, [partial(branch, 1 << level) for level in range(4)], *state)
 
 
-def partner_and_conv(by, chosen, own, other, taps, w_m, w_p, top, bottom):
+def partner_and_conv(by, chosen, own, other, taps, w_m, w_p):
     w_partner = weight_from_partner(chosen, by)
-    places = [
-        (0, 0, 0, ROWS), (1, 0, 0, ROWS), (0, 3, 0, ROWS), (0, 1, 0, ROWS),
-        (0, 2, 0, HALF), (0, 2, HALF, ROWS - HALF),
-    ]
-    return w_partner, conv(taps, places, (own, other, w_m, w_p, top, bottom))
+    places = [(0, 0, 0, ROWS), (1, 0, 0, ROWS), (0, 3, 0, ROWS), (0, 1, 0, ROWS)]
+    return w_partner, conv(taps, places, (own, other, w_m, w_p))
+
+
+def join_kernel(top, bottom, both):
+    both[0:HALF, :] = top[...]
+    both[HALF:ROWS, :] = bottom[...]
 
 
 def added(rows, *refs):
@@ -414,12 +416,14 @@
     )(*values)
 
 
-def finish(by, rounded, moved, own_weight, w_partner, taps, corner, acc):
+def finish(by, rounded, moved, own_weight, w_partner, taps, w_far, corner, acc):
     partner = from_partner(rounded, by).astype(jnp.float32)
     both = moved + partner
     new_moment = 0.5 * both
     new_weight = 0.5 * (own_weight + w_partner.astype(jnp.float32)) - 0.025 * both
-    return new_weight, new_moment, conv(taps, [(1, 2, 0, ROWS)], (corner,), (acc,))
+    return new_weight, new_moment, conv(
+        taps, [(0, 2, 0, ROWS), (1, 2, 0, ROWS)], (w_far, corner), (acc,), 256
+    )
 
 
 def on_device(latents, cotangent, gain, bias, weight, momentum, step):
@@ -454,16 +458,17 @@
     c_up = send_inner(to_up, 0, 1)
     c_dn = send_inner(to_dn, 0, -1)
     taps, top, bottom, b_y = together((taps, top, bottom, b_y), to_up, to_dn)
-    corner = send_inner(jnp.concatenate([top, bottom]), 1, 0)
+    w_far, = small(join_kernel, "join", (ROWS,), top, bottom)
+    corner = send_inner(w_far, 1, 0)
     w_partner, acc = from_switch(
-        step, partner_and_conv, chosen, own, w_y, taps, w_m, w_p, top, bottom
+        step, partner_and_conv, chosen, own, w_y, taps, w_m, w_p
     )
     w_y = together((w_y,), acc)[0]
     y_m = send_inner(w_y, 0, 1)
     y_p = send_inner(w_y, 0, -1)
     moved, rounded = moved_rows(own_moment, g00, b_y, c_up, c_dn)
     new_weight, new_moment, acc = from_switch(
-        step, finish, rounded, moved, own_weight, w_partner, taps, corner, acc
+        step, finish, rounded, moved, own_weight, w_partner, taps, w_far, corner, acc
     )
     y_m, y_p = together((y_m, y_p), new_weight, new_moment)
     block_out = conv(taps, [(1, 3, 0, ROWS), (1, 1, 0, ROWS)], (y_m, y_p), (acc, latents))

time: 144 us -> 143 us (level)
  starting transfers between devices: 25.6 us -> 30.1 us
  waiting for transfers between devices: 26.5 us -> 22.3 us
  Pallas kernels: 75.2 us -> 77.5 us
  other arithmetic: 10.4 us -> 8.52 us
    ppermute x1, waiting for transfers between devices: 8.01 us -> 3.42 us  [from_partner(): return lax.ppermute(value, 'group', [(i, (i - by) % 16) for i in range(16)])]
    concatenate x1 -> x0, other arithmetic: 2.51 us -> none  [on_device(): corner = send_inner(jnp.concatenate([top, bottom]), 1, 0)]
    pallas_call x2 -> x3, Pallas kernels: 4.13 us -> 6.59 us  [small(): pl.pallas_call(kernel, out_shape=[jax.ShapeDtypeStruct((count, CHANS), jn...]
    ppermute x1, starting transfers between devices: 3.08 us -> 5.54 us  [weight_from_partner(): return lax.ppermute(value, ('group', 'inner'), pairs)]
    ppermute x1, starting transfers between devices: 0.69 us -> 2.69 us  [from_partner(): return lax.ppermute(value, 'group', [(i, (i - by) % 16) for i in range(16)])]
  transfers between devices with their start and end apart: 18 -> 18, of which waited for: 6 -> 6; matrix products, arithmetic and copies ran while one was open for 7% -> 5% of each run, Pallas kernels for 45% -> 47%
where the time goes in v3:
time: 143 us; the launch traced here: 142 us
  Pallas kernels  77.5 us (54%)
  starting transfers between devices  30.1 us (21%)
  waiting for transfers between devices  22.3 us (16%)
  other arithmetic  8.52 us (6%)
  local copies, waits for them, and re-layouts  2.19 us (2%)
  between operations  1.7 us (1%)
    pallas_call x3, Pallas kernels, conv(): pl.pallas_call(partial(conv_kernel, places, len(others), tall), out_shape...  31.4 us
    ppermute x16, starting transfers between devices, send_inner(): return lax.ppermute(value, 'inner', [(i, place(i)) for i in range(8)])  21.8 us
    ppermute x16, waiting for transfers between devices, send_inner(): return lax.ppermute(value, 'inner', [(i, place(i)) for i in range(8)])  18.9 us
    pallas_call x1, Pallas kernels, norm_grad(): pl.pallas_call(norm_grad_kernel, out_shape=[jax.ShapeDtypeStruct((PIXELS,...  18.1 us
    pallas_call x1, Pallas kernels, rest_grad(): pl.pallas_call(rest_grad_kernel, out_shape=[jax.ShapeDtypeStruct((ROWS, C...  13.6 us
    pallas_call x3, Pallas kernels, small(): pl.pallas_call(kernel, out_shape=[jax.ShapeDtypeStruct((count, CHANS), jn...  6.59 us
    ppermute x1, starting transfers between devices, weight_from_partner(): return lax.ppermute(value, ('group', 'inner'), pairs)  5.54 us
    mul x1, other arithmetic, finish(): new_moment = 0.5 * both  4.09 us
  transfers between devices with their start and end apart: 18, of which 6 were waited for; matrix products, arithmetic and copies ran while one was open for 5% of the time, Pallas kernels for 47%

profile of v3, /device:TPU:0, one launch (start us, length us, event | category | flops | bytes accessed | tf_op | source)
XLA Modules:
  0.0 142.3 jit_solution(4070705606970101420)
XLA Ops:
  0.7 1.6 %bitcast_convert_fusion = bf16[720,640]{1,0:T(8,128)(2,1)S(1)} fusion(f32[1,720,640]{2,1,0:T(8,128)} %param.19), kind=kLoop, calls=%fused_computation.14 | loop fusion | flops 460800 | bytes 2764800 | tf_op jit(solution)/shard_map/convert_element_type | solution.py:431
  2.3 1.7 %collective-permute-start.10 = (bf16[720,640]{1,0:T(8,128)(2,1)S(1)}, bf16[720,640]{1,0:T(8,128)(2,1)S(1)}, u32[]{:S(2)}, u32[]{:S(2)}) collective-permute-start(bf16[720,640]{1,0:T(8,128)(2,1)S(1)} %bitcast_convert_fusion), channel_id=1, source_target_pairs={{0,4},{1,5},{2,6},{3,7},{4,0},{5,1},{6,2},{7,3},{8,12},{9,13},{10,... | collective-permute-start | bytes 2764808 | tf_op jit(solution)/shard_map/ppermute | solution.py:28
  4.0 4.0 %collective-permute-start.9 = (bf16[720,640]{1,0:T(8,128)(2,1)S(1)}, bf16[720,640]{1,0:T(8,128)(2,1)S(1)}, u32[]{:S(2)}, u32[]{:S(2)}) collective-permute-start(bf16[720,640]{1,0:T(8,128)(2,1)S(1)} %bitcast_convert_fusion), channel_id=1, source_target_pairs={{0,3},{1,0},{2,1},{3,2},{4,7},{5,4},{6,5},{7,6},{8,11},{9,8},{10,9... | collective-permute-start | bytes 2764808 | tf_op jit(solution)/shard_map/ppermute | solution.py:28
  8.7 18.1 %norm_grad.1 = (bf16[1536,640]{1,0:T(8,128)(2,1)}, bf16[640,1536]{1,0:T(8,128)(2,1)}, bf16[720,640]{1,0:T(8,128)(2,1)}, bf16[720,640]{1,0:T(8,128)(2,1)}, bf16[7...) custom-call(bf16[1536,640]{1,0:T(8,128)(2,1)} %bitcast.19, bf16[1536,640]{1,0:T(8,128)(2,1)} %bitcast.17, ...), custom_call_target="tpu_custom_call" | custom-call | flops 1000000 | bytes 100000 | tf_op jit(solution)/shard_map/norm_grad/pallas_call | solution.py:203
  27.5 3.4 %collective-permute-done.8.w_m = bf16[720,640]{1,0:T(8,128)(2,1)S(1)} collective-permute-done((bf16[720,640]{1,0:T(8,128)(2,1)S(1)}, bf16[720,640]{1,0:T(8,128)(2,1)S(1)}, u32[]{:S(2)}, u32[]{:S(2)}) %collective-permute-start.8) | collective-permute-done | bytes 921632 | tf_op jit(solution)/shard_map/ppermute | solution.py:28
  30.9 0.9 copy-done.15
  32.3 3.2 %collective-permute-start.13 = (bf16[720,640]{1,0:T(8,128)(2,1)}, bf16[720,640]{1,0:T(8,128)(2,1)S(1)}, u32[]{:S(2)}, u32[]{:S(2)}) collective-permute-start(bf16[720,640]{1,0:T(8,128)(2,1)} %get-tuple-element.227), channel_id=1, source_target_pairs={{0,3},{1,0},{2,1},{3,2},{4,7},{5,4},{6,5},{7,6},{8,11},{9,8},{10,9... | collective-permute-start | bytes 2764808 | tf_op jit(solution)/shard_map/ppermute | solution.py:28
  35.5 13.6 %rest_grad.1 = (bf16[720,640]{1,0:T(8,128)(2,1)}, bf16[720,640]{1,0:T(8,128)(2,1)}, bf16[720,640]{1,0:T(8,128)(2,1)}, bf16[720,640]{1,0:T(8,128)(2,1)}) custom-call(bf16[640,1536]{1,0:T(8,128)(2,1)} %get-tuple-element.229.turned, bf16[1536,640]{1,0:T(8,128)(2,1)} %bitcast.18), custom_call_target="tpu_custom_call" | custom-call | flops 1000000 | bytes 100000 | tf_op jit(solution)/shard_map/rest_grad/pallas_call | solution.py:222
  49.1 3.8 %spread.1.refs_0_ = bf16[1600,1920]{1,0:T(8,128)(2,1)} custom-call(bf16[1536,640]{1,0:T(8,128)(2,1)S(1)} %copy-done), custom_call_target="tpu_custom_call" | custom-call | flops 1000000 | bytes 100000 | tf_op jit(solution)/shard_map/spread/pallas_call | solution.py:235
  53.0 1.1 collective-permute-done.12.a_p
  54.2 1.7 %sums.1 = (bf16[352,640]{1,0:T(8,128)(2,1)}, bf16[368,640]{1,0:T(8,128)(2,1)}, bf16[720,640]{1,0:T(8,128)(2,1)}, bf16[352,640]{1,0:T(8,128)(2,1)}, bf16[368,640]{1,0:T(8,128)(2,1)}) custom-call(bf16[720,640]{1,0:T(8,128)(2,1)S(1)} %collective-permute-done.11.a_y, bf16[720,640]{1,0:T(8,128)(2,1)S(1)} %copy-done.6, ...), custom_call_target="tpu_custom_call" | custom-call | flops 1000000 | bytes 100000 | tf_op jit(solution)/shard_map/sums/pallas_call | solution.py:387
  55.8 1.6 %collective-permute-start.16 = (bf16[720,640]{1,0:T(8,128)(2,1)}, bf16[720,640]{1,0:T(8,128)(2,1)S(1)}, u32[]{:S(2)}, u32[]{:S(2)}) collective-permute-start(bf16[720,640]{1,0:T(8,128)(2,1)} %get-tuple-element.241), channel_id=1, source_target_pairs={{0,4},{1,5},{2,6},{3,7},{4,0},{5,1},{6,2},{7,3},{8,12},{9,13},{10,... | collective-permute-start | bytes 2764808 | tf_op jit(solution)/shard_map/ppermute | solution.py:28
  57.4 2.9 %collective-permute-start.18 = (bf16[368,640]{1,0:T(8,128)(2,1)}, bf16[368,640]{1,0:T(8,128)(2,1)}, u32[]{:S(2)}, u32[]{:S(2)}) collective-permute-start(bf16[368,640]{1,0:T(8,128)(2,1)} %get-tuple-element.243), channel_id=1, source_target_pairs={{0,3},{1,0},{2,1},{3,2},{4,7},{5,4},{6,5},{7,6},{8,11},{9,8},{10,9... | collective-permute-start | bytes 1413128 | tf_op jit(solution)/shard_map/ppermute | solution.py:28
  60.4 2.0 %collective-permute-start.17 = (bf16[352,640]{1,0:T(8,128)(2,1)}, bf16[352,640]{1,0:T(8,128)(2,1)}, u32[]{:S(2)}, u32[]{:S(2)}) collective-permute-start(bf16[352,640]{1,0:T(8,128)(2,1)} %get-tuple-element.242), channel_id=1, source_target_pairs={{0,1},{1,2},{2,3},{3,0},{4,5},{5,6},{6,7},{7,4},{8,9},{9,10},{10,1... | collective-permute-start | bytes 1351688 | tf_op jit(solution)/shard_map/ppermute | solution.py:28
  63.1 2.2 %broadcast_select_fusion = bf16[720,640]{1,0:T(8,128)(2,1)} fusion(bf16[720,640]{1,0:T(8,128)(2,1)} %copy-done.17, bf16[720,640]{1,0:T(8,128)(2,1)} %copy-done.13, pred[]{:T(512)S(6)} %ne.37), kind=kLoop, calls=%fused_computation.12 | loop fusion | flops 460800 | bytes 2764801 | tf_op jit(solution)/shard_map/jit(_where)/select_n | solution.py:38
  65.4 9.9 %collective-permute-done.17.b_up = bf16[352,640]{1,0:T(8,128)(2,1)} collective-permute-done((bf16[352,640]{1,0:T(8,128)(2,1)}, bf16[352,640]{1,0:T(8,128)(2,1)}, u32[]{:S(2)}, u32[]{:S(2)}) %collective-permute-start.17) | collective-permute-done | bytes 450592 | tf_op jit(solution)/shard_map/ppermute | solution.py:28
  75.2 2.6 %ends.1 = (bf16[720,640]{1,0:T(8,128)(2,1)}, bf16[720,640]{1,0:T(8,128)(2,1)}) custom-call(bf16[352,640]{1,0:T(8,128)(2,1)} %collective-permute-done.17.b_up, bf16[720,640]{1,0:T(8,128)(2,1)S(1)} %copy-done.7, bf16[368,640]{1,0:T(8,128)(2,1)} %collective-permute-done.18.b_dn, bf16[720,640]{1,0:T(8,128)(2,1)S(1)} %copy-done.8), custom_call_target="tpu_custom_call" | custom-call | flops 1000000 | bytes 100000 | tf_op jit(solution)/shard_map/ends/pallas_call | solution.py:387
  78.6 2.5 %collective-permute-start.22 = (bf16[720,640]{1,0:T(8,128)(2,1)}, bf16[720,640]{1,0:T(8,128)(2,1)}, u32[]{:S(2)}, u32[]{:S(2)}) collective-permute-start(bf16[720,640]{1,0:T(8,128)(2,1)} %get-tuple-element.252), channel_id=1, source_target_pairs={{0,3},{1,0},{2,1},{3,2},{4,7},{5,4},{6,5},{7,6},{8,11},{9,8},{10,9... | collective-permute-start | bytes 2764808 | tf_op jit(solution)/shard_map/ppermute | solution.py:28
  81.0 3.9 %collective-permute-done.14.top = bf16[352,640]{1,0:T(8,128)(2,1)} collective-permute-done((bf16[352,640]{1,0:T(8,128)(2,1)}, bf16[352,640]{1,0:T(8,128)(2,1)}, u32[]{:S(2)}, u32[]{:S(2)}) %collective-permute-start.14) | collective-permute-done | bytes 450592 | tf_op jit(solution)/shard_map/ppermute | solution.py:28
  84.9 2.4 %join.1 = bf16[720,640]{1,0:T(8,128)(2,1)} custom-call(bf16[352,640]{1,0:T(8,128)(2,1)} %collective-permute-done.14.top, bf16[368,640]{1,0:T(8,128)(2,1)S(1)} %collective-permute-done.15.bottom), custom_call_target="tpu_custom_call" | custom-call | flops 1000000 | bytes 100000 | tf_op jit(solution)/shard_map/join/pallas_call | solution.py:387
  87.7 19.2 %conditional.2 = (bf16[720,640]{1,0:T(8,128)(2,1)}, bf16[1536,640]{1,0:T(8,128)(2,1)S(1)}) conditional(s32[]{:T(128)} %clamp.4, (bf16[720,640]{1,0:T(8,128)(2,1)}, bf16[1600,1920]{1,0:T(8,128)(2,1)}, bf16[720,640]{1,0:T(8,128)(2,1)}, bf16[720,640]{1,0:T(8,128)(2,1)}, bf16[720,640]{1,0:T(8,128)(2,1)}, ...), branch_computations={%region_0.1_spmd, %region_1.2_spmd, %region_2.3_spmd, %region_3.4_... | conditional | flops 1000000 | bytes 3786456 | solution.py:352
  87.7 5.5 %collective-permute-start.2 = (bf16[720,640]{1,0:T(8,128)(2,1)}, bf16[720,640]{1,0:T(8,128)(2,1)}, u32[]{:S(2)}, u32[]{:S(2)}) collective-permute-start(bf16[720,640]{1,0:T(8,128)(2,1)} %get-tuple-element.124), channel_id=1, source_target_pairs={{0,100},{1,101},{2,102},{3,103},{4,96},{5,97},{6,98},{7,99},{8,108... | collective-permute-start | bytes 2764808 | tf_op jit(solution)/shard_map/cond/branch_2_fun/ppermute | solution.py:47
  93.2 13.6 %conv.11 = bf16[1536,640]{1,0:T(8,128)(2,1)S(1)} custom-call(bf16[1600,1920]{1,0:T(8,128)(2,1)} %get-tuple-element.125.refs_0_, bf16[720,640]{1,0:T(8,128)(2,1)} %get-tuple-element.126.refs_1_, bf16[720,640]{1,0:T(8,128)(2,1)} %get-tuple-element.127.refs_2_, bf16[720,640]{1,0:T(8,128)(2,1)} %get-tuple-element.128.refs_3_, ...), custom_call_target="tpu_custom_call" | custom-call | flops 1000000 | bytes 100000 | tf_op jit(solution)/shard_map/cond/branch_2_fun/conv/pallas_call | solution.py:326
  107.7 1.2 collective-permute-start.19
  109.0 1.2 copy-done.4
  110.1 4.0 %moved.1 = (f32[720,640]{1,0:T(8,128)}, bf16[720,640]{1,0:T(8,128)(2,1)}) custom-call(f32[720,640]{1,0:T(8,128)S(1)} %bitcast.12, bf16[720,640]{1,0:T(8,128)(2,1)S(1)} %copy-done.2, bf16[720,640]{1,0:T(8,128)(2,1)S(1)} %copy-done.4, bf16[720,640]{1,0:T(8,128)(2,1)} %collective-permute-done.21.c_up, bf16[720,640]{1,0:T(8,128)(2,1)} %collective-permute-done.22.c_dn), custom_call_target="tpu_custom_call" | custom-call | flops 1000000 | bytes 100000 | tf_op jit(solution)/shard_map/moved/pallas_call | solution.py:407
  114.1 19.3 %conditional.3 = (f32[720,640]{1,0:T(8,128)}, f32[720,640]{1,0:T(8,128)}, bf16[1536,640]{1,0:T(8,128)(2,1)}) conditional(s32[]{:T(128)} %clamp.4, (bf16[720,640]{1,0:T(8,128)(2,1)}, f32[720,640]{1,0:T(8,128)}, bf16[720,640]{1,0:T(8,128)(2,1)}, f32[720,640]{1,0:T(8,128)}, bf16[1600,1920]{1,0:T(8,128)(2,1)}, ...), branch_computations={%region_4.5_spmd, %region_5.6_spmd, %region_6.7_spmd, %region_7.8_... | conditional | flops 4686400 | bytes 20375292 | solution.py:352
  114.1 2.7 %collective-permute-start.6 = (bf16[720,640]{1,0:T(8,128)(2,1)}, bf16[720,640]{1,0:T(8,128)(2,1)S(1)}, u32[]{:S(2)}, u32[]{:S(2)}) collective-permute-start(bf16[720,640]{1,0:T(8,128)(2,1)} %get-tuple-element.155), channel_id=1, source_target_pairs={{0,96},{8,104},{16,112},{24,120},{32,0},{40,8},{48,16},{56,24},{64... | collective-permute-start | bytes 2764808 | tf_op jit(solution)/shard_map/cond/branch_2_fun/ppermute | solution.py:32
  116.8 9.1 %conv.15 = bf16[1536,640]{1,0:T(8,128)(2,1)} custom-call(bf16[1600,1920]{1,0:T(8,128)(2,1)} %get-tuple-element.156.refs_0_, bf16[720,640]{1,0:T(8,128)(2,1)} %get-tuple-element.157.refs_1_, bf16[720,640]{1,0:T(8,128)(2,1)} %get-tuple-element.158.refs_2_, bf16[1536,640]{1,0:T(8,128)(2,1)S(1)} %get-tuple-element.159.refs_3_), custom_call_target="tpu_custom_call" | custom-call | flops 1000000 | bytes 100000 | tf_op jit(solution)/shard_map/cond/branch_2_fun/conv/pallas_call | solution.py:326
  125.9 3.4 %collective-permute-done.6 = bf16[720,640]{1,0:T(8,128)(2,1)S(1)} collective-permute-done((bf16[720,640]{1,0:T(8,128)(2,1)}, bf16[720,640]{1,0:T(8,128)(2,1)S(1)}, u32[]{:S(2)}, u32[]{:S(2)}) %collective-permute-start.6) | collective-permute-done | bytes 921632 | tf_op jit(solution)/shard_map/cond/branch_2_fun/ppermute | solution.py:32
  129.3 4.1 %fusion.2 = (f32[720,640]{1,0:T(8,128)}, f32[720,640]{1,0:T(8,128)}) fusion(f32[720,640]{1,0:T(8,128)} %get-tuple-element.154, bf16[720,640]{1,0:T(8,128)(2,1)S(1)} %collective-permute-done.6, f32[720,640]{1,0:T(8,128)S(1)} %copy-done.11, bf16[720,640]{1,0:T(8,128)(2,1)} %get-tuple-element.153), kind=kLoop, calls=%fused_computation.8 | loop fusion | flops 3686400 | bytes 9216000 | tf_op jit(solution)/shard_map/cond/branch_2_fun/mul | solution.py:422
  133.4 8.7 %conv.17 = bf16[1536,640]{1,0:T(8,128)(2,1)} custom-call(bf16[1600,1920]{1,0:T(8,128)(2,1)} %spread.1.refs_0_, bf16[720,640]{1,0:T(8,128)(2,1)} %collective-permute-done.19.refs_1_, bf16[720,640]{1,0:T(8,128)(2,1)} %collective-permute-done.20.refs_2_, bf16[1536,640]{1,0:T(8,128)(2,1)} %get-tuple-element.268.refs_3_, bf16[1536,640]{1,0:T(8,128)(2,1)} %bitcast.20), custom_call_target="tpu_custom_call" | custom-call | flops 1000000 | bytes 100000 | tf_op jit(solution)/shard_map/conv/pallas_call | solution.py:326
  (56 shorter events, 3.9 us)
Async XLA Ops:
  0.6 7.4 %copy-start.18 = (f32[640]{0:T(1024)S(1)}, f32[640]{0:T(1024)}, u32[]{:S(2)}) copy-start(f32[640]{0:T(1024)} %param.17) | copy-start | bytes 7684
  0.6 7.4 %copy-start.19 = (f32[640]{0:T(1024)S(1)}, f32[640]{0:T(1024)}, u32[]{:S(2)}) copy-start(f32[640]{0:T(1024)} %param.18) | copy-start | bytes 7684
  2.3 28.6 %copy-start.13 = (bf16[720,640]{1,0:T(8,128)(2,1)}, bf16[720,640]{1,0:T(8,128)(2,1)S(1)}, u32[]{:S(2)}) copy-start(bf16[720,640]{1,0:T(8,128)(2,1)S(1)} %bitcast_convert_fusion) | copy-start | bytes 2764804
  2.3 24.6 %collective-permute-start.10 = (bf16[720,640]{1,0:T(8,128)(2,1)S(1)}, bf16[720,640]{1,0:T(8,128)(2,1)S(1)}, u32[]{:S(2)}, u32[]{:S(2)}) collective-permute-start(bf16[720,640]{1,0:T(8,128)(2,1)S(1)} %bitcast_convert_fusion), channel_id=1, source_target_pairs={{0,4},{1,5},{2,6},{3,7},{4,0},{5,1},{6,2},{7,3},{8,12},{9,13},{10,... | collective-permute-start | bytes 2764808 | tf_op jit(solution)/shard_map/ppermute | solution.py:28
  4.0 23.5 %collective-permute-start.9 = (bf16[720,640]{1,0:T(8,128)(2,1)S(1)}, bf16[720,640]{1,0:T(8,128)(2,1)S(1)}, u32[]{:S(2)}, u32[]{:S(2)}) collective-permute-start(bf16[720,640]{1,0:T(8,128)(2,1)S(1)} %bitcast_convert_fusion), channel_id=1, source_target_pairs={{0,3},{1,0},{2,1},{3,2},{4,7},{5,4},{6,5},{7,6},{8,11},{9,8},{10,9... | collective-permute-start | bytes 2764808 | tf_op jit(solution)/shard_map/ppermute | solution.py:28
  8.1 22.8 %collective-permute-start.8 = (bf16[720,640]{1,0:T(8,128)(2,1)S(1)}, bf16[720,640]{1,0:T(8,128)(2,1)S(1)}, u32[]{:S(2)}, u32[]{:S(2)}) collective-permute-start(bf16[720,640]{1,0:T(8,128)(2,1)S(1)} %bitcast_convert_fusion), channel_id=1, source_target_pairs={{0,1},{1,2},{2,3},{3,0},{4,5},{5,6},{6,7},{7,4},{8,9},{9,10},{10,1... | collective-permute-start | bytes 2764808 | tf_op jit(solution)/shard_map/ppermute | solution.py:28
  26.8 5.4 %copy-start.17 = (bf16[720,640]{1,0:T(8,128)(2,1)}, bf16[720,640]{1,0:T(8,128)(2,1)S(1)}, u32[]{:S(2)}) copy-start(bf16[720,640]{1,0:T(8,128)(2,1)S(1)} %collective-permute-done.10) | copy-start | bytes 2764804
  27.5 26.7 %copy-start.14 = (bf16[720,640]{1,0:T(8,128)(2,1)}, bf16[720,640]{1,0:T(8,128)(2,1)S(1)}, u32[]{:S(2)}) copy-start(bf16[720,640]{1,0:T(8,128)(2,1)S(1)} %collective-permute-done.9.w_p) | copy-start | bytes 2764804
  31.8 21.2 %collective-permute-start.11 = (bf16[720,640]{1,0:T(8,128)(2,1)}, bf16[720,640]{1,0:T(8,128)(2,1)S(1)}, u32[]{:S(2)}, u32[]{:S(2)}) collective-permute-start(bf16[720,640]{1,0:T(8,128)(2,1)} %get-tuple-element.225), channel_id=1, source_target_pairs={{0,4},{1,5},{2,6},{3,7},{4,0},{5,1},{6,2},{7,3},{8,12},{9,13},{10,... | collective-permute-start | bytes 2764808 | tf_op jit(solution)/shard_map/ppermute | solution.py:28
  32.3 21.8 %collective-permute-start.12 = (bf16[720,640]{1,0:T(8,128)(2,1)}, bf16[720,640]{1,0:T(8,128)(2,1)S(1)}, u32[]{:S(2)}, u32[]{:S(2)}) collective-permute-start(bf16[720,640]{1,0:T(8,128)(2,1)} %get-tuple-element.226), channel_id=1, source_target_pairs={{0,1},{1,2},{2,3},{3,0},{4,5},{5,6},{6,7},{7,4},{8,9},{9,10},{10,1... | collective-permute-start | bytes 2764808 | tf_op jit(solution)/shard_map/ppermute | solution.py:28
  32.3 21.8 %collective-permute-start.13 = (bf16[720,640]{1,0:T(8,128)(2,1)}, bf16[720,640]{1,0:T(8,128)(2,1)S(1)}, u32[]{:S(2)}, u32[]{:S(2)}) collective-permute-start(bf16[720,640]{1,0:T(8,128)(2,1)} %get-tuple-element.227), channel_id=1, source_target_pairs={{0,3},{1,0},{2,1},{3,2},{4,7},{5,4},{6,5},{7,6},{8,11},{9,8},{10,9... | collective-permute-start | bytes 2764808 | tf_op jit(solution)/shard_map/ppermute | solution.py:28
  35.5 13.6 %copy-start = (bf16[1536,640]{1,0:T(8,128)(2,1)S(1)}, bf16[1536,640]{1,0:T(8,128)(2,1)}, u32[]{:S(2)}) copy-start(bf16[1536,640]{1,0:T(8,128)(2,1)} %get-tuple-element.231.hidden) | copy-start | bytes 5898244
  49.1 5.0 %copy-start.5 = (bf16[720,640]{1,0:T(8,128)(2,1)S(1)}, bf16[720,640]{1,0:T(8,128)(2,1)}, u32[]{:S(2)}) copy-start(bf16[720,640]{1,0:T(8,128)(2,1)} %get-tuple-element.236.g10) | copy-start | bytes 2764804
  49.1 5.0 %copy-start.6 = (bf16[720,640]{1,0:T(8,128)(2,1)S(1)}, bf16[720,640]{1,0:T(8,128)(2,1)}, u32[]{:S(2)}) copy-start(bf16[720,640]{1,0:T(8,128)(2,1)} %get-tuple-element.230.g02) | copy-start | bytes 2764804
  49.1 5.0 %copy-start.16 = (bf16[720,640]{1,0:T(8,128)(2,1)S(1)}, bf16[720,640]{1,0:T(8,128)(2,1)}, u32[]{:S(2)}) copy-start(bf16[720,640]{1,0:T(8,128)(2,1)} %copy-done.15) | copy-start | bytes 2764804
  55.8 19.4 %copy-start.7 = (bf16[720,640]{1,0:T(8,128)(2,1)S(1)}, bf16[720,640]{1,0:T(8,128)(2,1)}, u32[]{:S(2)}) copy-start(bf16[720,640]{1,0:T(8,128)(2,1)} %get-tuple-element.248.g0p) | copy-start | bytes 2764804
  55.8 19.4 %copy-start.8 = (bf16[720,640]{1,0:T(8,128)(2,1)S(1)}, bf16[720,640]{1,0:T(8,128)(2,1)}, u32[]{:S(2)}) copy-start(bf16[720,640]{1,0:T(8,128)(2,1)} %get-tuple-element.250.g0m) | copy-start | bytes 2764804
  55.8 29.0 %collective-permute-start.16 = (bf16[720,640]{1,0:T(8,128)(2,1)}, bf16[720,640]{1,0:T(8,128)(2,1)S(1)}, u32[]{:S(2)}, u32[]{:S(2)}) collective-permute-start(bf16[720,640]{1,0:T(8,128)(2,1)} %get-tuple-element.241), channel_id=1, source_target_pairs={{0,4},{1,5},{2,6},{3,7},{4,0},{5,1},{6,2},{7,3},{8,12},{9,13},{10,... | collective-permute-start | bytes 2764808 | tf_op jit(solution)/shard_map/ppermute | solution.py:28
  57.4 17.8 %collective-permute-start.18 = (bf16[368,640]{1,0:T(8,128)(2,1)}, bf16[368,640]{1,0:T(8,128)(2,1)}, u32[]{:S(2)}, u32[]{:S(2)}) collective-permute-start(bf16[368,640]{1,0:T(8,128)(2,1)} %get-tuple-element.243), channel_id=1, source_target_pairs={{0,3},{1,0},{2,1},{3,2},{4,7},{5,4},{6,5},{7,6},{8,11},{9,8},{10,9... | collective-permute-start | bytes 1413128 | tf_op jit(solution)/shard_map/ppermute | solution.py:28
  60.4 24.5 %collective-permute-start.15 = (bf16[368,640]{1,0:T(8,128)(2,1)}, bf16[368,640]{1,0:T(8,128)(2,1)S(1)}, u32[]{:S(2)}, u32[]{:S(2)}) collective-permute-start(bf16[368,640]{1,0:T(8,128)(2,1)} %get-tuple-element.240), channel_id=1, source_target_pairs={{0,3},{1,0},{2,1},{3,2},{4,7},{5,4},{6,5},{7,6},{8,11},{9,8},{10,9... | collective-permute-start | bytes 1413128 | tf_op jit(solution)/shard_map/ppermute | solution.py:28
  60.4 14.8 %collective-permute-start.17 = (bf16[352,640]{1,0:T(8,128)(2,1)}, bf16[352,640]{1,0:T(8,128)(2,1)}, u32[]{:S(2)}, u32[]{:S(2)}) collective-permute-start(bf16[352,640]{1,0:T(8,128)(2,1)} %get-tuple-element.242), channel_id=1, source_target_pairs={{0,1},{1,2},{2,3},{3,0},{4,5},{5,6},{6,7},{7,4},{8,9},{9,10},{10,1... | collective-permute-start | bytes 1351688 | tf_op jit(solution)/shard_map/ppermute | solution.py:28
  62.4 22.5 %collective-permute-start.14 = (bf16[352,640]{1,0:T(8,128)(2,1)}, bf16[352,640]{1,0:T(8,128)(2,1)}, u32[]{:S(2)}, u32[]{:S(2)}) collective-permute-start(bf16[352,640]{1,0:T(8,128)(2,1)} %get-tuple-element.239), channel_id=1, source_target_pairs={{0,1},{1,2},{2,3},{3,0},{4,5},{5,6},{6,7},{7,4},{8,9},{9,10},{10,1... | collective-permute-start | bytes 1351688 | tf_op jit(solution)/shard_map/ppermute | solution.py:28
  77.8 31.2 %collective-permute-start.21 = (bf16[720,640]{1,0:T(8,128)(2,1)}, bf16[720,640]{1,0:T(8,128)(2,1)}, u32[]{:S(2)}, u32[]{:S(2)}) collective-permute-start(bf16[720,640]{1,0:T(8,128)(2,1)} %get-tuple-element.251), channel_id=1, source_target_pairs={{0,1},{1,2},{2,3},{3,0},{4,5},{5,6},{6,7},{7,4},{8,9},{9,10},{10,1... | collective-permute-start | bytes 2764808 | tf_op jit(solution)/shard_map/ppermute | solution.py:28
  78.6 30.4 %collective-permute-start.22 = (bf16[720,640]{1,0:T(8,128)(2,1)}, bf16[720,640]{1,0:T(8,128)(2,1)}, u32[]{:S(2)}, u32[]{:S(2)}) collective-permute-start(bf16[720,640]{1,0:T(8,128)(2,1)} %get-tuple-element.252), channel_id=1, source_target_pairs={{0,3},{1,0},{2,1},{3,2},{4,7},{5,4},{6,5},{7,6},{8,11},{9,8},{10,9... | collective-permute-start | bytes 2764808 | tf_op jit(solution)/shard_map/ppermute | solution.py:28
  87.2 26.9 %collective-permute-start.23 = (bf16[720,640]{1,0:T(8,128)(2,1)}, bf16[720,640]{1,0:T(8,128)(2,1)}, u32[]{:S(2)}, u32[]{:S(2)}) collective-permute-start(bf16[720,640]{1,0:T(8,128)(2,1)} %join.1), channel_id=1, source_target_pairs={{0,4},{1,5},{2,6},{3,7},{4,0},{5,1},{6,2},{7,3},{8,12},{9,13},{10,... | collective-permute-start | bytes 2764808 | tf_op jit(solution)/shard_map/ppermute | solution.py:28
  87.7 21.3 %copy-start.1 = (f32[1,720,640]{2,1,0:T(8,128)S(1)}, f32[1,720,640]{2,1,0:T(8,128)}, u32[]{:S(2)}) copy-start(f32[1,720,640]{2,1,0:T(8,128)} %param.20) | copy-start | bytes 5529604
  87.7 21.3 %copy-start.2 = (bf16[720,640]{1,0:T(8,128)(2,1)S(1)}, bf16[720,640]{1,0:T(8,128)(2,1)}, u32[]{:S(2)}) copy-start(bf16[720,640]{1,0:T(8,128)(2,1)} %get-tuple-element.258.g00) | copy-start | bytes 2764804
  87.7 19.1 %collective-permute-start.2 = (bf16[720,640]{1,0:T(8,128)(2,1)}, bf16[720,640]{1,0:T(8,128)(2,1)}, u32[]{:S(2)}, u32[]{:S(2)}) collective-permute-start(bf16[720,640]{1,0:T(8,128)(2,1)} %get-tuple-element.124), channel_id=1, source_target_pairs={{0,100},{1,101},{2,102},{3,103},{4,96},{5,97},{6,98},{7,99},{8,108... | collective-permute-start | bytes 2764808 | tf_op jit(solution)/shard_map/cond/branch_2_fun/ppermute | solution.py:47
  106.8 26.6 %collective-permute-start.20 = (bf16[720,640]{1,0:T(8,128)(2,1)}, bf16[720,640]{1,0:T(8,128)(2,1)}, u32[]{:S(2)}, u32[]{:S(2)}) collective-permute-start(bf16[720,640]{1,0:T(8,128)(2,1)} %copy-done.17), channel_id=1, source_target_pairs={{0,3},{1,0},{2,1},{3,2},{4,7},{5,4},{6,5},{7,6},{8,11},{9,8},{10,9... | collective-permute-start | bytes 2764808 | tf_op jit(solution)/shard_map/ppermute | solution.py:28
  107.7 25.7 %collective-permute-start.19 = (bf16[720,640]{1,0:T(8,128)(2,1)}, bf16[720,640]{1,0:T(8,128)(2,1)}, u32[]{:S(2)}, u32[]{:S(2)}) collective-permute-start(bf16[720,640]{1,0:T(8,128)(2,1)} %copy-done.17), channel_id=1, source_target_pairs={{0,1},{1,2},{2,3},{3,0},{4,5},{5,6},{6,7},{7,4},{8,9},{9,10},{10,1... | collective-permute-start | bytes 2764808 | tf_op jit(solution)/shard_map/ppermute | solution.py:28
  114.1 15.2 %collective-permute-start.6 = (bf16[720,640]{1,0:T(8,128)(2,1)}, bf16[720,640]{1,0:T(8,128)(2,1)S(1)}, u32[]{:S(2)}, u32[]{:S(2)}) collective-permute-start(bf16[720,640]{1,0:T(8,128)(2,1)} %get-tuple-element.155), channel_id=1, source_target_pairs={{0,96},{8,104},{16,112},{24,120},{32,0},{40,8},{48,16},{56,24},{64... | collective-permute-start | bytes 2764808 | tf_op jit(solution)/shard_map/cond/branch_2_fun/ppermute | solution.py:32
  116.8 12.5 %copy-start.11 = (f32[720,640]{1,0:T(8,128)S(1)}, f32[720,640]{1,0:T(8,128)}, u32[]{:S(2)}) copy-start(f32[720,640]{1,0:T(8,128)} %get-tuple-element.152) | copy-start | bytes 5529604 | tf_op jit(solution)/shard_map/cond
  (3 other events, 4.9 us)

commit v4 on v3

--- a/solution.py
+++ b/solution.py
@@ -191,9 +191,9 @@
     pltpu.VMEM((5 * CHANS, CHANS), jnp.bfloat16),
     pltpu.SemaphoreType.DMA((4,)),
 ]
-TILE = 6
+TILE = 8
 WINDOW = 7 * 128
-CHUNK = 128
+CHUNK = 256
 SHORT = pl.CostEstimate(flops=10**6, bytes_accessed=10**5, transcendentals=0)
 IN_VMEM = pl.BlockSpec(memory_space=pltpu.VMEM)
 IN_ANY = pl.BlockSpec(memory_space=pl.ANY)

time: 143 us -> 140 us (0.979)
  starting transfers between devices: 30.1 us -> 25.6 us
  waiting for transfers between devices: 22.3 us -> 24.7 us
    ppermute x1, starting transfers between devices: 5.54 us -> 3.01 us  [weight_from_partner(): return lax.ppermute(value, ('group', 'inner'), pairs)]
    ppermute x1, waiting for transfers between devices: 3.42 us -> 5.41 us  [from_partner(): return lax.ppermute(value, 'group', [(i, (i - by) % 16) for i in range(16)])]
    ppermute x1, starting transfers between devices: 2.69 us -> 0.73 us  [from_partner(): return lax.ppermute(value, 'group', [(i, (i - by) % 16) for i in range(16)])]
  transfers between devices with their start and end apart: 18 -> 18, of which waited for: 6 -> 6; matrix products, arithmetic and copies ran while one was open for 5% -> 5% of each run, Pallas kernels for 47% -> 48%
where the time goes in v4:
time: 140 us
  Pallas kernels  77 us (55%)
  starting transfers between devices  25.6 us (18%)
  waiting for transfers between devices  24.7 us (18%)
  other arithmetic  8.52 us (6%)
  local copies, waits for them, and re-layouts  2.19 us (2%)
  between operations  1.72 us (1%)
    pallas_call x3, Pallas kernels, conv(): pl.pallas_call(partial(conv_kernel, places, len(others), tall), out_shape...  31.4 us
    ppermute x16, starting transfers between devices, send_inner(): return lax.ppermute(value, 'inner', [(i, place(i)) for i in range(8)])  21.8 us
    ppermute x16, waiting for transfers between devices, send_inner(): return lax.ppermute(value, 'inner', [(i, place(i)) for i in range(8)])  19.3 us
    pallas_call x1, Pallas kernels, norm_grad(): pl.pallas_call(norm_grad_kernel, out_shape=[jax.ShapeDtypeStruct((PIXELS,...  17.8 us
    pallas_call x1, Pallas kernels, rest_grad(): pl.pallas_call(rest_grad_kernel, out_shape=[jax.ShapeDtypeStruct((ROWS, C...  13.5 us
    pallas_call x3, Pallas kernels, small(): pl.pallas_call(kernel, out_shape=[jax.ShapeDtypeStruct((count, CHANS), jn...  6.59 us
    ppermute x1, waiting for transfers between devices, from_partner(): return lax.ppermute(value, 'group', [(i, (i - by) % 16) for i in range(16)])  5.41 us
    mul x1, other arithmetic, finish(): new_moment = 0.5 * both  4.09 us
  transfers between devices with their start and end apart: 18, of which 6 were waited for; matrix products, arithmetic and copies ran while one was open for 5% of the time, Pallas kernels for 48%

profile of v4, /device:TPU:0, one launch (start us, length us, event | category | flops | bytes accessed | tf_op | source)
XLA Modules:
  0.0 140.0 jit_solution(15941079301484792773)
XLA Ops:
  0.7 1.6 %bitcast_convert_fusion = bf16[720,640]{1,0:T(8,128)(2,1)S(1)} fusion(f32[1,720,640]{2,1,0:T(8,128)} %param.19), kind=kLoop, calls=%fused_computation.14 | loop fusion | flops 460800 | bytes 2764800 | tf_op jit(solution)/shard_map/convert_element_type | solution.py:431
  2.3 1.7 %collective-permute-start.10 = (bf16[720,640]{1,0:T(8,128)(2,1)S(1)}, bf16[720,640]{1,0:T(8,128)(2,1)S(1)}, u32[]{:S(2)}, u32[]{:S(2)}) collective-permute-start(bf16[720,640]{1,0:T(8,128)(2,1)S(1)} %bitcast_convert_fusion), channel_id=1, source_target_pairs={{0,4},{1,5},{2,6},{3,7},{4,0},{5,1},{6,2},{7,3},{8,12},{9,13},{10,... | collective-permute-start | bytes 2764808 | tf_op jit(solution)/shard_map/ppermute | solution.py:28
  4.0 4.0 %collective-permute-start.9 = (bf16[720,640]{1,0:T(8,128)(2,1)S(1)}, bf16[720,640]{1,0:T(8,128)(2,1)S(1)}, u32[]{:S(2)}, u32[]{:S(2)}) collective-permute-start(bf16[720,640]{1,0:T(8,128)(2,1)S(1)} %bitcast_convert_fusion), channel_id=1, source_target_pairs={{0,3},{1,0},{2,1},{3,2},{4,7},{5,4},{6,5},{7,6},{8,11},{9,8},{10,9... | collective-permute-start | bytes 2764808 | tf_op jit(solution)/shard_map/ppermute | solution.py:28
  8.7 17.8 %norm_grad.1 = (bf16[1536,640]{1,0:T(8,128)(2,1)}, bf16[640,1536]{1,0:T(8,128)(2,1)}, bf16[720,640]{1,0:T(8,128)(2,1)}, bf16[720,640]{1,0:T(8,128)(2,1)}, bf16[7...) custom-call(bf16[1536,640]{1,0:T(8,128)(2,1)} %bitcast.19, bf16[1536,640]{1,0:T(8,128)(2,1)} %bitcast.17, ...), custom_call_target="tpu_custom_call" | custom-call | flops 1000000 | bytes 100000 | tf_op jit(solution)/shard_map/norm_grad/pallas_call | solution.py:203
  26.5 1.0 collective-permute-done.9.w_p
  27.5 3.4 %collective-permute-done.8.w_m = bf16[720,640]{1,0:T(8,128)(2,1)S(1)} collective-permute-done((bf16[720,640]{1,0:T(8,128)(2,1)S(1)}, bf16[720,640]{1,0:T(8,128)(2,1)S(1)}, u32[]{:S(2)}, u32[]{:S(2)}) %collective-permute-start.8) | collective-permute-done | bytes 921632 | tf_op jit(solution)/shard_map/ppermute | solution.py:28
  30.9 0.9 copy-done.15
  32.3 3.2 %collective-permute-start.13 = (bf16[720,640]{1,0:T(8,128)(2,1)}, bf16[720,640]{1,0:T(8,128)(2,1)S(1)}, u32[]{:S(2)}, u32[]{:S(2)}) collective-permute-start(bf16[720,640]{1,0:T(8,128)(2,1)} %get-tuple-element.227), channel_id=1, source_target_pairs={{0,3},{1,0},{2,1},{3,2},{4,7},{5,4},{6,5},{7,6},{8,11},{9,8},{10,9... | collective-permute-start | bytes 2764808 | tf_op jit(solution)/shard_map/ppermute | solution.py:28
  35.5 13.5 %rest_grad.1 = (bf16[720,640]{1,0:T(8,128)(2,1)}, bf16[720,640]{1,0:T(8,128)(2,1)}, bf16[720,640]{1,0:T(8,128)(2,1)}, bf16[720,640]{1,0:T(8,128)(2,1)}) custom-call(bf16[640,1536]{1,0:T(8,128)(2,1)} %get-tuple-element.229.turned, bf16[1536,640]{1,0:T(8,128)(2,1)} %bitcast.18), custom_call_target="tpu_custom_call" | custom-call | flops 1000000 | bytes 100000 | tf_op jit(solution)/shard_map/rest_grad/pallas_call | solution.py:222
  49.1 3.8 %spread.1.refs_0_ = bf16[1600,1920]{1,0:T(8,128)(2,1)} custom-call(bf16[1536,640]{1,0:T(8,128)(2,1)S(1)} %copy-done), custom_call_target="tpu_custom_call" | custom-call | flops 1000000 | bytes 100000 | tf_op jit(solution)/shard_map/spread/pallas_call | solution.py:235
  52.9 1.2 collective-permute-done.12.a_p
  54.2 1.7 %sums.1 = (bf16[352,640]{1,0:T(8,128)(2,1)}, bf16[368,640]{1,0:T(8,128)(2,1)}, bf16[720,640]{1,0:T(8,128)(2,1)}, bf16[352,640]{1,0:T(8,128)(2,1)}, bf16[368,640]{1,0:T(8,128)(2,1)}) custom-call(bf16[720,640]{1,0:T(8,128)(2,1)S(1)} %collective-permute-done.11.a_y, bf16[720,640]{1,0:T(8,128)(2,1)S(1)} %copy-done.6, ...), custom_call_target="tpu_custom_call" | custom-call | flops 1000000 | bytes 100000 | tf_op jit(solution)/shard_map/sums/pallas_call | solution.py:387
  55.8 1.6 %collective-permute-start.16 = (bf16[720,640]{1,0:T(8,128)(2,1)}, bf16[720,640]{1,0:T(8,128)(2,1)S(1)}, u32[]{:S(2)}, u32[]{:S(2)}) collective-permute-start(bf16[720,640]{1,0:T(8,128)(2,1)} %get-tuple-element.241), channel_id=1, source_target_pairs={{0,4},{1,5},{2,6},{3,7},{4,0},{5,1},{6,2},{7,3},{8,12},{9,13},{10,... | collective-permute-start | bytes 2764808 | tf_op jit(solution)/shard_map/ppermute | solution.py:28
  57.4 2.9 %collective-permute-start.18 = (bf16[368,640]{1,0:T(8,128)(2,1)}, bf16[368,640]{1,0:T(8,128)(2,1)}, u32[]{:S(2)}, u32[]{:S(2)}) collective-permute-start(bf16[368,640]{1,0:T(8,128)(2,1)} %get-tuple-element.243), channel_id=1, source_target_pairs={{0,3},{1,0},{2,1},{3,2},{4,7},{5,4},{6,5},{7,6},{8,11},{9,8},{10,9... | collective-permute-start | bytes 1413128 | tf_op jit(solution)/shard_map/ppermute | solution.py:28
  60.4 2.0 %collective-permute-start.17 = (bf16[352,640]{1,0:T(8,128)(2,1)}, bf16[352,640]{1,0:T(8,128)(2,1)}, u32[]{:S(2)}, u32[]{:S(2)}) collective-permute-start(bf16[352,640]{1,0:T(8,128)(2,1)} %get-tuple-element.242), channel_id=1, source_target_pairs={{0,1},{1,2},{2,3},{3,0},{4,5},{5,6},{6,7},{7,4},{8,9},{9,10},{10,1... | collective-permute-start | bytes 1351688 | tf_op jit(solution)/shard_map/ppermute | solution.py:28
  63.1 2.2 %broadcast_select_fusion = bf16[720,640]{1,0:T(8,128)(2,1)} fusion(bf16[720,640]{1,0:T(8,128)(2,1)} %copy-done.17, bf16[720,640]{1,0:T(8,128)(2,1)} %copy-done.13, pred[]{:T(512)S(6)} %ne.37), kind=kLoop, calls=%fused_computation.12 | loop fusion | flops 460800 | bytes 2764801 | tf_op jit(solution)/shard_map/jit(_where)/select_n | solution.py:38
  65.4 9.9 %collective-permute-done.17.b_up = bf16[352,640]{1,0:T(8,128)(2,1)} collective-permute-done((bf16[352,640]{1,0:T(8,128)(2,1)}, bf16[352,640]{1,0:T(8,128)(2,1)}, u32[]{:S(2)}, u32[]{:S(2)}) %collective-permute-start.17) | collective-permute-done | bytes 450592 | tf_op jit(solution)/shard_map/ppermute | solution.py:28
  75.2 2.6 %ends.1 = (bf16[720,640]{1,0:T(8,128)(2,1)}, bf16[720,640]{1,0:T(8,128)(2,1)}) custom-call(bf16[352,640]{1,0:T(8,128)(2,1)} %collective-permute-done.17.b_up, bf16[720,640]{1,0:T(8,128)(2,1)S(1)} %copy-done.7, bf16[368,640]{1,0:T(8,128)(2,1)} %collective-permute-done.18.b_dn, bf16[720,640]{1,0:T(8,128)(2,1)S(1)} %copy-done.8), custom_call_target="tpu_custom_call" | custom-call | flops 1000000 | bytes 100000 | tf_op jit(solution)/shard_map/ends/pallas_call | solution.py:387
  78.6 2.5 %collective-permute-start.22 = (bf16[720,640]{1,0:T(8,128)(2,1)}, bf16[720,640]{1,0:T(8,128)(2,1)}, u32[]{:S(2)}, u32[]{:S(2)}) collective-permute-start(bf16[720,640]{1,0:T(8,128)(2,1)} %get-tuple-element.252), channel_id=1, source_target_pairs={{0,3},{1,0},{2,1},{3,2},{4,7},{5,4},{6,5},{7,6},{8,11},{9,8},{10,9... | collective-permute-start | bytes 2764808 | tf_op jit(solution)/shard_map/ppermute | solution.py:28
  81.0 3.9 %collective-permute-done.14.top = bf16[352,640]{1,0:T(8,128)(2,1)} collective-permute-done((bf16[352,640]{1,0:T(8,128)(2,1)}, bf16[352,640]{1,0:T(8,128)(2,1)}, u32[]{:S(2)}, u32[]{:S(2)}) %collective-permute-start.14) | collective-permute-done | bytes 450592 | tf_op jit(solution)/shard_map/ppermute | solution.py:28
  84.9 2.4 %join.1 = bf16[720,640]{1,0:T(8,128)(2,1)} custom-call(bf16[352,640]{1,0:T(8,128)(2,1)} %collective-permute-done.14.top, bf16[368,640]{1,0:T(8,128)(2,1)S(1)} %collective-permute-done.15.bottom), custom_call_target="tpu_custom_call" | custom-call | flops 1000000 | bytes 100000 | tf_op jit(solution)/shard_map/join/pallas_call | solution.py:387
  87.7 16.6 %conditional.2 = (bf16[720,640]{1,0:T(8,128)(2,1)}, bf16[1536,640]{1,0:T(8,128)(2,1)S(1)}) conditional(s32[]{:T(128)} %clamp.4, (bf16[720,640]{1,0:T(8,128)(2,1)}, bf16[1600,1920]{1,0:T(8,128)(2,1)}, bf16[720,640]{1,0:T(8,128)(2,1)}, bf16[720,640]{1,0:T(8,128)(2,1)}, bf16[720,640]{1,0:T(8,128)(2,1)}, ...), branch_computations={%region_0.1_spmd, %region_1.2_spmd, %region_2.3_spmd, %region_3.4_... | conditional | flops 1000000 | bytes 3786456 | solution.py:352
  87.7 3.0 %collective-permute-start.3 = (bf16[720,640]{1,0:T(8,128)(2,1)}, bf16[720,640]{1,0:T(8,128)(2,1)}, u32[]{:S(2)}, u32[]{:S(2)}) collective-permute-start(bf16[720,640]{1,0:T(8,128)(2,1)} %get-tuple-element.130), channel_id=1, source_target_pairs={{0,68},{1,69},{2,70},{3,71},{4,64},{5,65},{6,66},{7,67},{8,76},{9,... | collective-permute-start | bytes 2764808 | tf_op jit(solution)/shard_map/cond/branch_3_fun/ppermute | solution.py:47
  90.7 13.6 %conv.12 = bf16[1536,640]{1,0:T(8,128)(2,1)S(1)} custom-call(bf16[1600,1920]{1,0:T(8,128)(2,1)} %get-tuple-element.131.refs_0_, bf16[720,640]{1,0:T(8,128)(2,1)} %get-tuple-element.132.refs_1_, bf16[720,640]{1,0:T(8,128)(2,1)} %get-tuple-element.133.refs_2_, bf16[720,640]{1,0:T(8,128)(2,1)} %get-tuple-element.134.refs_3_, ...), custom_call_target="tpu_custom_call" | custom-call | flops 1000000 | bytes 100000 | tf_op jit(solution)/shard_map/cond/branch_3_fun/conv/pallas_call | solution.py:326
  105.2 1.2 collective-permute-start.19
  106.4 1.2 copy-done.4
  107.6 4.0 %moved.1 = (f32[720,640]{1,0:T(8,128)}, bf16[720,640]{1,0:T(8,128)(2,1)}) custom-call(f32[720,640]{1,0:T(8,128)S(1)} %bitcast.12, bf16[720,640]{1,0:T(8,128)(2,1)S(1)} %copy-done.2, bf16[720,640]{1,0:T(8,128)(2,1)S(1)} %copy-done.4, bf16[720,640]{1,0:T(8,128)(2,1)} %collective-permute-done.21.c_up, bf16[720,640]{1,0:T(8,128)(2,1)} %collective-permute-done.22.c_dn), custom_call_target="tpu_custom_call" | custom-call | flops 1000000 | bytes 100000 | tf_op jit(solution)/shard_map/moved/pallas_call | solution.py:407
  111.6 19.5 %conditional.3 = (f32[720,640]{1,0:T(8,128)}, f32[720,640]{1,0:T(8,128)}, bf16[1536,640]{1,0:T(8,128)(2,1)}) conditional(s32[]{:T(128)} %clamp.4, (bf16[720,640]{1,0:T(8,128)(2,1)}, f32[720,640]{1,0:T(8,128)}, bf16[720,640]{1,0:T(8,128)(2,1)}, f32[720,640]{1,0:T(8,128)}, bf16[1600,1920]{1,0:T(8,128)(2,1)}, ...), branch_computations={%region_4.5_spmd, %region_5.6_spmd, %region_6.7_spmd, %region_7.8_... | conditional | flops 4686400 | bytes 20375292 | solution.py:352
  112.5 9.1 %conv.16 = bf16[1536,640]{1,0:T(8,128)(2,1)} custom-call(bf16[1600,1920]{1,0:T(8,128)(2,1)} %get-tuple-element.164.refs_0_, bf16[720,640]{1,0:T(8,128)(2,1)} %get-tuple-element.165.refs_1_, bf16[720,640]{1,0:T(8,128)(2,1)} %get-tuple-element.166.refs_2_, bf16[1536,640]{1,0:T(8,128)(2,1)S(1)} %get-tuple-element.167.refs_3_), custom_call_target="tpu_custom_call" | custom-call | flops 1000000 | bytes 100000 | tf_op jit(solution)/shard_map/cond/branch_3_fun/conv/pallas_call | solution.py:326
  121.6 5.4 %collective-permute-done.7 = bf16[720,640]{1,0:T(8,128)(2,1)S(1)} collective-permute-done((bf16[720,640]{1,0:T(8,128)(2,1)}, bf16[720,640]{1,0:T(8,128)(2,1)S(1)}, u32[]{:S(2)}, u32[]{:S(2)}) %collective-permute-start.7) | collective-permute-done | bytes 921632 | tf_op jit(solution)/shard_map/cond/branch_3_fun/ppermute | solution.py:32
  127.0 4.1 %fusion.3 = (f32[720,640]{1,0:T(8,128)}, f32[720,640]{1,0:T(8,128)}) fusion(f32[720,640]{1,0:T(8,128)} %get-tuple-element.162, bf16[720,640]{1,0:T(8,128)(2,1)S(1)} %collective-permute-done.7, f32[720,640]{1,0:T(8,128)S(1)} %copy-done.12, bf16[720,640]{1,0:T(8,128)(2,1)} %get-tuple-element.161), kind=kLoop, calls=%fused_computation.11 | loop fusion | flops 3686400 | bytes 9216000 | tf_op jit(solution)/shard_map/cond/branch_3_fun/mul | solution.py:422
  131.1 8.7 %conv.17 = bf16[1536,640]{1,0:T(8,128)(2,1)} custom-call(bf16[1600,1920]{1,0:T(8,128)(2,1)} %spread.1.refs_0_, bf16[720,640]{1,0:T(8,128)(2,1)} %collective-permute-done.19.refs_1_, bf16[720,640]{1,0:T(8,128)(2,1)} %collective-permute-done.20.refs_2_, bf16[1536,640]{1,0:T(8,128)(2,1)} %get-tuple-element.268.refs_3_, bf16[1536,640]{1,0:T(8,128)(2,1)} %bitcast.20), custom_call_target="tpu_custom_call" | custom-call | flops 1000000 | bytes 100000 | tf_op jit(solution)/shard_map/conv/pallas_call | solution.py:326
  (56 shorter events, 4.0 us)
Async XLA Ops:
  0.6 7.4 %copy-start.18 = (f32[640]{0:T(1024)S(1)}, f32[640]{0:T(1024)}, u32[]{:S(2)}) copy-start(f32[640]{0:T(1024)} %param.17) | copy-start | bytes 7684
  0.6 7.4 %copy-start.19 = (f32[640]{0:T(1024)S(1)}, f32[640]{0:T(1024)}, u32[]{:S(2)}) copy-start(f32[640]{0:T(1024)} %param.18) | copy-start | bytes 7684
  2.3 28.6 %copy-start.13 = (bf16[720,640]{1,0:T(8,128)(2,1)}, bf16[720,640]{1,0:T(8,128)(2,1)S(1)}, u32[]{:S(2)}) copy-start(bf16[720,640]{1,0:T(8,128)(2,1)S(1)} %bitcast_convert_fusion) | copy-start | bytes 2764804
  2.3 24.2 %collective-permute-start.10 = (bf16[720,640]{1,0:T(8,128)(2,1)S(1)}, bf16[720,640]{1,0:T(8,128)(2,1)S(1)}, u32[]{:S(2)}, u32[]{:S(2)}) collective-permute-start(bf16[720,640]{1,0:T(8,128)(2,1)S(1)} %bitcast_convert_fusion), channel_id=1, source_target_pairs={{0,4},{1,5},{2,6},{3,7},{4,0},{5,1},{6,2},{7,3},{8,12},{9,13},{10,... | collective-permute-start | bytes 2764808 | tf_op jit(solution)/shard_map/ppermute | solution.py:28
  4.0 23.5 %collective-permute-start.9 = (bf16[720,640]{1,0:T(8,128)(2,1)S(1)}, bf16[720,640]{1,0:T(8,128)(2,1)S(1)}, u32[]{:S(2)}, u32[]{:S(2)}) collective-permute-start(bf16[720,640]{1,0:T(8,128)(2,1)S(1)} %bitcast_convert_fusion), channel_id=1, source_target_pairs={{0,3},{1,0},{2,1},{3,2},{4,7},{5,4},{6,5},{7,6},{8,11},{9,8},{10,9... | collective-permute-start | bytes 2764808 | tf_op jit(solution)/shard_map/ppermute | solution.py:28
  8.1 22.8 %collective-permute-start.8 = (bf16[720,640]{1,0:T(8,128)(2,1)S(1)}, bf16[720,640]{1,0:T(8,128)(2,1)S(1)}, u32[]{:S(2)}, u32[]{:S(2)}) collective-permute-start(bf16[720,640]{1,0:T(8,128)(2,1)S(1)} %bitcast_convert_fusion), channel_id=1, source_target_pairs={{0,1},{1,2},{2,3},{3,0},{4,5},{5,6},{6,7},{7,4},{8,9},{9,10},{10,1... | collective-permute-start | bytes 2764808 | tf_op jit(solution)/shard_map/ppermute | solution.py:28
  26.5 5.8 %copy-start.17 = (bf16[720,640]{1,0:T(8,128)(2,1)}, bf16[720,640]{1,0:T(8,128)(2,1)S(1)}, u32[]{:S(2)}) copy-start(bf16[720,640]{1,0:T(8,128)(2,1)S(1)} %collective-permute-done.10) | copy-start | bytes 2764804
  27.5 26.7 %copy-start.14 = (bf16[720,640]{1,0:T(8,128)(2,1)}, bf16[720,640]{1,0:T(8,128)(2,1)S(1)}, u32[]{:S(2)}) copy-start(bf16[720,640]{1,0:T(8,128)(2,1)S(1)} %collective-permute-done.9.w_p) | copy-start | bytes 2764804
  31.8 21.1 %collective-permute-start.11 = (bf16[720,640]{1,0:T(8,128)(2,1)}, bf16[720,640]{1,0:T(8,128)(2,1)S(1)}, u32[]{:S(2)}, u32[]{:S(2)}) collective-permute-start(bf16[720,640]{1,0:T(8,128)(2,1)} %get-tuple-element.225), channel_id=1, source_target_pairs={{0,4},{1,5},{2,6},{3,7},{4,0},{5,1},{6,2},{7,3},{8,12},{9,13},{10,... | collective-permute-start | bytes 2764808 | tf_op jit(solution)/shard_map/ppermute | solution.py:28
  32.3 21.8 %collective-permute-start.12 = (bf16[720,640]{1,0:T(8,128)(2,1)}, bf16[720,640]{1,0:T(8,128)(2,1)S(1)}, u32[]{:S(2)}, u32[]{:S(2)}) collective-permute-start(bf16[720,640]{1,0:T(8,128)(2,1)} %get-tuple-element.226), channel_id=1, source_target_pairs={{0,1},{1,2},{2,3},{3,0},{4,5},{5,6},{6,7},{7,4},{8,9},{9,10},{10,1... | collective-permute-start | bytes 2764808 | tf_op jit(solution)/shard_map/ppermute | solution.py:28
  32.3 21.8 %collective-permute-start.13 = (bf16[720,640]{1,0:T(8,128)(2,1)}, bf16[720,640]{1,0:T(8,128)(2,1)S(1)}, u32[]{:S(2)}, u32[]{:S(2)}) collective-permute-start(bf16[720,640]{1,0:T(8,128)(2,1)} %get-tuple-element.227), channel_id=1, source_target_pairs={{0,3},{1,0},{2,1},{3,2},{4,7},{5,4},{6,5},{7,6},{8,11},{9,8},{10,9... | collective-permute-start | bytes 2764808 | tf_op jit(solution)/shard_map/ppermute | solution.py:28
  35.5 13.5 %copy-start = (bf16[1536,640]{1,0:T(8,128)(2,1)S(1)}, bf16[1536,640]{1,0:T(8,128)(2,1)}, u32[]{:S(2)}) copy-start(bf16[1536,640]{1,0:T(8,128)(2,1)} %get-tuple-element.231.hidden) | copy-start | bytes 5898244
  49.1 5.1 %copy-start.5 = (bf16[720,640]{1,0:T(8,128)(2,1)S(1)}, bf16[720,640]{1,0:T(8,128)(2,1)}, u32[]{:S(2)}) copy-start(bf16[720,640]{1,0:T(8,128)(2,1)} %get-tuple-element.236.g10) | copy-start | bytes 2764804
  49.1 5.1 %copy-start.6 = (bf16[720,640]{1,0:T(8,128)(2,1)S(1)}, bf16[720,640]{1,0:T(8,128)(2,1)}, u32[]{:S(2)}) copy-start(bf16[720,640]{1,0:T(8,128)(2,1)} %get-tuple-element.230.g02) | copy-start | bytes 2764804
  49.1 5.1 %copy-start.16 = (bf16[720,640]{1,0:T(8,128)(2,1)S(1)}, bf16[720,640]{1,0:T(8,128)(2,1)}, u32[]{:S(2)}) copy-start(bf16[720,640]{1,0:T(8,128)(2,1)} %copy-done.15) | copy-start | bytes 2764804
  55.8 19.4 %copy-start.7 = (bf16[720,640]{1,0:T(8,128)(2,1)S(1)}, bf16[720,640]{1,0:T(8,128)(2,1)}, u32[]{:S(2)}) copy-start(bf16[720,640]{1,0:T(8,128)(2,1)} %get-tuple-element.248.g0p) | copy-start | bytes 2764804
  55.8 19.4 %copy-start.8 = (bf16[720,640]{1,0:T(8,128)(2,1)S(1)}, bf16[720,640]{1,0:T(8,128)(2,1)}, u32[]{:S(2)}) copy-start(bf16[720,640]{1,0:T(8,128)(2,1)} %get-tuple-element.250.g0m) | copy-start | bytes 2764804
  55.8 29.0 %collective-permute-start.16 = (bf16[720,640]{1,0:T(8,128)(2,1)}, bf16[720,640]{1,0:T(8,128)(2,1)S(1)}, u32[]{:S(2)}, u32[]{:S(2)}) collective-permute-start(bf16[720,640]{1,0:T(8,128)(2,1)} %get-tuple-element.241), channel_id=1, source_target_pairs={{0,4},{1,5},{2,6},{3,7},{4,0},{5,1},{6,2},{7,3},{8,12},{9,13},{10,... | collective-permute-start | bytes 2764808 | tf_op jit(solution)/shard_map/ppermute | solution.py:28
  57.4 17.8 %collective-permute-start.18 = (bf16[368,640]{1,0:T(8,128)(2,1)}, bf16[368,640]{1,0:T(8,128)(2,1)}, u32[]{:S(2)}, u32[]{:S(2)}) collective-permute-start(bf16[368,640]{1,0:T(8,128)(2,1)} %get-tuple-element.243), channel_id=1, source_target_pairs={{0,3},{1,0},{2,1},{3,2},{4,7},{5,4},{6,5},{7,6},{8,11},{9,8},{10,9... | collective-permute-start | bytes 1413128 | tf_op jit(solution)/shard_map/ppermute | solution.py:28
  60.4 24.5 %collective-permute-start.15 = (bf16[368,640]{1,0:T(8,128)(2,1)}, bf16[368,640]{1,0:T(8,128)(2,1)S(1)}, u32[]{:S(2)}, u32[]{:S(2)}) collective-permute-start(bf16[368,640]{1,0:T(8,128)(2,1)} %get-tuple-element.240), channel_id=1, source_target_pairs={{0,3},{1,0},{2,1},{3,2},{4,7},{5,4},{6,5},{7,6},{8,11},{9,8},{10,9... | collective-permute-start | bytes 1413128 | tf_op jit(solution)/shard_map/ppermute | solution.py:28
  60.4 14.8 %collective-permute-start.17 = (bf16[352,640]{1,0:T(8,128)(2,1)}, bf16[352,640]{1,0:T(8,128)(2,1)}, u32[]{:S(2)}, u32[]{:S(2)}) collective-permute-start(bf16[352,640]{1,0:T(8,128)(2,1)} %get-tuple-element.242), channel_id=1, source_target_pairs={{0,1},{1,2},{2,3},{3,0},{4,5},{5,6},{6,7},{7,4},{8,9},{9,10},{10,1... | collective-permute-start | bytes 1351688 | tf_op jit(solution)/shard_map/ppermute | solution.py:28
  62.4 22.5 %collective-permute-start.14 = (bf16[352,640]{1,0:T(8,128)(2,1)}, bf16[352,640]{1,0:T(8,128)(2,1)}, u32[]{:S(2)}, u32[]{:S(2)}) collective-permute-start(bf16[352,640]{1,0:T(8,128)(2,1)} %get-tuple-element.239), channel_id=1, source_target_pairs={{0,1},{1,2},{2,3},{3,0},{4,5},{5,6},{6,7},{7,4},{8,9},{9,10},{10,1... | collective-permute-start | bytes 1351688 | tf_op jit(solution)/shard_map/ppermute | solution.py:28
  77.8 28.6 %collective-permute-start.21 = (bf16[720,640]{1,0:T(8,128)(2,1)}, bf16[720,640]{1,0:T(8,128)(2,1)}, u32[]{:S(2)}, u32[]{:S(2)}) collective-permute-start(bf16[720,640]{1,0:T(8,128)(2,1)} %get-tuple-element.251), channel_id=1, source_target_pairs={{0,1},{1,2},{2,3},{3,0},{4,5},{5,6},{6,7},{7,4},{8,9},{9,10},{10,1... | collective-permute-start | bytes 2764808 | tf_op jit(solution)/shard_map/ppermute | solution.py:28
  78.6 27.9 %collective-permute-start.22 = (bf16[720,640]{1,0:T(8,128)(2,1)}, bf16[720,640]{1,0:T(8,128)(2,1)}, u32[]{:S(2)}, u32[]{:S(2)}) collective-permute-start(bf16[720,640]{1,0:T(8,128)(2,1)} %get-tuple-element.252), channel_id=1, source_target_pairs={{0,3},{1,0},{2,1},{3,2},{4,7},{5,4},{6,5},{7,6},{8,11},{9,8},{10,9... | collective-permute-start | bytes 2764808 | tf_op jit(solution)/shard_map/ppermute | solution.py:28
  87.2 24.3 %collective-permute-start.23 = (bf16[720,640]{1,0:T(8,128)(2,1)}, bf16[720,640]{1,0:T(8,128)(2,1)}, u32[]{:S(2)}, u32[]{:S(2)}) collective-permute-start(bf16[720,640]{1,0:T(8,128)(2,1)} %join.1), channel_id=1, source_target_pairs={{0,4},{1,5},{2,6},{3,7},{4,0},{5,1},{6,2},{7,3},{8,12},{9,13},{10,... | collective-permute-start | bytes 2764808 | tf_op jit(solution)/shard_map/ppermute | solution.py:28
  87.7 18.7 %copy-start.1 = (f32[1,720,640]{2,1,0:T(8,128)S(1)}, f32[1,720,640]{2,1,0:T(8,128)}, u32[]{:S(2)}) copy-start(f32[1,720,640]{2,1,0:T(8,128)} %param.20) | copy-start | bytes 5529604
  87.7 18.7 %copy-start.2 = (bf16[720,640]{1,0:T(8,128)(2,1)S(1)}, bf16[720,640]{1,0:T(8,128)(2,1)}, u32[]{:S(2)}) copy-start(bf16[720,640]{1,0:T(8,128)(2,1)} %get-tuple-element.258.g00) | copy-start | bytes 2764804
  87.7 16.6 %collective-permute-start.3 = (bf16[720,640]{1,0:T(8,128)(2,1)}, bf16[720,640]{1,0:T(8,128)(2,1)}, u32[]{:S(2)}, u32[]{:S(2)}) collective-permute-start(bf16[720,640]{1,0:T(8,128)(2,1)} %get-tuple-element.130), channel_id=1, source_target_pairs={{0,68},{1,69},{2,70},{3,71},{4,64},{5,65},{6,66},{7,67},{8,76},{9,... | collective-permute-start | bytes 2764808 | tf_op jit(solution)/shard_map/cond/branch_3_fun/ppermute | solution.py:47
  104.3 26.8 %collective-permute-start.20 = (bf16[720,640]{1,0:T(8,128)(2,1)}, bf16[720,640]{1,0:T(8,128)(2,1)}, u32[]{:S(2)}, u32[]{:S(2)}) collective-permute-start(bf16[720,640]{1,0:T(8,128)(2,1)} %copy-done.17), channel_id=1, source_target_pairs={{0,3},{1,0},{2,1},{3,2},{4,7},{5,4},{6,5},{7,6},{8,11},{9,8},{10,9... | collective-permute-start | bytes 2764808 | tf_op jit(solution)/shard_map/ppermute | solution.py:28
  105.2 25.9 %collective-permute-start.19 = (bf16[720,640]{1,0:T(8,128)(2,1)}, bf16[720,640]{1,0:T(8,128)(2,1)}, u32[]{:S(2)}, u32[]{:S(2)}) collective-permute-start(bf16[720,640]{1,0:T(8,128)(2,1)} %copy-done.17), channel_id=1, source_target_pairs={{0,1},{1,2},{2,3},{3,0},{4,5},{5,6},{6,7},{7,4},{8,9},{9,10},{10,1... | collective-permute-start | bytes 2764808 | tf_op jit(solution)/shard_map/ppermute | solution.py:28
  111.8 15.2 %collective-permute-start.7 = (bf16[720,640]{1,0:T(8,128)(2,1)}, bf16[720,640]{1,0:T(8,128)(2,1)S(1)}, u32[]{:S(2)}, u32[]{:S(2)}) collective-permute-start(bf16[720,640]{1,0:T(8,128)(2,1)} %get-tuple-element.163), channel_id=1, source_target_pairs={{0,64},{8,72},{16,80},{24,88},{32,96},{40,104},{48,112},{56,120},{... | collective-permute-start | bytes 2764808 | tf_op jit(solution)/shard_map/cond/branch_3_fun/ppermute | solution.py:32
  112.5 14.5 %copy-start.12 = (f32[720,640]{1,0:T(8,128)S(1)}, f32[720,640]{1,0:T(8,128)}, u32[]{:S(2)}) copy-start(f32[720,640]{1,0:T(8,128)} %get-tuple-element.160) | copy-start | bytes 5529604 | tf_op jit(solution)/shard_map/cond
  (3 other events, 4.9 us)
